TPU v7x, 256 devices: a whole 4x4x8 slice. The times are simulated.
256 devices in a mesh: seq: 32 (over y, x, core), mp: 8 (over z).
Axes of the slice: x: 4, y: 4, z: 8, core: 2. Of those that a mesh axis runs over, the one named last changes fastest.
Arguments:
- span_states: bfloat16 [4096, 4096], P('seq'), may hold values from -6 to 6
- dec_query: bfloat16 [4096, 2048], P('seq', 'mp'), may hold values from -256 to 256
- nbr_query: bfloat16 [256, 128, 2048], P('seq', None, 'mp'), may hold values from -256 to 256
- nbr_index: int32 [64, 4], P('seq'), may hold values from 0 to 255, as said below
- nbr_count: int32 [64], P('seq'), may hold values from 2 to 4
- wkv_enc: bfloat16 [4096, 2, 2048], P(None, None, 'mp'), may hold values from -0.09375 to 0.09375
- wo_enc: bfloat16 [2048, 4096], P('mp'), may hold values from -0.125 to 0.125
- wkv_dec: bfloat16 [4096, 2, 2048], P(None, None, 'mp'), may hold values from -0.09375 to 0.09375
- grad_out: bfloat16 [4096, 4096], P('seq'), may hold values from -6 to 6
Outputs:
- attended: bfloat16 [4096, 2048], P('seq', 'mp')
- grad_wo: float32 [2048, 4096], P('mp', 'seq')
Inputs may be any that keep to these rules, and one draw needn't show every extreme that they name: `nbr_index`: every row of nbr_query is named exactly once. The entries of the spans of one device name rows in exactly 8 distinct aligned blocks of 8 rows, 1 in each. Entries of slots k >= nbr_count[c] name rows that are not used.
All inputs are finite; a program needn't handle non-finite values.
Results may differ from a plain program's by a relative error of at most 0.025.
Values may be sent and summed in bfloat16 or wider, within the bound.
No kernel may reach another device: no remote copies, remote signals or barrier semaphores. Data moves between devices by JAX's collectives and lax.ppermute only.
A program may use at most 128 MiB of HBM per device.

v0:
```python
import math

import jax
import jax.numpy as jnp
from jax import lax
from jax.sharding import PartitionSpec as P

DH = 128


def normalize(scores, usable):
    scores = jnp.where(usable, scores, -1e30)
    highest = jnp.max(scores, axis=-1, keepdims=True)
    exponent = jnp.exp(scores - highest)
    return (exponent / jnp.sum(exponent, axis=-1, keepdims=True)).astype(jnp.bfloat16)


def encode(queries, key_values):
    amount = queries.shape[0]
    nbr_len = queries.shape[1]
    head_count = queries.shape[2] // DH
    query_heads = queries.reshape(amount, nbr_len, head_count, DH)
    pairs = key_values.reshape(amount, -1, 2, head_count, DH)
    scores = jnp.einsum(
        "mnhd,mlhd->mhnl", query_heads, pairs[:, :, 0], preferred_element_type=jnp.float32
    ) / math.sqrt(DH)
    weights = normalize(scores, True)
    result = jnp.einsum(
        "mhnl,mlhd->mnhd", weights, pairs[:, :, 1], preferred_element_type=jnp.float32
    )
    return result.astype(jnp.bfloat16).reshape(amount, nbr_len, head_count * DH)


def route_first(matrix, values):
    return lax.dot_general(
        matrix, values, (((0,), (0,)), ((), ())), preferred_element_type=jnp.float32
    ).astype(jnp.bfloat16)


def local(
    span_states, dec_query, nbr_query, nbr_index, nbr_count, wkv_enc, wo_enc, wkv_dec, grad_out
):
    seq_count = lax.axis_size("seq")
    span_count = nbr_count.shape[0]
    most_slots = nbr_index.shape[1]
    slot_total = span_count * most_slots
    span_len = span_states.shape[0] // span_count
    nbr_len = nbr_query.shape[1]
    local_width = nbr_query.shape[2]
    head_count = local_width // DH
    hidden_width = span_states.shape[1]
    capacity = max(1, slot_total // seq_count)
    buckets = seq_count * capacity
    target = nbr_index.reshape(slot_total)
    home_device = target // slot_total
    row_there = target % slot_total
    ordinal = jnp.arange(slot_total, dtype=jnp.int32)
    same_home = home_device[:, None] == home_device[None, :]
    position = jnp.sum(jnp.where(same_home & (ordinal[None, :] < ordinal[:, None]), 1, 0), axis=1)
    bucket_of = home_device * capacity + position
    dispatch_mask = jnp.arange(buckets, dtype=jnp.int32)[:, None] == bucket_of[None, :]
    dispatch = dispatch_mask.astype(jnp.bfloat16)
    row_tags = jnp.sum(jnp.where(dispatch_mask, (row_there + 1)[None, :], 0), axis=1)
    enc_pairs = jnp.dot(
        span_states,
        wkv_enc.reshape(hidden_width, 2 * local_width),
        preferred_element_type=jnp.float32,
    ).astype(jnp.bfloat16)
    span_pairs = enc_pairs.reshape(span_count, span_len * 2 * local_width)
    span_dispatch = jnp.sum(dispatch.reshape(buckets, span_count, most_slots), axis=2)
    outbox = jnp.dot(span_dispatch, span_pairs, preferred_element_type=jnp.float32).astype(
        jnp.bfloat16
    )
    outbox = outbox.reshape(seq_count, capacity, span_len, 2 * local_width)
    inbox, in_tags = (
        lax.all_to_all(outbox, "seq", split_axis=0, concat_axis=0, tiled=True),
        lax.all_to_all(
            row_tags.astype(jnp.bfloat16).reshape(seq_count, capacity),
            "seq",
            split_axis=0,
            concat_axis=0,
            tiled=True,
        ),
    )
    picker = (
        in_tags.astype(jnp.float32).reshape(1, buckets)
        == (ordinal + 1).astype(jnp.float32)[:, None]
    ).astype(jnp.bfloat16)
    row_pairs = jnp.dot(
        picker, inbox.reshape(buckets, -1), preferred_element_type=jnp.float32
    ).astype(jnp.bfloat16)
    encoder_row_states = encode(nbr_query, row_pairs.reshape(slot_total, span_len, 2 * local_width))
    reply = route_first(picker, encoder_row_states.reshape(slot_total, -1)).reshape(
        seq_count, capacity, nbr_len * local_width
    )
    returned = lax.all_to_all(reply, "seq", split_axis=0, concat_axis=0, tiled=True)
    slot_heads = route_first(dispatch, returned.reshape(buckets, -1))
    partial_value = jnp.dot(
        slot_heads.reshape(slot_total * nbr_len, local_width),
        wo_enc,
        preferred_element_type=jnp.float32,
    )
    encoded_share = lax.psum_scatter(partial_value, "mp", scatter_dimension=1, tiled=True).astype(
        jnp.bfloat16
    )
    encoded = lax.all_gather(encoded_share, "mp", axis=1, tiled=True)
    dec_pairs = jnp.dot(
        encoded, wkv_dec.reshape(hidden_width, 2 * local_width), preferred_element_type=jnp.float32
    ).astype(jnp.bfloat16)
    dec_pairs = dec_pairs.reshape(span_count, most_slots * nbr_len, 2, head_count, DH)
    span_query = dec_query.reshape(span_count, span_len, head_count, DH)
    dec_scores = jnp.einsum(
        "clhd,cjhd->chlj", span_query, dec_pairs[:, :, 0], preferred_element_type=jnp.float32
    ) / math.sqrt(DH)
    usable = (
        jnp.arange(most_slots * nbr_len, dtype=jnp.int32)[None, :] // nbr_len < nbr_count[:, None]
    )
    dec_weights = normalize(dec_scores, usable[:, None, None, :])
    attended = jnp.einsum(
        "chlj,cjhd->clhd", dec_weights, dec_pairs[:, :, 1], preferred_element_type=jnp.float32
    )
    attended = attended.astype(jnp.bfloat16).reshape(span_count * span_len, local_width)
    grad_term = lax.dot_general(
        attended, grad_out, (((0,), (0,)), ((), ())), preferred_element_type=jnp.float32
    )
    grad_wo = lax.psum_scatter(
        grad_term.astype(jnp.bfloat16), "seq", scatter_dimension=1, tiled=True
    ).astype(jnp.float32)
    return (attended, grad_wo)


def solution(mesh):
    return jax.shard_map(
        local,
        mesh=mesh,
        in_specs=(
            P("seq", None),
            P("seq", "mp"),
            P("seq", None, "mp"),
            P("seq", None),
            P("seq"),
            P(None, None, "mp"),
            P("mp", None),
            P(None, None, "mp"),
            P("seq", None),
        ),
        out_specs=(P("seq", "mp"), P("mp", "seq")),
        check_vma=False,
    )
```

profile of v0, /device:TPU:1, one launch (start us, length us, event | category | flops | bytes accessed | tf_op | source)
XLA Modules:
  0.0 516.2 jit_solution(6437038359119100068)
XLA Ops:
  7.2 0.9 reshape.235
  8.4 0.7 copy.47
  9.1 8.6 %all-to-all-start = ((bf16[32,1,1]{2,1,0:T(2,128)(2,1)}), bf16[32,1,1]{2,1,0:T(2,128)(2,1)S(1)}, u32[]{:S(2)}, u32[]{:S(2)}) async-start(bf16[32,1,1]{2,1,0:T(2,128)(2,1)} %copy.47), calls=%async_computation | async-start | bytes 32768 | tf_op jit(solution)/shard_map/all_to_all | solution.py:77
  17.8 0.7 fusion.32
  18.6 3.0 copy.66
  21.6 0.7 convolution_convert_fusion.7
  22.4 0.8 convolution_convert_fusion.1
  23.2 2.0 copy.67
  25.2 7.4 %all-to-all-start.1 = ((bf16[32,1,64,512]{3,2,1,0:T(8,128)(2,1)}), bf16[32,1,64,512]{3,2,1,0:T(8,128)(2,1)}, u32[]{:S(2)}, u32[]{:S(2)}) async-start(bf16[32,1,64,512]{3,2,1,0:T(8,128)(2,1)} %bitcast.72), calls=%async_computation.1 | async-start | bytes 4194304 | tf_op jit(solution)/shard_map/all_to_all | solution.py:76
  33.0 27.5 %all-to-all-done.1 = bf16[32,1,64,512]{3,2,1,0:T(8,128)(2,1)} async-done(((bf16[32,1,64,512]{3,2,1,0:T(8,128)(2,1)}), bf16[32,1,64,512]{3,2,1,0:T(8,128)(2,1)}, u32[]{:S(2)}, u32[]{:S(2)}) %all-to-all-start.1) | async-done | bytes 2097184 | tf_op jit(solution)/shard_map/all_to_all | solution.py:76
  60.5 2.8 copy.68
  64.9 1.2 fusion.9
  66.1 1.3 copy.52
  67.8 2.1 fusion.2
  70.4 4.6 reduce.3
  75.0 4.5 reshape.252
  79.5 35.3 %all_to_all.16 = bf16[32,2,16384]{2,1,0:T(2,128)(2,1)} all-to-all(bf16[32,2,16384]{2,1,0:T(2,128)(2,1)} %reshape.252), channel_id=1, replica_groups=mesh['seq'=32,'mp'=8] {'seq'}, dimensions={0} | all-to-all | bytes 4194304 | tf_op jit(solution)/shard_map/all_to_all | solution.py:96
  114.8 10.5 %reshape.253 = bf16[32,1,32768]{2,1,0:T(2,128)(2,1)} reshape(bf16[32,2,16384]{2,1,0:T(2,128)(2,1)} %all_to_all.16) | data formatting | bytes 4194304
  125.2 4.5 convolution_convert_fusion.2
  130.0 8.1 %fusion.40 = f32[1024,4096]{1,0:T(8,128)} fusion(bf16[1024,256]{1,0:T(8,128)(2,1)S(1)} %reshape.243, bf16[256,4096]{1,0:T(8,128)(2,1)S(1)} %copy-done), kind=kOutput, calls=%fused_computation.80 | convolution fusion | flops 2147483648 | bytes 19398656 | tf_op jit(solution)/shard_map/dot_general | solution.py:98
  138.1 172.6 %reduce-scatter.5.cloned.1.call-done = f32[1024,512]{1,0:T(8,128)} async-done(((f32[1024,4096]{1,0:T(8,128)}), f32[1024,512]{1,0:T(8,128)}) %reduce-scatter.5.cloned.1.call-update) | async-done | bytes 2097168 | tf_op jit(solution)/shard_map/reduce_scatter | solution.py:103
  310.8 2.8 convert_element_type.99
  313.6 4.9 copy.69
  318.7 87.8 %all-gather.2.cloned.1.call-done = bf16[1024,4096]{1,0:T(8,128)(2,1)} async-done(((bf16[1024,512]{1,0:T(8,128)(2,1)}), bf16[1024,4096]{1,0:T(8,128)(2,1)}) %all-gather.2.cloned.1.call-update) | async-done | bytes 8388624 | tf_op jit(solution)/shard_map/all_gather | solution.py:106
  406.4 9.0 %convolution_convert_fusion.5 = bf16[1024,512]{1,0:T(8,128)(2,1)S(1)} fusion(bf16[1024,4096]{1,0:T(8,128)(2,1)} %all-gather.2.cloned.1.call-done, bf16[4096,512]{1,0:T(8,128)(2,1)} %bitcast.78), kind=kOutput, calls=%fused_computation.10 | convolution fusion | flops 4295491584 | bytes 13631488 | tf_op jit(solution)/shard_map/dot_general | solution.py:107
  415.8 0.7 fusion.36
  417.1 0.6 fusion.13
  418.0 2.0 convolution_convert_fusion.4
  420.1 4.3 copy.58
  424.4 83.6 %reduce-scatter.7.cloned.1.call-done = bf16[128,256]{1,0:T(8,128)(2,1)} async-done(((bf16[4096,256]{1,0:T(8,128)(2,1)}), bf16[128,256]{1,0:T(8,128)(2,1)}) %reduce-scatter.7.cloned.1.call-update) | async-done | bytes 65552
  508.0 0.9 copy.59
  509.0 0.7 convert_element_type.105
  (48 shorter events, 5.2 us)
Async XLA Ops:
  7.2 122.8 %copy-start = (bf16[256,4096]{1,0:T(8,128)(2,1)S(1)}, bf16[256,4096]{1,0:T(8,128)(2,1)}, u32[]{:S(2)}) copy-start(bf16[256,4096]{1,0:T(8,128)(2,1)} %param.15) | copy-start | bytes 6291460
  9.1 16.1 %all-to-all-start = ((bf16[32,1,1]{2,1,0:T(2,128)(2,1)}), bf16[32,1,1]{2,1,0:T(2,128)(2,1)S(1)}, u32[]{:S(2)}, u32[]{:S(2)}) async-start(bf16[32,1,1]{2,1,0:T(2,128)(2,1)} %copy.47), calls=%async_computation | async-start | bytes 32768 | tf_op jit(solution)/shard_map/all_to_all | solution.py:77
  18.6 3.0 copy-start.3
  25.2 35.3 %all-to-all-start.1 = ((bf16[32,1,64,512]{3,2,1,0:T(8,128)(2,1)}), bf16[32,1,64,512]{3,2,1,0:T(8,128)(2,1)}, u32[]{:S(2)}, u32[]{:S(2)}) async-start(bf16[32,1,64,512]{3,2,1,0:T(8,128)(2,1)} %bitcast.72), calls=%async_computation.1 | async-start | bytes 4194304 | tf_op jit(solution)/shard_map/all_to_all | solution.py:76
  32.6 278.1 %reduce-scatter.5.cloned.1.call-start = ((), (), s32[]{:S(2)}) async-start(), calls=%async_computation.5 | async-start | bytes 18874368 | tf_op jit(solution)/shard_map/reduce_scatter | solution.py:103
  63.3 1.0 copy-start.4
  138.1 268.4 %all-gather.2.cloned.1.call-start = ((), (), s32[]{:S(2)}) async-start(), calls=%async_computation.6 | async-start | bytes 9437184 | tf_op jit(solution)/shard_map/all_gather | solution.py:106
  313.6 194.4 %reduce-scatter.7.cloned.1.call-start = ((), (), s32[]{:S(2)}) async-start(), calls=%async_computation.7 | async-start | bytes 2162688
  313.6 5.0 copy-start.6
  313.6 5.0 copy-start.7
  416.8 1.2 copy-start.2
  417.7 6.6 %copy-start.5 = (bf16[16,8,2,128]{3,1,2,0:T(8,128)(2,1)}, bf16[16,8,2,128]{3,1,2,0:T(8,128)(2,1)S(1)}, u32[]{:S(2)}) copy-start(bf16[16,8,2,128]{3,1,2,0:T(8,128)(2,1)S(1)} %copy.90) | copy-start | bytes 196612
  420.1 89.6 %copy-start.1 = (bf16[256,4096]{1,0:T(8,128)(2,1)S(1)}, bf16[256,4096]{1,0:T(8,128)(2,1)}, u32[]{:S(2)}) copy-start(bf16[256,4096]{1,0:T(8,128)(2,1)} %param.15) | copy-start | bytes 6291460
Sparse Core Ops, SparseCore 0:
  138.2 172.5 reduce-scatter.4
  313.7 92.7 all-gather.1
  424.5 83.4 reduce-scatter.6
where the time goes:
time: 518 us; the launch traced here: 516 us
  waiting for transfers between devices  372 us (72%)
  local copies, waits for them, and re-layouts  39.1 us (8%)
  blocking collectives  35.3 us (7%)
  matrix products  30.2 us (6%)
  starting transfers between devices  16.1 us (3%)
  between operations  14 us (3%)
  other arithmetic  9.87 us (2%)
    reduce_scatter x1, waiting for transfers between devices, local(): lax.psum_scatter(partial_value, 'mp', scatter_dimension=1, tiled=True)  173 us
    all_gather x1, waiting for transfers between devices, local(): encoded = lax.all_gather(encoded_share, 'mp', axis=1, tiled=True)  87.8 us
    unnamed x4, waiting for transfers between devices  83.7 us
    all_to_all x1, blocking collectives, local(): lax.all_to_all(reply, 'seq', split_axis=0, concat_axis=0, tiled=True)  35.3 us
    unnamed x25, local copies, waits for them, and re-layouts  33.7 us
    all_to_all x1, waiting for transfers between devices, local(): lax.all_to_all(outbox, 'seq', split_axis=0, concat_axis=0, tiled=True)  27.5 us
  transfers between devices with their start and end apart: 5, of which 4 were waited for; matrix products, arithmetic and copies ran while one was open for 2% of the time, Pallas kernels for 0%

commit v1 on v0

v1 whole, which is shorter than its diff:
```python
import functools
import math

import jax
import jax.numpy as jnp
from jax import lax
from jax.experimental import pallas as pl
from jax.experimental.pallas import tpu as pltpu
from jax.sharding import PartitionSpec as P

DH = 128
BF = jnp.bfloat16
F32 = jnp.float32
VMEM = pl.BlockSpec(memory_space=pltpu.VMEM)
SMEM = pl.BlockSpec(memory_space=pltpu.SMEM)
ANY = pl.BlockSpec(memory_space=pl.ANY)
NT = (((1,), (1,)), ((), ()))


def params():
    return pltpu.CompilerParams(vmem_limit_bytes=32 * 1024 * 1024)


def outbox_kernel(tags, query, out0, out1, sems):
    count = out0.shape[0]

    def copies(dest):
        row = tags[dest] - 1
        return [
            pltpu.make_async_copy(
                query.at[row, :, pl.ds(h * DH, DH)], out.at[dest], sems.at[h, dest]
            )
            for h, out in enumerate((out0, out1))
        ]

    for dest in range(count):

        @pl.when(tags[dest] > 0)
        def _():
            for copy in copies(dest):
                copy.start()

    for dest in range(count):

        @pl.when(tags[dest] > 0)
        def _():
            for copy in copies(dest):
                copy.wait()


def outbox(tags, query, buckets):
    rows, length, width = query.shape
    shape = jax.ShapeDtypeStruct((buckets, length, DH), BF)
    return pl.pallas_call(
        outbox_kernel,
        out_shape=(shape, shape),
        in_specs=[SMEM, ANY],
        out_specs=(ANY, ANY),
        scratch_shapes=[pltpu.SemaphoreType.DMA((2, buckets))],
        compiler_params=params(),
    )(tags, query)


def encode_kernel(head, rows, index, inbox, pairs, out, held, sems):
    spans, slots = index.shape
    span_len = pairs.shape[0] // spans
    copies = []
    for j in range(spans * slots):
        home = index[j // slots, j % slots] // rows
        copies.append(pltpu.make_async_copy(inbox.at[home], held.at[j], sems.at[j]))
        copies[-1].start()
    for j in range(spans * slots):
        c, k = j // slots, j % slots
        copies[j].wait()
        keys = pairs[c * span_len : (c + 1) * span_len, head * DH : (head + 1) * DH]
        scores = lax.dot_general(keys, held[j], NT, preferred_element_type=F32) / math.sqrt(DH)
        exponent = jnp.exp(scores - jnp.max(scores, axis=0, keepdims=True))
        weights = exponent / jnp.sum(exponent, axis=0, keepdims=True)
        out[c * span_len : (c + 1) * span_len, k * DH : (k + 1) * DH] = weights.astype(BF)


def encode(head, index, inbox, pairs):
    spans, slots = index.shape
    return pl.pallas_call(
        functools.partial(encode_kernel, head, spans * slots),
        out_shape=jax.ShapeDtypeStruct((pairs.shape[0], slots * inbox.shape[1]), BF),
        in_specs=[SMEM, ANY, VMEM],
        out_specs=VMEM,
        scratch_shapes=[
            pltpu.VMEM((spans * slots,) + inbox.shape[1:], BF),
            pltpu.SemaphoreType.DMA((spans * slots,)),
        ],
        compiler_params=params(),
    )(index, inbox, pairs)


def fold_kernel(place, values, mine, other, out):
    groups = values.shape[0]
    spans = out.shape[0]
    span_len = values.shape[1] // spans
    z, core = place[0], place[1]
    for rel in range(groups):
        g = lax.rem(z + rel, groups)
        own = mine[g]
        far = other[g]
        first = jnp.where(core == 0, own, far)
        second = jnp.where(core == 0, far, own)
        low = jnp.dot(values[g, :, :DH], first, preferred_element_type=F32)
        high = jnp.dot(values[g, :, DH:], second, preferred_element_type=F32)
        for c in range(spans):
            at = slice(c * span_len, (c + 1) * span_len)
            both = jnp.concatenate([low[at], high[at]], axis=0)
            out[c, :, rel * 2 * span_len : (rel + 1) * 2 * span_len] = both.T.astype(BF)


def fold(place, values, mine, other, spans):
    groups, tokens, _ = values.shape
    width = mine.shape[2]
    return pl.pallas_call(
        fold_kernel,
        out_shape=jax.ShapeDtypeStruct((spans, width, groups * 2 * tokens // spans), BF),
        in_specs=[SMEM, VMEM, VMEM, VMEM],
        out_specs=VMEM,
        compiler_params=params(),
    )(place, values, mine, other)


def decode_kernel(place, counts, folded, query, *refs):
    spans = folded.shape[0]
    span_len = query.shape[0] // spans
    pieces, (out, send, held, sems) = refs[:-4], refs[-4:]
    copies = []
    for c in range(spans):
        row = []
        for i, piece in enumerate(pieces):
            row.append(
                pltpu.make_async_copy(
                    piece.at[pl.ds(c * span_len, span_len)],
                    held.at[c, pl.ds(i * span_len, span_len)],
                    sems.at[c, i],
                )
            )
            row[-1].start()
        copies.append(row)
    slot_tokens = held.shape[2]
    for c in range(spans):
        for copy in copies[c]:
            copy.wait()
        both = jnp.dot(folded[c], held[c], preferred_element_type=F32).astype(BF)
        usable = lax.broadcasted_iota(jnp.int32, (span_len, slot_tokens), 1) < counts[c] * DH
        for h in range(2):
            at = slice(c * span_len, (c + 1) * span_len)
            keys = both[h * DH : (h + 1) * DH]
            values = both[(2 + h) * DH : (3 + h) * DH]
            scores = jnp.dot(
                query[at, h * DH : (h + 1) * DH], keys, preferred_element_type=F32
            ) / math.sqrt(DH)
            scores = jnp.where(usable, scores, -1e30)
            exponent = jnp.exp(scores - jnp.max(scores, axis=1, keepdims=True))
            weights = (exponent / jnp.sum(exponent, axis=1, keepdims=True)).astype(BF)
            result = lax.dot_general(weights, values, NT, preferred_element_type=F32)
            out[at, h * DH : (h + 1) * DH] = result.astype(BF)
    send[...] = jnp.where(place[1] == 0, out[:, DH:], out[:, :DH])


def decode(place, counts, folded, query, pieces):
    spans = folded.shape[0]
    tokens, width = query.shape
    return pl.pallas_call(
        decode_kernel,
        out_shape=(
            jax.ShapeDtypeStruct((tokens, width), BF),
            jax.ShapeDtypeStruct((tokens, DH), BF),
        ),
        in_specs=[SMEM, SMEM, VMEM, VMEM] + [ANY] * len(pieces),
        out_specs=(VMEM, VMEM),
        scratch_shapes=[
            pltpu.VMEM((spans, folded.shape[2], pieces[0].shape[1]), BF),
            pltpu.SemaphoreType.DMA((spans, len(pieces))),
        ],
        compiler_params=params(),
    )(place, counts, folded, query, *pieces)


def partial_kernel(place, attended, near, grad, near_grad, out):
    own = jnp.where(place[1] == 0, attended[:, :DH], attended[:, DH:])
    left = jnp.concatenate([own, near[...]], axis=0).T
    half = left.shape[1] // 2
    chunk = grad.shape[1] // out.shape[0]
    wide = 4
    for s in range(0, out.shape[0], wide):
        at = slice(s * chunk, (s + wide) * chunk)
        term = jnp.dot(left[:, :half], grad[:, at], preferred_element_type=F32)
        term += jnp.dot(left[:, half:], near_grad[:, at], preferred_element_type=F32)
        term = term.astype(BF)
        for i in range(wide):
            out[s + i] = term[:, i * chunk : (i + 1) * chunk]


def partial_grad(place, attended, near, grad, near_grad, buckets):
    return pl.pallas_call(
        partial_kernel,
        out_shape=jax.ShapeDtypeStruct((buckets, DH, grad.shape[1] // buckets), BF),
        in_specs=[SMEM, VMEM, VMEM, VMEM, VMEM],
        out_specs=VMEM,
        compiler_params=params(),
    )(place, attended, near, grad, near_grad)


def total_kernel(parts, out):
    for core in range(2):
        total = parts[core].astype(F32)
        for p in range(1, parts.shape[0] // 2):
            total += parts[2 * p + core].astype(F32)
        out[core * DH : (core + 1) * DH] = total


def total_grad(parts):
    return pl.pallas_call(
        total_kernel,
        out_shape=jax.ShapeDtypeStruct((2 * DH, parts.shape[2]), F32),
        in_specs=[VMEM],
        out_specs=VMEM,
        compiler_params=params(),
    )(parts)


def shift(x, axis, step):
    n = lax.axis_size(axis)
    return lax.ppermute(x, axis, [(i, (i + step) % n) for i in range(n)])


def sibling(x):
    n = lax.axis_size("seq")
    return lax.ppermute(x, "seq", [(i, i ^ 1) for i in range(n)])


def everywhere(x, axis, groups=None):
    n = lax.axis_size(axis) if groups is None else len(groups[0])
    copies = jnp.broadcast_to(x[None], (n,) + x.shape)
    return lax.all_to_all(
        copies, axis, split_axis=0, concat_axis=0, axis_index_groups=groups, tiled=True
    )


def exchange(x):
    return lax.all_to_all(x, "seq", split_axis=0, concat_axis=0, tiled=True)


def local(
    span_states, dec_query, nbr_query, nbr_index, nbr_count, wkv_enc, wo_enc, wkv_dec, grad_out
):
    devices = lax.axis_size("seq")
    groups = lax.axis_size("mp")
    s, z = lax.axis_index("seq"), lax.axis_index("mp")
    core, chip = s % 2, s // 2
    place = jnp.stack([z, core]).astype(jnp.int32)
    spans = nbr_count.shape[0]
    rows = nbr_query.shape[0]
    hidden = span_states.shape[1]
    same_core = [[2 * p + c for p in range(devices // 2)] for c in range(2)]

    home = nbr_index // rows
    mine = jnp.arange(devices, dtype=jnp.int32)[:, None, None] == home[None]
    tags = jnp.sum(jnp.where(mine, (nbr_index % rows + 1)[None], 0), axis=(1, 2))
    tags = exchange(tags.reshape(devices, 1, 1)).reshape(devices)
    box0, box1 = outbox(tags, nbr_query, devices)
    in0 = exchange(box0)
    in1 = exchange(box1)

    part = DH // (devices // 2)
    wo_rows = lax.dynamic_slice_in_dim(wo_enc, core * DH + chip * part, part, 0)
    wo_rows = everywhere(wo_rows, "mp").reshape(groups * part, hidden)
    product = jnp.dot(
        wo_rows, wkv_dec.reshape(hidden, -1), preferred_element_type=F32
    ).astype(BF)
    product = everywhere(product, "seq", same_core)
    product = product.reshape(devices // 2, groups, part, -1).transpose(1, 0, 2, 3)
    product = product.reshape(groups, DH, -1)
    product_far = sibling(product)

    pairs = jnp.dot(
        span_states, wkv_enc.reshape(hidden, -1), preferred_element_type=F32
    ).astype(BF)
    values = everywhere(pairs[:, 2 * DH :], "mp")
    folded = fold(place, values, product, product_far, spans)
    grad_near = sibling(grad_out)

    def ring(x, forward):
        up = [x]
        down = [x]
        for _ in range(3):
            up.append(shift(up[-1], "mp", -1))
            down.append(shift(down[-1], "mp", 1))
        last = shift(up[-1], "mp", -1) if forward else shift(down[-1], "mp", 1)
        return up + [last] + down[:0:-1]

    w0 = ring(encode(0, nbr_index, in0, pairs), True)
    w1 = ring(encode(1, nbr_index, in1, pairs), False)
    pieces = [piece for both in zip(w0, w1) for piece in both]
    attended, send = decode(place, nbr_count, folded, dec_query, pieces)

    near = sibling(send)
    parts = exchange(partial_grad(place, attended, near, grad_out, grad_near, devices))
    return attended, total_grad(parts)


def solution(mesh):
    return jax.shard_map(
        local,
        mesh=mesh,
        in_specs=(
            P("seq", None),
            P("seq", "mp"),
            P("seq", None, "mp"),
            P("seq", None),
            P("seq"),
            P(None, None, "mp"),
            P("mp", None),
            P(None, None, "mp"),
            P("seq", None),
        ),
        out_specs=(P("seq", "mp"), P("mp", "seq")),
        check_vma=False,
    )
```

time: 518 us -> 192 us (0.37)
  waiting for transfers between devices: 372 us -> 61.7 us
  starting transfers between devices: 16.1 us -> 48.4 us
  matrix products: 30.2 us -> 1.55 us
  local copies, waits for them, and re-layouts: 39.1 us -> 18.5 us
  Pallas kernels: 0 us -> 17.7 us
  between operations: 14 us -> 1.01 us
  other arithmetic: 9.87 us -> 1.66 us
  blocking collectives: 35.3 us -> 41.1 us
    reduce_scatter x1 -> x0, waiting for transfers between devices: 173 us -> none  [local(): lax.psum_scatter(partial_value, 'mp', scatter_dimension=1, tiled=True)]
    all_gather x1 -> x0, waiting for transfers between devices: 87.8 us -> none  [local(): encoded = lax.all_gather(encoded_share, 'mp', axis=1, tiled=True)]
    unnamed x4 -> x0, waiting for transfers between devices: 83.7 us -> none
    dot_general x12 -> x2, matrix products: 30.2 us -> 1.55 us  [the longest x1 0.83 us: local(): jnp.dot(wo_rows, wkv_dec.reshape(hidden, -1), preferred_element_type=F32)]
    all_to_all x2 -> x5, waiting for transfers between devices: 27.5 us -> 45.6 us  [the longest x3 33 us: exchange(): return lax.all_to_all(x, 'seq', split_axis=0, concat_axis=0, tiled=True)]
    unnamed x25 -> x56, local copies, waits for them, and re-layouts: 33.7 us -> 15.9 us
    pallas_call x0 -> x7, Pallas kernels: none -> 17.7 us  [the longest x2 5.57 us: encode(): pl.pallas_call(functools.partial(encode_kernel, head, spans * slots), out...]
    ppermute x0 -> x17, starting transfers between devices: none -> 17.5 us  [the longest x14 14.3 us: shift(): return lax.ppermute(x, axis, [(i, (i + step) % n) for i in range(n)])]
  transfers between devices with their start and end apart: 5 -> 22, of which waited for: 4 -> 11; matrix products, arithmetic and copies ran while one was open for 2% -> 5% of each run, Pallas kernels for 0% -> 8%
where the time goes in v1:
time: 192 us
  waiting for transfers between devices  61.7 us (32%)
  starting transfers between devices  48.4 us (25%)
  blocking collectives  41.1 us (21%)
  local copies, waits for them, and re-layouts  18.5 us (10%)
  Pallas kernels  17.7 us (9%)
    all_to_all x3, waiting for transfers between devices, exchange(): return lax.all_to_all(x, 'seq', split_axis=0, concat_axis=0, tiled=True)  33 us
    all_to_all x1, blocking collectives, exchange(): return lax.all_to_all(x, 'seq', split_axis=0, concat_axis=0, tiled=True)  21.2 us
    all_to_all x1, blocking collectives, everywhere(): lax.all_to_all(copies, axis, split_axis=0, concat_axis=0, axis_index_grou...  19.9 us
    all_to_all x3, starting transfers between devices, exchange(): return lax.all_to_all(x, 'seq', split_axis=0, concat_axis=0, tiled=True)  18.4 us
    unnamed x56, local copies, waits for them, and re-layouts  15.9 us
    ppermute x14, waiting for transfers between devices, shift(): return lax.ppermute(x, axis, [(i, (i + step) % n) for i in range(n)])  15.2 us
    ppermute x14, starting transfers between devices, shift(): return lax.ppermute(x, axis, [(i, (i + step) % n) for i in range(n)])  14.3 us
    all_to_all x2, waiting for transfers between devices, everywhere(): lax.all_to_all(copies, axis, split_axis=0, concat_axis=0, axis_index_grou...  12.6 us
  transfers between devices with their start and end apart: 22, of which 11 were waited for; matrix products, arithmetic and copies ran while one was open for 5% of the time, Pallas kernels for 8%

profile of v1, /device:TPU:1, one launch (start us, length us, event | category | flops | bytes accessed | tf_op | source)
XLA Modules:
  0.0 191.5 jit_solution(5218703110914298046)
XLA Ops:
  2.3 8.6 %all-to-all-start.3 = ((s32[32,1,1]{2,1,0:T(1,128)}), s32[32,1,1]{2,1,0:T(1,128)S(1)}, u32[]{:S(2)}, u32[]{:S(2)}) async-start(s32[32,1,1]{2,1,0:T(1,128)} %copy.17), calls=%async_computation.3 | async-start | bytes 32768 | tf_op jit(solution)/shard_map/all_to_all | solution.py:247
  10.9 6.8 %all-to-all-done.3 = s32[32,1,1]{2,1,0:T(1,128)S(1)} async-done(((s32[32,1,1]{2,1,0:T(1,128)}), s32[32,1,1]{2,1,0:T(1,128)S(1)}, u32[]{:S(2)}, u32[]{:S(2)}) %all-to-all-start.3) | async-done | bytes 160 | tf_op jit(solution)/shard_map/all_to_all | solution.py:247
  18.6 8.2 %all-to-all-start.1 = ((bf16[8,8,4096]{2,1,0:T(8,128)(2,1)}), bf16[8,8,4096]{2,1,0:T(8,128)(2,1)S(1)}, u32[]{:S(2)}, u32[]{:S(2)}) async-start(bf16[8,8,4096]{2,1,0:T(8,128)(2,1)} %broadcast_in_dim.19), calls=%async_computation.1 | async-start | bytes 1048576 | tf_op jit(solution)/shard_map/all_to_all | solution.py:241
  27.4 1.0 copy-done.6
  28.5 1.7 shard_map.105
  32.1 12.6 %all-to-all-done.1 = bf16[8,8,4096]{2,1,0:T(8,128)(2,1)S(1)} async-done(((bf16[8,8,4096]{2,1,0:T(8,128)(2,1)}), bf16[8,8,4096]{2,1,0:T(8,128)(2,1)S(1)}, u32[]{:S(2)}, u32[]{:S(2)}) %all-to-all-start.1) | async-done | bytes 524320 | tf_op jit(solution)/shard_map/all_to_all | solution.py:241
  45.6 4.1 %all-to-all-start.4 = ((bf16[32,128,128]{2,1,0:T(8,128)(2,1)}), bf16[32,128,128]{2,1,0:T(8,128)(2,1)S(1)}, u32[]{:S(2)}, u32[]{:S(2)}) async-start(bf16[32,128,128]{2,1,0:T(8,128)(2,1)} %copy-done.5), calls=%async_computation.4 | async-start | bytes 2097152 | tf_op jit(solution)/shard_map/all_to_all | solution.py:247
  49.7 3.0 %copy.19 = bf16[512,8,2,256]{3,1,2,0:T(8,128)(2,1)S(1)} copy(bf16[512,8,2,256]{3,2,1,0:T(2,128)(2,1)} %bitcast.22) | data formatting | bytes 8388608
  53.5 13.4 %all-to-all-done.4.inbox = bf16[32,128,128]{2,1,0:T(8,128)(2,1)S(1)} async-done(((bf16[32,128,128]{2,1,0:T(8,128)(2,1)}), bf16[32,128,128]{2,1,0:T(8,128)(2,1)S(1)}, u32[]{:S(2)}, u32[]{:S(2)}) %all-to-all-start.4) | async-done | bytes 1048608 | tf_op jit(solution)/shard_map/all_to_all | solution.py:247
  67.0 19.9 %all_to_all.35 = bf16[16,64,512]{2,1,0:T(8,128)(2,1)} all-to-all(bf16[16,64,512]{2,1,0:T(8,128)(2,1)S(1)} %broadcast_in_dim.20), channel_id=1, replica_groups={{0,16,32,48,64,80,96,112,128,144,160,176,192,208,224,240},{8,24,40,56,7..., dimensions={0} | all-to-all | bytes 2097152 | tf_op jit(solution)/shard_map/all_to_all | solution.py:241
  87.0 5.8 %all-to-all-start.5 = ((bf16[32,128,128]{2,1,0:T(8,128)(2,1)}), bf16[32,128,128]{2,1,0:T(8,128)(2,1)}, u32[]{:S(2)}, u32[]{:S(2)}) async-start(bf16[32,128,128]{2,1,0:T(8,128)(2,1)} %copy-done.4), calls=%async_computation.5 | async-start | bytes 2097152 | tf_op jit(solution)/shard_map/all_to_all | solution.py:247
  93.2 3.1 %copy.18 = bf16[512,8,2,256]{3,1,2,0:T(8,128)(2,1)S(1)} copy(bf16[512,8,2,256]{3,2,1,0:T(2,128)(2,1)} %bitcast.23) | data formatting | bytes 8388608
  97.4 12.7 %all-to-all-done.5.inbox = bf16[32,128,128]{2,1,0:T(8,128)(2,1)} async-done(((bf16[32,128,128]{2,1,0:T(8,128)(2,1)}), bf16[32,128,128]{2,1,0:T(8,128)(2,1)}, u32[]{:S(2)}, u32[]{:S(2)}) %all-to-all-start.5) | async-done | bytes 1048608 | tf_op jit(solution)/shard_map/all_to_all | solution.py:247
  110.9 4.3 %all-to-all-start = ((bf16[8,128,256]{2,1,0:T(8,128)(2,1)}), bf16[8,128,256]{2,1,0:T(8,128)(2,1)}, u32[]{:S(2)}, u32[]{:S(2)}) async-start(bf16[8,128,256]{2,1,0:T(8,128)(2,1)} %broadcast_in_dim.18), calls=%async_computation | async-start | bytes 1048576 | tf_op jit(solution)/shard_map/all_to_all | solution.py:241
  115.2 1.2 copy-done.2
  116.4 2.6 %shard_map.106.refs_0_ = bf16[128,512]{1,0:T(8,128)(2,1)S(1)} custom-call(s32[2,4]{1,0:T(2,128)S(1)} %copy-done.21, bf16[32,128,128]{2,1,0:T(8,128)(2,1)S(1)} %copy-done.2, bf16[128,512]{1,0:T(8,128)(2,1)S(1)} %convolution_convert_fusion.pairs), custom_call_target="tpu_custom_call" | custom-call | tf_op jit(solution)/shard_map/pallas_call | solution.py:84
  119.0 2.7 %collective-permute-start.1 = (bf16[128,512]{1,0:T(8,128)(2,1)S(1)}, bf16[128,512]{1,0:T(8,128)(2,1)S(1)}, u32[]{:S(2)}, u32[]{:S(2)}) collective-permute-start(bf16[128,512]{1,0:T(8,128)(2,1)S(1)} %shard_map.106.refs_0_), channel_id=1, source_target_pairs={{0,7},{1,0},{2,1},{3,2},{4,3},{5,4},{6,5},{7,6},{8,15},{9,8},{10,9... | collective-permute-start | bytes 393224 | tf_op jit(solution)/shard_map/ppermute | solution.py:230
  121.7 3.0 %shard_map.107.refs_1_ = bf16[128,512]{1,0:T(8,128)(2,1)S(1)} custom-call(s32[2,4]{1,0:T(2,128)S(1)} %copy-done.21, bf16[32,128,128]{2,1,0:T(8,128)(2,1)} %all-to-all-done.5.inbox, bf16[128,512]{1,0:T(8,128)(2,1)S(1)} %convolution_convert_fusion.pairs), custom_call_target="tpu_custom_call" | custom-call | tf_op jit(solution)/shard_map/pallas_call | solution.py:84
  124.6 1.3 collective-permute-start.2
  126.2 5.1 %collective-permute-done.1.refs_2_ = bf16[128,512]{1,0:T(8,128)(2,1)S(1)} collective-permute-done((bf16[128,512]{1,0:T(8,128)(2,1)S(1)}, bf16[128,512]{1,0:T(8,128)(2,1)S(1)}, u32[]{:S(2)}, u32[]{:S(2)}) %collective-permute-start.1) | collective-permute-done | bytes 131104 | tf_op jit(solution)/shard_map/ppermute | solution.py:230
  131.3 2.7 %collective-permute-done.2.refs_3_ = bf16[128,512]{1,0:T(8,128)(2,1)S(1)} collective-permute-done((bf16[128,512]{1,0:T(8,128)(2,1)S(1)}, bf16[128,512]{1,0:T(8,128)(2,1)S(1)}, u32[]{:S(2)}, u32[]{:S(2)}) %collective-permute-start.2) | collective-permute-done | bytes 131104 | tf_op jit(solution)/shard_map/ppermute | solution.py:230
  134.0 1.9 collective-permute-start.3
  139.9 1.9 collective-permute-done.4.refs_5_
  141.8 2.6 %collective-permute-start.5 = (bf16[128,512]{1,0:T(8,128)(2,1)S(1)}, bf16[128,512]{1,0:T(8,128)(2,1)}, u32[]{:S(2)}, u32[]{:S(2)}) collective-permute-start(bf16[128,512]{1,0:T(8,128)(2,1)S(1)} %collective-permute-done.3.refs_4_), channel_id=1, source_target_pairs={{0,7},{1,0},{2,1},{3,2},{4,3},{5,4},{6,5},{7,6},{8,15},{9,8},{10,9... | collective-permute-start | bytes 393224 | tf_op jit(solution)/shard_map/ppermute | solution.py:230
  145.7 2.7 %collective-permute-start.6 = (bf16[128,512]{1,0:T(8,128)(2,1)}, bf16[128,512]{1,0:T(8,128)(2,1)}, u32[]{:S(2)}, u32[]{:S(2)}) collective-permute-start(bf16[128,512]{1,0:T(8,128)(2,1)} %collective-permute-done.4.refs_5_), channel_id=1, source_target_pairs={{0,7},{1,0},{2,1},{3,2},{4,3},{5,4},{6,5},{7,6},{8,15},{9,8},{10,9... | collective-permute-start | bytes 393224 | tf_op jit(solution)/shard_map/ppermute | solution.py:230
  148.4 1.8 collective-permute-done.10.refs_11_
  151.8 2.4 %shard_map.104.folded = bf16[2,512,1024]{2,1,0:T(8,128)(2,1)S(1)} custom-call(s32[2]{0:T(128)S(1)} %pad_add_fusion.place, bf16[8,128,256]{2,1,0:T(8,128)(2,1)} %all-to-all-done.values, bf16[8,128,512]{2,1,0:T(8,128)(2,1)S(1)} %copy_bitcast_fusion.mine, bf16[8,128,512]{2,1,0:T(8,128)(2,1)} %collective-permute-done.other), custom_call_target="tpu_custom_call" | custom-call | tf_op jit(solution)/shard_map/pallas_call | solution.py:119
  154.5 3.5 %collective-permute-done.11.refs_9_ = bf16[128,512]{1,0:T(8,128)(2,1)} collective-permute-done((bf16[128,512]{1,0:T(8,128)(2,1)}, bf16[128,512]{1,0:T(8,128)(2,1)}, u32[]{:S(2)}, u32[]{:S(2)}) %collective-permute-start.11) | collective-permute-done | bytes 131104 | tf_op jit(solution)/shard_map/ppermute | solution.py:230
  158.1 5.3 %shard_map.108 = (bf16[128,256]{1,0:T(8,128)(2,1)}, bf16[128,128]{1,0:T(8,128)(2,1)S(1)}) custom-call(s32[2]{0:T(128)S(1)} %pad_add_fusion.place, s32[2]{0:T(128)S(1)} %copy-done.22, bf16[2,512,1024]{2,1,0:T(8,128)(2,1)S(1)} %shard_map.104.folded, bf16[128,256]{1,0:T(8,128)(2,1)S(1)} %copy-done.19, bf16[128,512]{1,0:T(8,128)(2,1)S(1)} %shard_map.106.refs_0_, ...), custom_call_target="tpu_custom_call" | custom-call | tf_op jit(solution)/shard_map/pallas_call | solution.py:169
  163.4 2.5 %collective-permute-start.15 = (bf16[128,128]{1,0:T(8,128)(2,1)S(1)}, bf16[128,128]{1,0:T(8,128)(2,1)S(1)}, u32[]{:S(2)}, u32[]{:S(2)}) collective-permute-start(bf16[128,128]{1,0:T(8,128)(2,1)S(1)} %get-tuple-element.9), channel_id=1, source_target_pairs={{0,8},{8,0},{16,24},{24,16},{32,40},{40,32},{48,56},{56,48},{64,72... | collective-permute-start | bytes 98312 | tf_op jit(solution)/shard_map/ppermute | solution.py:235
  167.6 2.0 %shard_map.109 = bf16[32,128,128]{2,1,0:T(8,128)(2,1)S(1)} custom-call(s32[2]{0:T(128)S(1)} %pad_add_fusion.place, bf16[128,256]{1,0:T(8,128)(2,1)S(1)} %copy-done.20, bf16[128,128]{1,0:T(8,128)(2,1)S(1)} %collective-permute-done.15.near, bf16[128,4096]{1,0:T(8,128)(2,1)S(1)} %copy-done.3, bf16[128,4096]{1,0:T(8,128)(2,1)} %collective-permute-done.16.near_grad), custom_call_target="tpu_custom_call" | custom-call | tf_op jit(solution)/shard_map/pallas_call | solution.py:201
  169.6 21.2 %all_to_all.36.parts = bf16[32,128,128]{2,1,0:T(8,128)(2,1)S(1)} all-to-all(bf16[32,128,128]{2,1,0:T(8,128)(2,1)S(1)} %shard_map.109), channel_id=1, replica_groups=mesh['seq'=32,'mp'=8] {'seq'}, dimensions={0} | all-to-all | bytes 2097152 | tf_op jit(solution)/shard_map/all_to_all | solution.py:247
  (90 shorter events, 19.3 us)
Async XLA Ops:
  0.6 10.3 %copy-start = (bf16[256,4096]{1,0:T(8,128)(2,1)S(1)}, bf16[256,4096]{1,0:T(8,128)(2,1)}, u32[]{:S(2)}) copy-start(bf16[256,4096]{1,0:T(8,128)(2,1)} %param.15) | copy-start | bytes 6291460
  2.3 15.5 %all-to-all-start.3 = ((s32[32,1,1]{2,1,0:T(1,128)}), s32[32,1,1]{2,1,0:T(1,128)S(1)}, u32[]{:S(2)}, u32[]{:S(2)}) async-start(s32[32,1,1]{2,1,0:T(1,128)} %copy.17), calls=%async_computation.3 | async-start | bytes 32768 | tf_op jit(solution)/shard_map/all_to_all | solution.py:247
  18.6 26.1 %all-to-all-start.1 = ((bf16[8,8,4096]{2,1,0:T(8,128)(2,1)}), bf16[8,8,4096]{2,1,0:T(8,128)(2,1)S(1)}, u32[]{:S(2)}, u32[]{:S(2)}) async-start(bf16[8,8,4096]{2,1,0:T(8,128)(2,1)} %broadcast_in_dim.19), calls=%async_computation.1 | async-start | bytes 1048576 | tf_op jit(solution)/shard_map/all_to_all | solution.py:241
  45.6 21.4 %all-to-all-start.4 = ((bf16[32,128,128]{2,1,0:T(8,128)(2,1)}), bf16[32,128,128]{2,1,0:T(8,128)(2,1)S(1)}, u32[]{:S(2)}, u32[]{:S(2)}) async-start(bf16[32,128,128]{2,1,0:T(8,128)(2,1)} %copy-done.5), calls=%async_computation.4 | async-start | bytes 2097152 | tf_op jit(solution)/shard_map/all_to_all | solution.py:247
  66.9 26.3 %copy-start.1 = (bf16[32,128,128]{2,1,0:T(8,128)(2,1)}, bf16[32,128,128]{2,1,0:T(8,128)(2,1)S(1)}, u32[]{:S(2)}) copy-start(bf16[32,128,128]{2,1,0:T(8,128)(2,1)S(1)} %all-to-all-done.4.inbox) | copy-start | bytes 3145732
  87.0 23.1 %all-to-all-start.5 = ((bf16[32,128,128]{2,1,0:T(8,128)(2,1)}), bf16[32,128,128]{2,1,0:T(8,128)(2,1)}, u32[]{:S(2)}, u32[]{:S(2)}) async-start(bf16[32,128,128]{2,1,0:T(8,128)(2,1)} %copy-done.4), calls=%async_computation.5 | async-start | bytes 2097152 | tf_op jit(solution)/shard_map/all_to_all | solution.py:247
  92.7 73.2 %collective-permute-start.16 = (bf16[128,4096]{1,0:T(8,128)(2,1)}, bf16[128,4096]{1,0:T(8,128)(2,1)}, u32[]{:S(2)}, u32[]{:S(2)}) collective-permute-start(bf16[128,4096]{1,0:T(8,128)(2,1)} %grad.1), channel_id=1, source_target_pairs={{0,8},{8,0},{16,24},{24,16},{32,40},{40,32},{48,56},{56,48},{64,72... | collective-permute-start | bytes 3145736 | tf_op jit(solution)/shard_map/ppermute | solution.py:235
  96.3 18.8 %copy-start.21 = (s32[2,4]{1,0:T(2,128)S(1)}, s32[2,4]{1,0:T(2,128)}, u32[]{:S(2)}) copy-start(s32[2,4]{1,0:T(2,128)} %index.3) | copy-start | bytes 100
  96.4 54.6 %collective-permute-start = (bf16[8,128,512]{2,1,0:T(8,128)(2,1)S(1)}, bf16[8,128,512]{2,1,0:T(8,128)(2,1)}, u32[]{:S(2)}, u32[]{:S(2)}) collective-permute-start(bf16[8,128,512]{2,1,0:T(8,128)(2,1)S(1)} %copy_bitcast_fusion.mine), channel_id=1, source_target_pairs={{0,8},{8,0},{16,24},{24,16},{32,40},{40,32},{48,56},{56,48},{64,72... | collective-permute-start | bytes 3145736 | tf_op jit(solution)/shard_map/ppermute | solution.py:235
  110.9 47.1 %copy-start.22 = (s32[2]{0:T(128)S(1)}, s32[2]{0:T(128)}, u32[]{:S(2)}) copy-start(s32[2]{0:T(128)} %counts.1) | copy-start | bytes 28
  110.9 40.8 %all-to-all-start = ((bf16[8,128,256]{2,1,0:T(8,128)(2,1)}), bf16[8,128,256]{2,1,0:T(8,128)(2,1)}, u32[]{:S(2)}, u32[]{:S(2)}) async-start(bf16[8,128,256]{2,1,0:T(8,128)(2,1)} %broadcast_in_dim.18), calls=%async_computation | async-start | bytes 1048576 | tf_op jit(solution)/shard_map/all_to_all | solution.py:241
  119.0 12.2 %collective-permute-start.1 = (bf16[128,512]{1,0:T(8,128)(2,1)S(1)}, bf16[128,512]{1,0:T(8,128)(2,1)S(1)}, u32[]{:S(2)}, u32[]{:S(2)}) collective-permute-start(bf16[128,512]{1,0:T(8,128)(2,1)S(1)} %shard_map.106.refs_0_), channel_id=1, source_target_pairs={{0,7},{1,0},{2,1},{3,2},{4,3},{5,4},{6,5},{7,6},{8,15},{9,8},{10,9... | collective-permute-start | bytes 393224 | tf_op jit(solution)/shard_map/ppermute | solution.py:230
  124.6 9.3 %collective-permute-start.2 = (bf16[128,512]{1,0:T(8,128)(2,1)S(1)}, bf16[128,512]{1,0:T(8,128)(2,1)S(1)}, u32[]{:S(2)}, u32[]{:S(2)}) collective-permute-start(bf16[128,512]{1,0:T(8,128)(2,1)S(1)} %shard_map.107.refs_1_), channel_id=1, source_target_pairs={{0,7},{1,0},{2,1},{3,2},{4,3},{5,4},{6,5},{7,6},{8,15},{9,8},{10,9... | collective-permute-start | bytes 393224 | tf_op jit(solution)/shard_map/ppermute | solution.py:230
  125.9 10.6 %collective-permute-start.8 = (bf16[128,512]{1,0:T(8,128)(2,1)S(1)}, bf16[128,512]{1,0:T(8,128)(2,1)S(1)}, u32[]{:S(2)}, u32[]{:S(2)}) collective-permute-start(bf16[128,512]{1,0:T(8,128)(2,1)S(1)} %shard_map.107.refs_1_), channel_id=1, source_target_pairs={{0,1},{1,2},{2,3},{3,4},{4,5},{5,6},{6,7},{7,0},{8,9},{9,10},{10,1... | collective-permute-start | bytes 393224 | tf_op jit(solution)/shard_map/ppermute | solution.py:230
  131.3 6.9 %collective-permute-start.12 = (bf16[128,512]{1,0:T(8,128)(2,1)S(1)}, bf16[128,512]{1,0:T(8,128)(2,1)S(1)}, u32[]{:S(2)}, u32[]{:S(2)}) collective-permute-start(bf16[128,512]{1,0:T(8,128)(2,1)S(1)} %shard_map.106.refs_0_), channel_id=1, source_target_pairs={{0,1},{1,2},{2,3},{3,4},{4,5},{5,6},{6,7},{7,0},{8,9},{9,10},{10,1... | collective-permute-start | bytes 393224 | tf_op jit(solution)/shard_map/ppermute | solution.py:230
  134.0 5.3 %collective-permute-start.3 = (bf16[128,512]{1,0:T(8,128)(2,1)S(1)}, bf16[128,512]{1,0:T(8,128)(2,1)S(1)}, u32[]{:S(2)}, u32[]{:S(2)}) collective-permute-start(bf16[128,512]{1,0:T(8,128)(2,1)S(1)} %collective-permute-done.1.refs_2_), channel_id=1, source_target_pairs={{0,7},{1,0},{2,1},{3,2},{4,3},{5,4},{6,5},{7,6},{8,15},{9,8},{10,9... | collective-permute-start | bytes 393224 | tf_op jit(solution)/shard_map/ppermute | solution.py:230
  136.5 21.5 %copy-start.8 = (bf16[128,512]{1,0:T(8,128)(2,1)S(1)}, bf16[128,512]{1,0:T(8,128)(2,1)}, u32[]{:S(2)}) copy-start(bf16[128,512]{1,0:T(8,128)(2,1)} %copy-done.7) | copy-start | bytes 393220
  136.5 5.3 %collective-permute-start.4 = (bf16[128,512]{1,0:T(8,128)(2,1)S(1)}, bf16[128,512]{1,0:T(8,128)(2,1)}, u32[]{:S(2)}, u32[]{:S(2)}) collective-permute-start(bf16[128,512]{1,0:T(8,128)(2,1)S(1)} %collective-permute-done.2.refs_3_), channel_id=1, source_target_pairs={{0,7},{1,0},{2,1},{3,2},{4,3},{5,4},{6,5},{7,6},{8,15},{9,8},{10,9... | collective-permute-start | bytes 393224 | tf_op jit(solution)/shard_map/ppermute | solution.py:230
  138.1 6.9 %collective-permute-start.9 = (bf16[128,512]{1,0:T(8,128)(2,1)S(1)}, bf16[128,512]{1,0:T(8,128)(2,1)S(1)}, u32[]{:S(2)}, u32[]{:S(2)}) collective-permute-start(bf16[128,512]{1,0:T(8,128)(2,1)S(1)} %collective-permute-done.8.refs_15_), channel_id=1, source_target_pairs={{0,1},{1,2},{2,3},{3,4},{4,5},{5,6},{6,7},{7,0},{8,9},{9,10},{10,1... | collective-permute-start | bytes 393224 | tf_op jit(solution)/shard_map/ppermute | solution.py:230
  139.3 6.4 %collective-permute-start.13 = (bf16[128,512]{1,0:T(8,128)(2,1)S(1)}, bf16[128,512]{1,0:T(8,128)(2,1)}, u32[]{:S(2)}, u32[]{:S(2)}) collective-permute-start(bf16[128,512]{1,0:T(8,128)(2,1)S(1)} %collective-permute-done.12.refs_14_), channel_id=1, source_target_pairs={{0,1},{1,2},{2,3},{3,4},{4,5},{5,6},{6,7},{7,0},{8,9},{9,10},{10,1... | collective-permute-start | bytes 393224 | tf_op jit(solution)/shard_map/ppermute | solution.py:230
  141.8 6.6 %collective-permute-start.5 = (bf16[128,512]{1,0:T(8,128)(2,1)S(1)}, bf16[128,512]{1,0:T(8,128)(2,1)}, u32[]{:S(2)}, u32[]{:S(2)}) collective-permute-start(bf16[128,512]{1,0:T(8,128)(2,1)S(1)} %collective-permute-done.3.refs_4_), channel_id=1, source_target_pairs={{0,7},{1,0},{2,1},{3,2},{4,3},{5,4},{6,5},{7,6},{8,15},{9,8},{10,9... | collective-permute-start | bytes 393224 | tf_op jit(solution)/shard_map/ppermute | solution.py:230
  145.1 5.1 %collective-permute-start.10 = (bf16[128,512]{1,0:T(8,128)(2,1)S(1)}, bf16[128,512]{1,0:T(8,128)(2,1)}, u32[]{:S(2)}, u32[]{:S(2)}) collective-permute-start(bf16[128,512]{1,0:T(8,128)(2,1)S(1)} %collective-permute-done.9.refs_13_), channel_id=1, source_target_pairs={{0,1},{1,2},{2,3},{3,4},{4,5},{5,6},{6,7},{7,0},{8,9},{9,10},{10,1... | collective-permute-start | bytes 393224 | tf_op jit(solution)/shard_map/ppermute | solution.py:230
  145.7 8.5 %collective-permute-start.6 = (bf16[128,512]{1,0:T(8,128)(2,1)}, bf16[128,512]{1,0:T(8,128)(2,1)}, u32[]{:S(2)}, u32[]{:S(2)}) collective-permute-start(bf16[128,512]{1,0:T(8,128)(2,1)} %collective-permute-done.4.refs_5_), channel_id=1, source_target_pairs={{0,7},{1,0},{2,1},{3,2},{4,3},{5,4},{6,5},{7,6},{8,15},{9,8},{10,9... | collective-permute-start | bytes 393224 | tf_op jit(solution)/shard_map/ppermute | solution.py:230
  148.4 5.8 %collective-permute-start.14 = (bf16[128,512]{1,0:T(8,128)(2,1)}, bf16[128,512]{1,0:T(8,128)(2,1)}, u32[]{:S(2)}, u32[]{:S(2)}) collective-permute-start(bf16[128,512]{1,0:T(8,128)(2,1)} %collective-permute-done.13.refs_12_), channel_id=1, source_target_pairs={{0,1},{1,2},{2,3},{3,4},{4,5},{5,6},{6,7},{7,0},{8,9},{9,10},{10,1... | collective-permute-start | bytes 393224 | tf_op jit(solution)/shard_map/ppermute | solution.py:230
  150.2 4.3 %collective-permute-start.7 = (bf16[128,512]{1,0:T(8,128)(2,1)}, bf16[128,512]{1,0:T(8,128)(2,1)}, u32[]{:S(2)}, u32[]{:S(2)}) collective-permute-start(bf16[128,512]{1,0:T(8,128)(2,1)} %collective-permute-done.5.refs_6_), channel_id=1, source_target_pairs={{0,7},{1,0},{2,1},{3,2},{4,3},{5,4},{6,5},{7,6},{8,15},{9,8},{10,9... | collective-permute-start | bytes 393224 | tf_op jit(solution)/shard_map/ppermute | solution.py:230
  151.1 6.9 %collective-permute-start.11 = (bf16[128,512]{1,0:T(8,128)(2,1)}, bf16[128,512]{1,0:T(8,128)(2,1)}, u32[]{:S(2)}, u32[]{:S(2)}) collective-permute-start(bf16[128,512]{1,0:T(8,128)(2,1)} %collective-permute-done.10.refs_11_), channel_id=1, source_target_pairs={{0,1},{1,2},{2,3},{3,4},{4,5},{5,6},{6,7},{7,0},{8,9},{9,10},{10,1... | collective-permute-start | bytes 393224 | tf_op jit(solution)/shard_map/ppermute | solution.py:230
  151.7 6.3 %copy-start.14 = (bf16[128,512]{1,0:T(8,128)(2,1)S(1)}, bf16[128,512]{1,0:T(8,128)(2,1)}, u32[]{:S(2)}) copy-start(bf16[128,512]{1,0:T(8,128)(2,1)} %copy-done.13) | copy-start | bytes 393220
  151.7 6.3 %copy-start.16 = (bf16[128,512]{1,0:T(8,128)(2,1)S(1)}, bf16[128,512]{1,0:T(8,128)(2,1)}, u32[]{:S(2)}) copy-start(bf16[128,512]{1,0:T(8,128)(2,1)} %copy-done.15) | copy-start | bytes 393220
  151.8 6.3 %copy-start.18 = (bf16[128,512]{1,0:T(8,128)(2,1)S(1)}, bf16[128,512]{1,0:T(8,128)(2,1)}, u32[]{:S(2)}) copy-start(bf16[128,512]{1,0:T(8,128)(2,1)} %copy-done.17) | copy-start | bytes 393220
  151.8 6.3 %copy-start.19 = (bf16[128,256]{1,0:T(8,128)(2,1)S(1)}, bf16[128,256]{1,0:T(8,128)(2,1)}, u32[]{:S(2)}) copy-start(bf16[128,256]{1,0:T(8,128)(2,1)} %query.3) | copy-start | bytes 196612
  151.8 15.0 %copy-start.3 = (bf16[128,4096]{1,0:T(8,128)(2,1)S(1)}, bf16[128,4096]{1,0:T(8,128)(2,1)}, u32[]{:S(2)}) copy-start(bf16[128,4096]{1,0:T(8,128)(2,1)} %grad.1) | copy-start | bytes 3145732
  163.4 3.4 %collective-permute-start.15 = (bf16[128,128]{1,0:T(8,128)(2,1)S(1)}, bf16[128,128]{1,0:T(8,128)(2,1)S(1)}, u32[]{:S(2)}, u32[]{:S(2)}) collective-permute-start(bf16[128,128]{1,0:T(8,128)(2,1)S(1)} %get-tuple-element.9), channel_id=1, source_target_pairs={{0,8},{8,0},{16,24},{24,16},{32,40},{40,32},{48,56},{56,48},{64,72... | collective-permute-start | bytes 98312 | tf_op jit(solution)/shard_map/ppermute | solution.py:235
  (17 other events, 31.8 us)

commit v2 on v1

v2 whole, which is shorter than its diff:
```python
import functools
import math

import jax
import jax.numpy as jnp
from jax import lax
from jax.experimental import pallas as pl
from jax.experimental.pallas import tpu as pltpu
from jax.sharding import Mesh, PartitionSpec as P

DH = 128
BF = jnp.bfloat16
F32 = jnp.float32
VMEM = pl.BlockSpec(memory_space=pltpu.VMEM)
SMEM = pl.BlockSpec(memory_space=pltpu.SMEM)
HBM = pl.BlockSpec(memory_space=pltpu.HBM)
SEQ = ("chip", "core")
ANY = pl.BlockSpec(memory_space=pl.ANY)
NT = (((1,), (1,)), ((), ()))


def params(mebibytes=16):
    return pltpu.CompilerParams(vmem_limit_bytes=mebibytes * 1024 * 1024)


def tags_kernel(rows, index, out):
    spans, slots = index.shape
    for dest in range(out.shape[0]):
        out[dest, 0, 0] = 0
    for j in range(spans * slots):
        entry = index[j // slots, j % slots]
        out[entry // rows, 0, 0] = entry % rows + 1


def make_tags(rows, index, devices):
    return pl.pallas_call(
        functools.partial(tags_kernel, rows),
        out_shape=jax.ShapeDtypeStruct((devices, 1, 1), jnp.int32),
        in_specs=[SMEM],
        out_specs=SMEM,
    )(index)


def product_kernel(place, matrix, *refs):
    pieces, (out, left, sems) = refs[:-3], refs[-3:]
    part = left.shape[0] // len(pieces)
    copies = [
        pltpu.make_async_copy(p, left.at[pl.ds(i * part, part)], sems.at[i])
        for i, p in enumerate(pieces)
    ]
    for copy in copies:
        copy.start()
    for copy in copies:
        copy.wait()
    first = pl.multiple_of(place[1] * 2 * DH, 2 * DH)
    right = matrix[:, pl.ds(first, 2 * DH)]
    result = jnp.dot(left[...], right, preferred_element_type=F32).astype(BF)
    for p in range(out.shape[0]):
        out[p] = result


def multiply(place, matrix, pieces, copies):
    return pl.pallas_call(
        product_kernel,
        out_shape=jax.ShapeDtypeStruct((copies, len(pieces) * pieces[0].shape[0], 2 * DH), BF),
        in_specs=[SMEM, VMEM] + [ANY] * len(pieces),
        out_specs=VMEM,
        scratch_shapes=[
            pltpu.VMEM((len(pieces) * pieces[0].shape[0], pieces[0].shape[1]), BF),
            pltpu.SemaphoreType.DMA((len(pieces),)),
        ],
        compiler_params=params(),
    )(place, matrix, *pieces)


def outbox_kernel(tags, query, out, sems):
    count = out.shape[0]

    def copy(dest):
        return pltpu.make_async_copy(query.at[tags[dest, 0, 0] - 1], out.at[dest], sems.at[dest])

    for dest in range(count):

        @pl.when(tags[dest, 0, 0] > 0)
        def _():
            copy(dest).start()

    for dest in range(count):

        @pl.when(tags[dest, 0, 0] > 0)
        def _():
            copy(dest).wait()


def outbox(tags, query, buckets):
    return pl.pallas_call(
        outbox_kernel,
        out_shape=jax.ShapeDtypeStruct((buckets,) + query.shape[1:], BF),
        in_specs=[SMEM, VMEM],
        out_specs=HBM,
        scratch_shapes=[pltpu.SemaphoreType.DMA((buckets,))],
        compiler_params=params(60),
    )(tags, query)


def encode_kernel(rows, index, inbox, pairs, out0, out1, held, sems):
    spans, slots = index.shape
    span_len = pairs.shape[0] // spans
    copies = []
    for j in range(spans * slots):
        home = index[j // slots, j % slots] // rows
        copies.append(pltpu.make_async_copy(inbox.at[home], held.at[j], sems.at[j]))
        copies[-1].start()
    for j in range(spans * slots):
        c, k = j // slots, j % slots
        copies[j].wait()
        for head, out in enumerate((out0, out1)):
            at = slice(head * DH, (head + 1) * DH)
            keys = pairs[c * span_len : (c + 1) * span_len, at]
            scores = lax.dot_general(
                keys, held[j, :, at], NT, preferred_element_type=F32
            ) / math.sqrt(DH)
            exponent = jnp.exp(scores - jnp.max(scores, axis=0, keepdims=True))
            weights = exponent / jnp.sum(exponent, axis=0, keepdims=True)
            out[c * span_len : (c + 1) * span_len, k * DH : (k + 1) * DH] = weights.astype(BF)
    tokens = pairs.shape[0]
    rows = tokens // slots
    for head, out in enumerate((out0, out1)):
        values = pairs[:, (2 + head) * DH : (3 + head) * DH]
        out[tokens:] = jnp.concatenate(
            [values[k * rows : (k + 1) * rows] for k in range(slots)], axis=1
        )


def encode(index, inbox, pairs):
    spans, slots = index.shape
    tokens = pairs.shape[0]
    shape = jax.ShapeDtypeStruct((tokens + tokens // slots, slots * inbox.shape[1]), BF)
    return pl.pallas_call(
        functools.partial(encode_kernel, spans * slots),
        out_shape=(shape, shape),
        in_specs=[SMEM, HBM, VMEM],
        out_specs=(VMEM, VMEM),
        scratch_shapes=[
            pltpu.VMEM((spans * slots,) + inbox.shape[1:], BF),
            pltpu.SemaphoreType.DMA((spans * slots,)),
        ],
        compiler_params=params(),
    )(index, inbox, pairs)


def absorb_kernel(tokens, *refs):
    weights, values = refs[-2:]
    spans = weights.shape[0]
    span_len = tokens // spans
    for i, piece in enumerate(refs[:-2]):
        for c in range(spans):
            weights[c, i * span_len : (i + 1) * span_len] = piece[
                c * span_len : (c + 1) * span_len
            ]
        values[i] = piece[tokens:]


def absorb(tokens, spans, pieces):
    total, width = pieces[0].shape
    return pl.pallas_call(
        functools.partial(absorb_kernel, tokens),
        out_shape=(
            jax.ShapeDtypeStruct((spans, len(pieces) * tokens // spans, width), BF),
            jax.ShapeDtypeStruct((len(pieces), total - tokens, width), BF),
        ),
        in_specs=[VMEM] * len(pieces),
        out_specs=(VMEM, VMEM),
        compiler_params=params(),
    )(*pieces)


def decode_kernel(part, order, place, counts, query, mine, *refs):
    out, send, folded, weights, values, held, sems = refs[-7:]
    groups = mine.shape[1] // part
    late = refs[:-10]
    spans = folded.shape[0]
    tokens = query.shape[0]
    span_len = tokens // spans
    core = place[1]
    slots = weights.shape[2] // DH
    slot_tokens = slots * DH
    copies = [
        pltpu.make_async_copy(source, target, sems.at[i])
        for i, (source, target) in enumerate(zip(refs[-10:-7], (values, held, weights)))
    ]
    for copy in copies:
        copy.start()
    copies[0].wait()

    def riding(i):
        first = values.shape[0]
        rows = values[i] if i < first else late[i - first][tokens:]
        return jnp.concatenate([rows[:, k * DH : (k + 1) * DH] for k in range(slots)], axis=0)

    for which, near in ((core, mine), (1 - core, held)):
        if near is held:
            copies[1].wait()
        for n, g in enumerate(order):
            at = slice(g * part, (g + 1) * part)
            rows = jnp.concatenate([near[p, at] for p in range(near.shape[0])], axis=0)
            low = jnp.dot(riding(2 * n), rows[:DH], preferred_element_type=F32)
            high = jnp.dot(riding(2 * n + 1), rows[DH:], preferred_element_type=F32)
            for c in range(spans):
                span = slice(c * span_len, (c + 1) * span_len)
                both = jnp.concatenate([low[span], high[span]], axis=0)
                first = pl.multiple_of(which * 2 * DH, 2 * DH)
                columns = slice(n * 2 * span_len, (n + 1) * 2 * span_len)
                folded[c, pl.ds(first, 2 * DH), columns] = both.T.astype(BF)
    copies[2].wait()
    early = weights.shape[1]
    for c in range(spans):
        rest = jnp.concatenate([p[c * span_len : (c + 1) * span_len] for p in late], axis=0)
        both = jnp.dot(folded[c, :, :early], weights[c], preferred_element_type=F32)
        both += jnp.dot(folded[c, :, early:], rest, preferred_element_type=F32)
        both = both.astype(BF)
        usable = lax.broadcasted_iota(jnp.int32, (span_len, slot_tokens), 1) < counts[c] * DH
        for h in range(2):
            at = slice(c * span_len, (c + 1) * span_len)
            keys = both[h * DH : (h + 1) * DH]
            head_values = both[(2 + h) * DH : (3 + h) * DH]
            scores = jnp.dot(
                query[at, h * DH : (h + 1) * DH], keys, preferred_element_type=F32
            ) / math.sqrt(DH)
            scores = jnp.where(usable, scores, -1e30)
            exponent = jnp.exp(scores - jnp.max(scores, axis=1, keepdims=True))
            share = (exponent / jnp.sum(exponent, axis=1, keepdims=True)).astype(BF)
            result = lax.dot_general(share, head_values, NT, preferred_element_type=F32)
            out[at, h * DH : (h + 1) * DH] = result.astype(BF)
    send[...] = jnp.where(core == 0, out[:, DH:], out[:, :DH])


def decode(place, counts, query, mine, held, values, late, other, order):
    tokens, width = query.shape
    spans = counts.shape[0]
    groups = len(order)
    part = mine.shape[1] // groups
    return pl.pallas_call(
        functools.partial(decode_kernel, part, order),
        out_shape=(
            jax.ShapeDtypeStruct((tokens, width), BF),
            jax.ShapeDtypeStruct((tokens, DH), BF),
        ),
        in_specs=[SMEM, SMEM] + [VMEM] * (2 + len(late)) + [ANY] * 3,
        out_specs=(VMEM, VMEM),
        scratch_shapes=[
            pltpu.VMEM((spans, 4 * DH, 2 * groups * tokens // spans), BF),
            pltpu.VMEM(held.shape, BF),
            pltpu.VMEM(values.shape, BF),
            pltpu.VMEM(mine.shape, BF),
            pltpu.SemaphoreType.DMA((3,)),
        ],
        compiler_params=params(),
    )(place, counts, query, mine, *late, values, other, held)


def partial_kernel(place, attended, near, grad, near_grad, out):
    own = jnp.where(place[1] == 0, attended[:, :DH], attended[:, DH:])
    left = jnp.concatenate([own, near[...]], axis=0).T
    half = left.shape[1] // 2
    chunk = grad.shape[1] // out.shape[0]
    wide = 4
    for s in range(0, out.shape[0], wide):
        at = slice(s * chunk, (s + wide) * chunk)
        term = jnp.dot(left[:, :half], grad[:, at], preferred_element_type=F32)
        term += jnp.dot(left[:, half:], near_grad[:, at], preferred_element_type=F32)
        term = term.astype(BF)
        for i in range(wide):
            out[s + i] = term[:, i * chunk : (i + 1) * chunk]


def partial_grad(place, attended, near, grad, near_grad, buckets):
    return pl.pallas_call(
        partial_kernel,
        out_shape=jax.ShapeDtypeStruct((buckets, DH, grad.shape[1] // buckets), BF),
        in_specs=[SMEM, VMEM, VMEM, VMEM, VMEM],
        out_specs=VMEM,
        compiler_params=params(),
    )(place, attended, near, grad, near_grad)


def total_kernel(parts, out):
    for core in range(2):
        total = parts[core].astype(F32)
        for p in range(1, parts.shape[0] // 2):
            total += parts[2 * p + core].astype(F32)
        out[core * DH : (core + 1) * DH] = total


def total_grad(parts):
    return pl.pallas_call(
        total_kernel,
        out_shape=jax.ShapeDtypeStruct((2 * DH, parts.shape[2]), F32),
        in_specs=[VMEM],
        out_specs=VMEM,
        compiler_params=params(),
    )(parts)


def shift(x, axis, step):
    n = lax.axis_size(axis)
    return lax.ppermute(x, axis, [(i, (i + step) % n) for i in range(n)])


def sibling(x):
    return lax.ppermute(x, "core", [(0, 1), (1, 0)])


def exchange_over(x, axis):
    return lax.all_to_all(x, axis, split_axis=0, concat_axis=0, tiled=True)


def exchange(x):
    return lax.all_to_all(x, SEQ, split_axis=0, concat_axis=0, tiled=True)


def local(
    span_states, dec_query, nbr_query, nbr_index, nbr_count, wkv_enc, wo_enc, wkv_dec, grad_out
):
    chips = lax.axis_size("chip")
    devices = 2 * chips
    groups = lax.axis_size("mp")
    chip, core, z = lax.axis_index("chip"), lax.axis_index("core"), lax.axis_index("mp")
    place = jnp.stack([z, core]).astype(jnp.int32)
    spans = nbr_count.shape[0]
    rows = nbr_query.shape[0]
    hidden = span_states.shape[1]

    def ring(x, forward):
        up = [x]
        down = [x]
        for _ in range(3):
            up.append(shift(up[-1], "mp", -1))
            down.append(shift(down[-1], "mp", 1))
        last = shift(up[-1], "mp", -1) if forward else shift(down[-1], "mp", 1)
        return up + [last] + down[:0:-1]

    tags = exchange(make_tags(rows, nbr_index, devices))

    pairs = jnp.dot(
        span_states, wkv_enc.reshape(hidden, -1), preferred_element_type=F32
    ).astype(BF)
    part = 2 * DH // chips
    wo_rows = lax.dynamic_slice_in_dim(wo_enc, chip * part, part, 0)
    tags, wo_rows, pairs = lax.optimization_barrier((tags, wo_rows, pairs))

    box = outbox(tags, nbr_query, devices)
    box, wkv_dec, wo_rows, pairs = lax.optimization_barrier((box, wkv_dec, wo_rows, pairs))
    inbox = exchange(box)

    wo_rows = ring(wo_rows, True)
    product = multiply(place, wkv_dec.reshape(hidden, -1), wo_rows, chips)
    grad_near = sibling(grad_out)
    inbox, product, grad_near = lax.optimization_barrier((inbox, product, grad_near))

    w0, w1 = encode(nbr_index, inbox, pairs)
    product = exchange_over(product, "chip")

    up, down = [[w0, w1]], [[w0, w1]]
    for _ in range(3):
        up.append([shift(w, "mp", -1) for w in up[-1]])
        down.append([shift(w, "mp", 1) for w in down[-1]])
    first = [w0, w1] + up[1] + down[1] + up[2] + down[2]
    held, values = absorb(pairs.shape[0], spans, first)
    held, values, up[3][0], down[3][1], product = lax.optimization_barrier(
        (held, values, up[3][0], down[3][1], product)
    )
    far = sibling(product)
    last = [shift(up[3][0], "mp", -1), shift(down[3][1], "mp", 1)]
    order = (0, 1, groups - 1, 2, groups - 2, 3, groups - 3, 4)
    attended, send = decode(
        place, nbr_count, dec_query, product, held, values, up[3] + down[3] + last, far, order
    )

    near = sibling(send)
    parts = exchange(partial_grad(place, attended, near, grad_out, grad_near, devices))
    return attended, total_grad(parts)


def solution(mesh):
    devices = mesh.devices
    fine = Mesh(devices.reshape(-1, 2, devices.shape[1]), SEQ + ("mp",))
    return jax.shard_map(
        local,
        mesh=fine,
        in_specs=(
            P(SEQ, None),
            P(SEQ, "mp"),
            P(SEQ, None, "mp"),
            P(SEQ, None),
            P(SEQ),
            P(None, None, "mp"),
            P("mp", None),
            P(None, None, "mp"),
            P(SEQ, None),
        ),
        out_specs=(P(SEQ, "mp"), P("mp", SEQ)),
        check_vma=False,
    )
```

time: 192 us -> 146 us (0.76)
  waiting for transfers between devices: 61.7 us -> 20 us
  blocking collectives: 41.1 us -> 25.2 us
  starting transfers between devices: 48.4 us -> 64.2 us
  local copies, waits for them, and re-layouts: 18.5 us -> 13.2 us
    all_to_all x5 -> x3, waiting for transfers between devices: 45.6 us -> 0.01 us  [the longest x2 0.01 us: exchange(): return lax.all_to_all(x, SEQ, split_axis=0, concat_axis=0, tiled=True)]
    ppermute x14 -> x21, starting transfers between devices: 14.3 us -> 33.2 us  [shift(): return lax.ppermute(x, axis, [(i, (i + step) % n) for i in range(n)])]
    all_to_all x2 -> x1, blocking collectives: 41.1 us -> 25.2 us  [exchange(): return lax.all_to_all(x, SEQ, split_axis=0, concat_axis=0, tiled=True)]
    all_to_all x5 -> x3, starting transfers between devices: 30.9 us -> 22.8 us  [the longest x2 16 us: exchange(): return lax.all_to_all(x, SEQ, split_axis=0, concat_axis=0, tiled=True)]
    ppermute x3, starting transfers between devices: 3.2 us -> 8.23 us  [sibling(): return lax.ppermute(x, 'core', [(0, 1), (1, 0)])]
    ppermute x14 -> x21, waiting for transfers between devices: 15.2 us -> 19.1 us  [shift(): return lax.ppermute(x, axis, [(i, (i + step) % n) for i in range(n)])]
    unnamed x56 -> x36, local copies, waits for them, and re-layouts: 15.9 us -> 13.2 us
    dot_general x1, matrix products: 0.72 us -> 2.9 us  [local(): jnp.dot(span_states, wkv_enc.reshape(hidden, -1), preferred_element_type=...]
  transfers between devices with their start and end apart: 22 -> 27, of which waited for: 11 -> 12; matrix products, arithmetic and copies ran while one was open for 5% -> 8% of each run, Pallas kernels for 8% -> 5%
where the time goes in v2:
time: 146 us; the launch traced here: 145 us
  starting transfers between devices  64.2 us (44%)
  blocking collectives  25.2 us (17%)
  waiting for transfers between devices  20 us (14%)
  Pallas kernels  19 us (13%)
  local copies, waits for them, and re-layouts  13.2 us (9%)
  matrix products  2.9 us (2%)
    ppermute x21, starting transfers between devices, shift(): return lax.ppermute(x, axis, [(i, (i + step) % n) for i in range(n)])  33.2 us
    all_to_all x1, blocking collectives, exchange(): return lax.all_to_all(x, SEQ, split_axis=0, concat_axis=0, tiled=True)  25.2 us
    ppermute x21, waiting for transfers between devices, shift(): return lax.ppermute(x, axis, [(i, (i + step) % n) for i in range(n)])  19.1 us
    all_to_all x2, starting transfers between devices, exchange(): return lax.all_to_all(x, SEQ, split_axis=0, concat_axis=0, tiled=True)  16 us
    unnamed x36, local copies, waits for them, and re-layouts  13.2 us
    ppermute x3, starting transfers between devices, sibling(): return lax.ppermute(x, 'core', [(0, 1), (1, 0)])  8.23 us
    all_to_all x1, starting transfers between devices, exchange_over(): return lax.all_to_all(x, axis, split_axis=0, concat_axis=0, tiled=True)  6.73 us
    pallas_call x1, Pallas kernels, decode(): pl.pallas_call(functools.partial(decode_kernel, part, order), out_shape=(...  5.46 us
  transfers between devices with their start and end apart: 27, of which 12 were waited for; matrix products, arithmetic and copies ran while one was open for 8% of the time, Pallas kernels for 5%

profile of v2, /device:TPU:1, one launch (start us, length us, event | category | flops | bytes accessed | tf_op | source)
XLA Modules:
  0.0 145.4 jit_solution(6079153104828186958)
XLA Ops:
  0.6 1.7 %shard_map.104 = s32[32,1,1]{2,1,0:T(1,128)} custom-call(s32[2,4]{1,0:T(2,128)} %index.3), custom_call_target="tpu_custom_call" | custom-call | tf_op jit(solution)/shard_map/pallas_call | solution.py:36
  2.3 8.6 %all-to-all-start = ((s32[32,1,1]{2,1,0:T(1,128)}), s32[32,1,1]{2,1,0:T(1,128)S(1)}, u32[]{:S(2)}, u32[]{:S(2)}) async-start(s32[32,1,1]{2,1,0:T(1,128)} %shard_map.104), calls=%async_computation | async-start | bytes 32768 | tf_op jit(solution)/shard_map/all_to_all | solution.py:319
  10.9 5.0 %copy.11 = bf16[512,8,2,256]{3,1,2,0:T(8,128)(2,1)} copy(bf16[512,8,2,256]{3,2,1,0:T(2,128)(2,1)} %bitcast.10) | data formatting | bytes 8388608
  15.9 2.9 %convolution_convert_fusion.pairs = bf16[128,512]{1,0:T(8,128)(2,1)S(1)} fusion(bf16[128,4096]{1,0:T(8,128)(2,1)S(1)} %copy-done.15, bf16[4096,512]{1,0:T(8,128)(2,1)} %bitcast.9), kind=kOutput, calls=%fused_computation | convolution fusion | flops 536936448 | bytes 5373952 | tf_op jit(solution)/shard_map/dot_general | solution.py:345
  19.5 2.2 %shard_map.105 = bf16[32,128,256]{2,1,0:T(8,128)(2,1)} custom-call(s32[32,1,1]{2,1,0:T(1,128)} %copy-done.16, bf16[8,128,256]{2,1,0:T(8,128)(2,1)} %query.2), custom_call_target="tpu_custom_call" | custom-call | tf_op jit(solution)/shard_map/pallas_call | solution.py:96
  21.6 7.4 %all-to-all-start.1 = ((bf16[32,128,256]{2,1,0:T(8,128)(2,1)}), bf16[32,128,256]{2,1,0:T(8,128)(2,1)}, u32[]{:S(2)}, u32[]{:S(2)}) async-start(bf16[32,128,256]{2,1,0:T(8,128)(2,1)} %shard_map.105), calls=%async_computation.1 | async-start | bytes 4194304 | tf_op jit(solution)/shard_map/all_to_all | solution.py:319
  29.5 5.6 %collective-permute-start = (bf16[16,4096]{1,0:T(8,128)(2,1)S(1)}, bf16[16,4096]{1,0:T(8,128)(2,1)S(1)}, u32[]{:S(2)}, u32[]{:S(2)}) collective-permute-start(bf16[16,4096]{1,0:T(8,128)(2,1)S(1)} %constant_dynamic-slice_fusion.refs_0_), channel_id=1, source_target_pairs={{0,7},{1,0},{2,1},{3,2},{4,3},{5,4},{6,5},{7,6},{8,15},{9,8},{10,9... | collective-permute-start | bytes 393224 | tf_op jit(solution)/shard_map/ppermute | solution.py:307
  35.1 2.7 %collective-permute-done.refs_1_ = bf16[16,4096]{1,0:T(8,128)(2,1)S(1)} collective-permute-done((bf16[16,4096]{1,0:T(8,128)(2,1)S(1)}, bf16[16,4096]{1,0:T(8,128)(2,1)S(1)}, u32[]{:S(2)}, u32[]{:S(2)}) %collective-permute-start) | collective-permute-done | bytes 131104 | tf_op jit(solution)/shard_map/ppermute | solution.py:307
  37.8 3.5 %collective-permute-start.1 = (bf16[16,4096]{1,0:T(8,128)(2,1)S(1)}, bf16[16,4096]{1,0:T(8,128)(2,1)S(1)}, u32[]{:S(2)}, u32[]{:S(2)}) collective-permute-start(bf16[16,4096]{1,0:T(8,128)(2,1)S(1)} %collective-permute-done.refs_1_), channel_id=1, source_target_pairs={{0,7},{1,0},{2,1},{3,2},{4,3},{5,4},{6,5},{7,6},{8,15},{9,8},{10,9... | collective-permute-start | bytes 393224 | tf_op jit(solution)/shard_map/ppermute | solution.py:307
  42.0 1.3 collective-permute-done.1.refs_2_
  43.2 3.5 %collective-permute-start.2 = (bf16[16,4096]{1,0:T(8,128)(2,1)S(1)}, bf16[16,4096]{1,0:T(8,128)(2,1)}, u32[]{:S(2)}, u32[]{:S(2)}) collective-permute-start(bf16[16,4096]{1,0:T(8,128)(2,1)S(1)} %collective-permute-done.1.refs_2_), channel_id=1, source_target_pairs={{0,7},{1,0},{2,1},{3,2},{4,3},{5,4},{6,5},{7,6},{8,15},{9,8},{10,9... | collective-permute-start | bytes 393224 | tf_op jit(solution)/shard_map/ppermute | solution.py:307
  47.4 1.3 collective-permute-done.2.refs_3_
  48.7 3.5 %collective-permute-start.3 = (bf16[16,4096]{1,0:T(8,128)(2,1)}, bf16[16,4096]{1,0:T(8,128)(2,1)}, u32[]{:S(2)}, u32[]{:S(2)}) collective-permute-start(bf16[16,4096]{1,0:T(8,128)(2,1)} %collective-permute-done.2.refs_3_), channel_id=1, source_target_pairs={{0,7},{1,0},{2,1},{3,2},{4,3},{5,4},{6,5},{7,6},{8,15},{9,8},{10,9... | collective-permute-start | bytes 393224 | tf_op jit(solution)/shard_map/ppermute | solution.py:307
  52.2 3.0 %copy.12 = bf16[512,8,2,256]{3,1,2,0:T(8,128)(2,1)S(1)} copy(bf16[512,8,2,256]{3,2,1,0:T(2,128)(2,1)} %bitcast.11) | data formatting | bytes 8388608
  55.2 3.7 %shard_map.106 = bf16[16,128,256]{2,1,0:T(8,128)(2,1)} custom-call(s32[2]{0:T(128)S(1)} %pad_add_fusion.place, bf16[4096,512]{1,0:T(8,128)(2,1)S(1)} %bitcast.8, bf16[16,4096]{1,0:T(8,128)(2,1)S(1)} %constant_dynamic-slice_fusion.refs_0_, bf16[16,4096]{1,0:T(8,128)(2,1)S(1)} %collective-permute-done.refs_1_, bf16[16,4096]{1,0:T(8,128)(2,1)S(1)} %copy-done.10, ...), custom_call_target="tpu_custom_call" | custom-call | tf_op jit(solution)/shard_map/pallas_call | solution.py:63
  59.0 6.7 %all-to-all-start.2 = ((bf16[16,128,256]{2,1,0:T(8,128)(2,1)}), bf16[16,128,256]{2,1,0:T(8,128)(2,1)S(1)}, u32[]{:S(2)}, u32[]{:S(2)}) async-start(bf16[16,128,256]{2,1,0:T(8,128)(2,1)} %shard_map.106), calls=%async_computation.2 | async-start | bytes 2097152 | tf_op jit(solution)/shard_map/all_to_all | solution.py:315
  65.8 3.1 %shard_map.107 = (bf16[160,512]{1,0:T(8,128)(2,1)S(1)}, bf16[160,512]{1,0:T(8,128)(2,1)S(1)}) custom-call(s32[2,4]{1,0:T(2,128)S(1)} %copy-done.13, bf16[32,128,256]{2,1,0:T(8,128)(2,1)} %all-to-all-done.1.inbox, bf16[128,512]{1,0:T(8,128)(2,1)S(1)} %convolution_convert_fusion.pairs), custom_call_target="tpu_custom_call" | custom-call | tf_op jit(solution)/shard_map/pallas_call | solution.py:139
  68.9 2.5 %collective-permute-start.8 = (bf16[160,512]{1,0:T(8,128)(2,1)S(1)}, bf16[160,512]{1,0:T(8,128)(2,1)S(1)}, u32[]{:S(2)}, u32[]{:S(2)}) collective-permute-start(bf16[160,512]{1,0:T(8,128)(2,1)S(1)} %get-tuple-element.31.refs_0_), channel_id=1, source_target_pairs={{0,7},{1,0},{2,1},{3,2},{4,3},{5,4},{6,5},{7,6},{8,15},{9,8},{10,9... | collective-permute-start | bytes 491528 | tf_op jit(solution)/shard_map/ppermute | solution.py:307
  71.3 2.7 %collective-permute-start.9 = (bf16[160,512]{1,0:T(8,128)(2,1)S(1)}, bf16[160,512]{1,0:T(8,128)(2,1)S(1)}, u32[]{:S(2)}, u32[]{:S(2)}) collective-permute-start(bf16[160,512]{1,0:T(8,128)(2,1)S(1)} %get-tuple-element.32.refs_1_), channel_id=1, source_target_pairs={{0,7},{1,0},{2,1},{3,2},{4,3},{5,4},{6,5},{7,6},{8,15},{9,8},{10,9... | collective-permute-start | bytes 491528 | tf_op jit(solution)/shard_map/ppermute | solution.py:307
  74.0 3.0 %collective-permute-start.12 = (bf16[160,512]{1,0:T(8,128)(2,1)S(1)}, bf16[160,512]{1,0:T(8,128)(2,1)S(1)}, u32[]{:S(2)}, u32[]{:S(2)}) collective-permute-start(bf16[160,512]{1,0:T(8,128)(2,1)S(1)} %collective-permute-done.8.refs_2_), channel_id=1, source_target_pairs={{0,7},{1,0},{2,1},{3,2},{4,3},{5,4},{6,5},{7,6},{8,15},{9,8},{10,9... | collective-permute-start | bytes 491528 | tf_op jit(solution)/shard_map/ppermute | solution.py:307
  77.0 2.7 %collective-permute-start.13 = (bf16[160,512]{1,0:T(8,128)(2,1)S(1)}, bf16[160,512]{1,0:T(8,128)(2,1)S(1)}, u32[]{:S(2)}, u32[]{:S(2)}) collective-permute-start(bf16[160,512]{1,0:T(8,128)(2,1)S(1)} %collective-permute-done.9.refs_3_), channel_id=1, source_target_pairs={{0,7},{1,0},{2,1},{3,2},{4,3},{5,4},{6,5},{7,6},{8,15},{9,8},{10,9... | collective-permute-start | bytes 491528 | tf_op jit(solution)/shard_map/ppermute | solution.py:307
  80.1 3.4 %collective-permute-start.16 = (bf16[160,512]{1,0:T(8,128)(2,1)S(1)}, bf16[160,512]{1,0:T(8,128)(2,1)}, u32[]{:S(2)}, u32[]{:S(2)}) collective-permute-start(bf16[160,512]{1,0:T(8,128)(2,1)S(1)} %collective-permute-done.12.refs_6_), channel_id=1, source_target_pairs={{0,7},{1,0},{2,1},{3,2},{4,3},{5,4},{6,5},{7,6},{8,15},{9,8},{10,9... | collective-permute-start | bytes 491528 | tf_op jit(solution)/shard_map/ppermute | solution.py:307
  83.6 3.0 %collective-permute-done.14.refs_8_ = bf16[160,512]{1,0:T(8,128)(2,1)S(1)} collective-permute-done((bf16[160,512]{1,0:T(8,128)(2,1)S(1)}, bf16[160,512]{1,0:T(8,128)(2,1)S(1)}, u32[]{:S(2)}, u32[]{:S(2)}) %collective-permute-start.14) | collective-permute-done | bytes 163872 | tf_op jit(solution)/shard_map/ppermute | solution.py:307
  87.9 2.5 %collective-permute-done.17.refs_3_ = bf16[160,512]{1,0:T(8,128)(2,1)} collective-permute-done((bf16[160,512]{1,0:T(8,128)(2,1)S(1)}, bf16[160,512]{1,0:T(8,128)(2,1)}, u32[]{:S(2)}, u32[]{:S(2)}) %collective-permute-start.17) | collective-permute-done | bytes 163872 | tf_op jit(solution)/shard_map/ppermute | solution.py:307
  90.4 6.9 %collective-permute-start.22 = (bf16[16,128,256]{2,1,0:T(8,128)(2,1)S(1)}, bf16[16,128,256]{2,1,0:T(8,128)(2,1)S(1)}, u32[]{:S(2)}, u32[]{:S(2)}) collective-permute-start(bf16[16,128,256]{2,1,0:T(8,128)(2,1)S(1)} %all-to-all-done.2.mine), channel_id=1, source_target_pairs={{0,8},{8,0},{1,9},{9,1},{2,10},{10,2},{3,11},{11,3},{4,12},{12,4},... | collective-permute-start | bytes 3145736 | tf_op jit(solution)/shard_map/ppermute | solution.py:311
  97.3 1.5 %collective-permute-start.19 = (bf16[160,512]{1,0:T(8,128)(2,1)}, bf16[160,512]{1,0:T(8,128)(2,1)S(1)}, u32[]{:S(2)}, u32[]{:S(2)}) collective-permute-start(bf16[160,512]{1,0:T(8,128)(2,1)} %copy-done.6), channel_id=1, source_target_pairs={{0,1},{1,2},{2,3},{3,4},{4,5},{5,6},{6,7},{7,0},{8,9},{9,10},{10,1... | collective-permute-start | bytes 491528 | tf_op jit(solution)/shard_map/ppermute | solution.py:307
  100.2 3.1 %collective-permute-done.18.refs_1_ = bf16[160,512]{1,0:T(8,128)(2,1)S(1)} collective-permute-done((bf16[160,512]{1,0:T(8,128)(2,1)}, bf16[160,512]{1,0:T(8,128)(2,1)S(1)}, u32[]{:S(2)}, u32[]{:S(2)}) %collective-permute-start.18) | collective-permute-done | bytes 163872 | tf_op jit(solution)/shard_map/ppermute | solution.py:307
  104.5 2.4 %collective-permute-done.20.refs_4_ = bf16[160,512]{1,0:T(8,128)(2,1)S(1)} collective-permute-done((bf16[160,512]{1,0:T(8,128)(2,1)}, bf16[160,512]{1,0:T(8,128)(2,1)S(1)}, u32[]{:S(2)}, u32[]{:S(2)}) %collective-permute-start.20) | collective-permute-done | bytes 163872 | tf_op jit(solution)/shard_map/ppermute | solution.py:307
  108.0 1.3 copy-done.2
  109.3 5.5 %shard_map.109 = (bf16[128,256]{1,0:T(8,128)(2,1)}, bf16[128,128]{1,0:T(8,128)(2,1)S(1)}) custom-call(s32[2]{0:T(128)S(1)} %pad_add_fusion.place, s32[2]{0:T(128)S(1)} %copy-done.14, bf16[128,256]{1,0:T(8,128)(2,1)S(1)} %copy-done.12, bf16[16,128,256]{2,1,0:T(8,128)(2,1)S(1)} %all-to-all-done.2.mine, bf16[160,512]{1,0:T(8,128)(2,1)} %collective-permute-done.16.refs_0_, ...), custom_call_target="tpu_custom_call" | custom-call | tf_op jit(solution)/shard_map/pallas_call | solution.py:243
  117.5 2.0 %shard_map.110 = bf16[32,128,128]{2,1,0:T(8,128)(2,1)S(1)} custom-call(s32[2]{0:T(128)S(1)} %pad_add_fusion.place, bf16[128,256]{1,0:T(8,128)(2,1)S(1)} %copy-done.11, bf16[128,128]{1,0:T(8,128)(2,1)S(1)} %collective-permute-done.23.near, bf16[128,4096]{1,0:T(8,128)(2,1)S(1)} %copy-done.4, bf16[128,4096]{1,0:T(8,128)(2,1)} %collective-permute-done.7.near_grad), custom_call_target="tpu_custom_call" | custom-call | tf_op jit(solution)/shard_map/pallas_call | solution.py:278
  119.4 25.2 %all_to_all.20.parts = bf16[32,128,128]{2,1,0:T(8,128)(2,1)S(1)} all-to-all(bf16[32,128,128]{2,1,0:T(8,128)(2,1)S(1)} %shard_map.110), channel_id=1, replica_groups=mesh['chip'=16,'core'=2,'mp'=8] {'chip','core'}, dimensions={0} | all-to-all | bytes 2097152 | tf_op jit(solution)/shard_map/all_to_all | solution.py:319
  (70 shorter events, 11.4 us)
Async XLA Ops:
  0.6 15.3 %copy-start = (bf16[256,4096]{1,0:T(8,128)(2,1)S(1)}, bf16[256,4096]{1,0:T(8,128)(2,1)}, u32[]{:S(2)}) copy-start(bf16[256,4096]{1,0:T(8,128)(2,1)} %param.15) | copy-start | bytes 6291460
  2.3 16.5 %all-to-all-start = ((s32[32,1,1]{2,1,0:T(1,128)}), s32[32,1,1]{2,1,0:T(1,128)S(1)}, u32[]{:S(2)}, u32[]{:S(2)}) async-start(s32[32,1,1]{2,1,0:T(1,128)} %shard_map.104), calls=%async_computation | async-start | bytes 32768 | tf_op jit(solution)/shard_map/all_to_all | solution.py:319
  18.8 10.3 %copy-start.3 = (bf16[128,4096]{1,0:T(8,128)(2,1)S(1)}, bf16[128,4096]{1,0:T(8,128)(2,1)}, u32[]{:S(2)}) copy-start(bf16[128,4096]{1,0:T(8,128)(2,1)} %grad.1) | copy-start | bytes 3145732
  21.6 37.4 %all-to-all-start.1 = ((bf16[32,128,256]{2,1,0:T(8,128)(2,1)}), bf16[32,128,256]{2,1,0:T(8,128)(2,1)}, u32[]{:S(2)}, u32[]{:S(2)}) async-start(bf16[32,128,256]{2,1,0:T(8,128)(2,1)} %shard_map.105), calls=%async_computation.1 | async-start | bytes 4194304 | tf_op jit(solution)/shard_map/all_to_all | solution.py:319
  29.1 29.9 %collective-permute-start.7 = (bf16[128,4096]{1,0:T(8,128)(2,1)S(1)}, bf16[128,4096]{1,0:T(8,128)(2,1)}, u32[]{:S(2)}, u32[]{:S(2)}) collective-permute-start(bf16[128,4096]{1,0:T(8,128)(2,1)S(1)} %copy-done.3), channel_id=1, source_target_pairs={{0,8},{8,0},{1,9},{9,1},{2,10},{10,2},{3,11},{11,3},{4,12},{12,4},... | collective-permute-start | bytes 3145736 | tf_op jit(solution)/shard_map/ppermute | solution.py:311
  29.5 8.3 %collective-permute-start = (bf16[16,4096]{1,0:T(8,128)(2,1)S(1)}, bf16[16,4096]{1,0:T(8,128)(2,1)S(1)}, u32[]{:S(2)}, u32[]{:S(2)}) collective-permute-start(bf16[16,4096]{1,0:T(8,128)(2,1)S(1)} %constant_dynamic-slice_fusion.refs_0_), channel_id=1, source_target_pairs={{0,7},{1,0},{2,1},{3,2},{4,3},{5,4},{6,5},{7,6},{8,15},{9,8},{10,9... | collective-permute-start | bytes 393224 | tf_op jit(solution)/shard_map/ppermute | solution.py:307
  35.1 6.2 %collective-permute-start.4 = (bf16[16,4096]{1,0:T(8,128)(2,1)S(1)}, bf16[16,4096]{1,0:T(8,128)(2,1)S(1)}, u32[]{:S(2)}, u32[]{:S(2)}) collective-permute-start(bf16[16,4096]{1,0:T(8,128)(2,1)S(1)} %constant_dynamic-slice_fusion.refs_0_), channel_id=1, source_target_pairs={{0,1},{1,2},{2,3},{3,4},{4,5},{5,6},{6,7},{7,0},{8,9},{9,10},{10,1... | collective-permute-start | bytes 393224 | tf_op jit(solution)/shard_map/ppermute | solution.py:307
  37.8 5.5 %collective-permute-start.1 = (bf16[16,4096]{1,0:T(8,128)(2,1)S(1)}, bf16[16,4096]{1,0:T(8,128)(2,1)S(1)}, u32[]{:S(2)}, u32[]{:S(2)}) collective-permute-start(bf16[16,4096]{1,0:T(8,128)(2,1)S(1)} %collective-permute-done.refs_1_), channel_id=1, source_target_pairs={{0,7},{1,0},{2,1},{3,2},{4,3},{5,4},{6,5},{7,6},{8,15},{9,8},{10,9... | collective-permute-start | bytes 393224 | tf_op jit(solution)/shard_map/ppermute | solution.py:307
  41.3 6.1 %collective-permute-start.5 = (bf16[16,4096]{1,0:T(8,128)(2,1)S(1)}, bf16[16,4096]{1,0:T(8,128)(2,1)}, u32[]{:S(2)}, u32[]{:S(2)}) collective-permute-start(bf16[16,4096]{1,0:T(8,128)(2,1)S(1)} %collective-permute-done.4.refs_7_), channel_id=1, source_target_pairs={{0,1},{1,2},{2,3},{3,4},{4,5},{5,6},{6,7},{7,0},{8,9},{9,10},{10,1... | collective-permute-start | bytes 393224 | tf_op jit(solution)/shard_map/ppermute | solution.py:307
  43.2 5.4 %collective-permute-start.2 = (bf16[16,4096]{1,0:T(8,128)(2,1)S(1)}, bf16[16,4096]{1,0:T(8,128)(2,1)}, u32[]{:S(2)}, u32[]{:S(2)}) collective-permute-start(bf16[16,4096]{1,0:T(8,128)(2,1)S(1)} %collective-permute-done.1.refs_2_), channel_id=1, source_target_pairs={{0,7},{1,0},{2,1},{3,2},{4,3},{5,4},{6,5},{7,6},{8,15},{9,8},{10,9... | collective-permute-start | bytes 393224 | tf_op jit(solution)/shard_map/ppermute | solution.py:307
  47.4 7.8 %collective-permute-start.6 = (bf16[16,4096]{1,0:T(8,128)(2,1)}, bf16[16,4096]{1,0:T(8,128)(2,1)}, u32[]{:S(2)}, u32[]{:S(2)}) collective-permute-start(bf16[16,4096]{1,0:T(8,128)(2,1)} %collective-permute-done.5.refs_6_), channel_id=1, source_target_pairs={{0,1},{1,2},{2,3},{3,4},{4,5},{5,6},{6,7},{7,0},{8,9},{9,10},{10,1... | collective-permute-start | bytes 393224 | tf_op jit(solution)/shard_map/ppermute | solution.py:307
  48.7 6.5 %collective-permute-start.3 = (bf16[16,4096]{1,0:T(8,128)(2,1)}, bf16[16,4096]{1,0:T(8,128)(2,1)}, u32[]{:S(2)}, u32[]{:S(2)}) collective-permute-start(bf16[16,4096]{1,0:T(8,128)(2,1)} %collective-permute-done.2.refs_3_), channel_id=1, source_target_pairs={{0,7},{1,0},{2,1},{3,2},{4,3},{5,4},{6,5},{7,6},{8,15},{9,8},{10,9... | collective-permute-start | bytes 393224 | tf_op jit(solution)/shard_map/ppermute | solution.py:307
  55.2 10.5 %copy-start.13 = (s32[2,4]{1,0:T(2,128)S(1)}, s32[2,4]{1,0:T(2,128)}, u32[]{:S(2)}) copy-start(s32[2,4]{1,0:T(2,128)} %index.3) | copy-start | bytes 100
  59.0 49.0 %copy-start.12 = (bf16[128,256]{1,0:T(8,128)(2,1)S(1)}, bf16[128,256]{1,0:T(8,128)(2,1)}, u32[]{:S(2)}) copy-start(bf16[128,256]{1,0:T(8,128)(2,1)} %query.3) | copy-start | bytes 196612
  59.0 49.0 %copy-start.14 = (s32[2]{0:T(128)S(1)}, s32[2]{0:T(128)}, u32[]{:S(2)}) copy-start(s32[2]{0:T(128)} %counts.1) | copy-start | bytes 28
  59.0 31.4 %all-to-all-start.2 = ((bf16[16,128,256]{2,1,0:T(8,128)(2,1)}), bf16[16,128,256]{2,1,0:T(8,128)(2,1)S(1)}, u32[]{:S(2)}, u32[]{:S(2)}) async-start(bf16[16,128,256]{2,1,0:T(8,128)(2,1)} %shard_map.106), calls=%async_computation.2 | async-start | bytes 2097152 | tf_op jit(solution)/shard_map/all_to_all | solution.py:315
  68.9 5.1 %collective-permute-start.8 = (bf16[160,512]{1,0:T(8,128)(2,1)S(1)}, bf16[160,512]{1,0:T(8,128)(2,1)S(1)}, u32[]{:S(2)}, u32[]{:S(2)}) collective-permute-start(bf16[160,512]{1,0:T(8,128)(2,1)S(1)} %get-tuple-element.31.refs_0_), channel_id=1, source_target_pairs={{0,7},{1,0},{2,1},{3,2},{4,3},{5,4},{6,5},{7,6},{8,15},{9,8},{10,9... | collective-permute-start | bytes 491528 | tf_op jit(solution)/shard_map/ppermute | solution.py:307
  71.3 5.7 %collective-permute-start.11 = (bf16[160,512]{1,0:T(8,128)(2,1)S(1)}, bf16[160,512]{1,0:T(8,128)(2,1)S(1)}, u32[]{:S(2)}, u32[]{:S(2)}) collective-permute-start(bf16[160,512]{1,0:T(8,128)(2,1)S(1)} %get-tuple-element.32.refs_1_), channel_id=1, source_target_pairs={{0,1},{1,2},{2,3},{3,4},{4,5},{5,6},{6,7},{7,0},{8,9},{9,10},{10,1... | collective-permute-start | bytes 491528 | tf_op jit(solution)/shard_map/ppermute | solution.py:307
  71.3 5.7 %collective-permute-start.9 = (bf16[160,512]{1,0:T(8,128)(2,1)S(1)}, bf16[160,512]{1,0:T(8,128)(2,1)S(1)}, u32[]{:S(2)}, u32[]{:S(2)}) collective-permute-start(bf16[160,512]{1,0:T(8,128)(2,1)S(1)} %get-tuple-element.32.refs_1_), channel_id=1, source_target_pairs={{0,7},{1,0},{2,1},{3,2},{4,3},{5,4},{6,5},{7,6},{8,15},{9,8},{10,9... | collective-permute-start | bytes 491528 | tf_op jit(solution)/shard_map/ppermute | solution.py:307
  74.0 5.7 %collective-permute-start.10 = (bf16[160,512]{1,0:T(8,128)(2,1)S(1)}, bf16[160,512]{1,0:T(8,128)(2,1)S(1)}, u32[]{:S(2)}, u32[]{:S(2)}) collective-permute-start(bf16[160,512]{1,0:T(8,128)(2,1)S(1)} %get-tuple-element.31.refs_0_), channel_id=1, source_target_pairs={{0,1},{1,2},{2,3},{3,4},{4,5},{5,6},{6,7},{7,0},{8,9},{9,10},{10,1... | collective-permute-start | bytes 491528 | tf_op jit(solution)/shard_map/ppermute | solution.py:307
  74.0 6.1 %collective-permute-start.12 = (bf16[160,512]{1,0:T(8,128)(2,1)S(1)}, bf16[160,512]{1,0:T(8,128)(2,1)S(1)}, u32[]{:S(2)}, u32[]{:S(2)}) collective-permute-start(bf16[160,512]{1,0:T(8,128)(2,1)S(1)} %collective-permute-done.8.refs_2_), channel_id=1, source_target_pairs={{0,7},{1,0},{2,1},{3,2},{4,3},{5,4},{6,5},{7,6},{8,15},{9,8},{10,9... | collective-permute-start | bytes 491528 | tf_op jit(solution)/shard_map/ppermute | solution.py:307
  77.0 6.6 %collective-permute-start.15 = (bf16[160,512]{1,0:T(8,128)(2,1)S(1)}, bf16[160,512]{1,0:T(8,128)(2,1)S(1)}, u32[]{:S(2)}, u32[]{:S(2)}) collective-permute-start(bf16[160,512]{1,0:T(8,128)(2,1)S(1)} %collective-permute-done.11.refs_5_), channel_id=1, source_target_pairs={{0,1},{1,2},{2,3},{3,4},{4,5},{5,6},{6,7},{7,0},{8,9},{9,10},{10,1... | collective-permute-start | bytes 491528 | tf_op jit(solution)/shard_map/ppermute | solution.py:307
  77.0 6.6 %collective-permute-start.13 = (bf16[160,512]{1,0:T(8,128)(2,1)S(1)}, bf16[160,512]{1,0:T(8,128)(2,1)S(1)}, u32[]{:S(2)}, u32[]{:S(2)}) collective-permute-start(bf16[160,512]{1,0:T(8,128)(2,1)S(1)} %collective-permute-done.9.refs_3_), channel_id=1, source_target_pairs={{0,7},{1,0},{2,1},{3,2},{4,3},{5,4},{6,5},{7,6},{8,15},{9,8},{10,9... | collective-permute-start | bytes 491528 | tf_op jit(solution)/shard_map/ppermute | solution.py:307
  79.7 6.9 %collective-permute-start.14 = (bf16[160,512]{1,0:T(8,128)(2,1)S(1)}, bf16[160,512]{1,0:T(8,128)(2,1)S(1)}, u32[]{:S(2)}, u32[]{:S(2)}) collective-permute-start(bf16[160,512]{1,0:T(8,128)(2,1)S(1)} %collective-permute-done.10.refs_4_), channel_id=1, source_target_pairs={{0,1},{1,2},{2,3},{3,4},{4,5},{5,6},{6,7},{7,0},{8,9},{9,10},{10,1... | collective-permute-start | bytes 491528 | tf_op jit(solution)/shard_map/ppermute | solution.py:307
  80.1 7.8 %collective-permute-start.16 = (bf16[160,512]{1,0:T(8,128)(2,1)S(1)}, bf16[160,512]{1,0:T(8,128)(2,1)}, u32[]{:S(2)}, u32[]{:S(2)}) collective-permute-start(bf16[160,512]{1,0:T(8,128)(2,1)S(1)} %collective-permute-done.12.refs_6_), channel_id=1, source_target_pairs={{0,7},{1,0},{2,1},{3,2},{4,3},{5,4},{6,5},{7,6},{8,15},{9,8},{10,9... | collective-permute-start | bytes 491528 | tf_op jit(solution)/shard_map/ppermute | solution.py:307
  83.6 6.8 %collective-permute-start.17 = (bf16[160,512]{1,0:T(8,128)(2,1)S(1)}, bf16[160,512]{1,0:T(8,128)(2,1)}, u32[]{:S(2)}, u32[]{:S(2)}) collective-permute-start(bf16[160,512]{1,0:T(8,128)(2,1)S(1)} %collective-permute-done.15.refs_9_), channel_id=1, source_target_pairs={{0,1},{1,2},{2,3},{3,4},{4,5},{5,6},{6,7},{7,0},{8,9},{9,10},{10,1... | collective-permute-start | bytes 491528 | tf_op jit(solution)/shard_map/ppermute | solution.py:307
  90.4 17.6 %collective-permute-start.22 = (bf16[16,128,256]{2,1,0:T(8,128)(2,1)S(1)}, bf16[16,128,256]{2,1,0:T(8,128)(2,1)S(1)}, u32[]{:S(2)}, u32[]{:S(2)}) collective-permute-start(bf16[16,128,256]{2,1,0:T(8,128)(2,1)S(1)} %all-to-all-done.2.mine), channel_id=1, source_target_pairs={{0,8},{8,0},{1,9},{9,1},{2,10},{10,2},{3,11},{11,3},{4,12},{12,4},... | collective-permute-start | bytes 3145736 | tf_op jit(solution)/shard_map/ppermute | solution.py:311
  97.3 6.0 %collective-permute-start.18 = (bf16[160,512]{1,0:T(8,128)(2,1)}, bf16[160,512]{1,0:T(8,128)(2,1)S(1)}, u32[]{:S(2)}, u32[]{:S(2)}) collective-permute-start(bf16[160,512]{1,0:T(8,128)(2,1)} %copy-done.5), channel_id=1, source_target_pairs={{0,7},{1,0},{2,1},{3,2},{4,3},{5,4},{6,5},{7,6},{8,15},{9,8},{10,9... | collective-permute-start | bytes 491528 | tf_op jit(solution)/shard_map/ppermute | solution.py:307
  97.3 7.2 %collective-permute-start.19 = (bf16[160,512]{1,0:T(8,128)(2,1)}, bf16[160,512]{1,0:T(8,128)(2,1)S(1)}, u32[]{:S(2)}, u32[]{:S(2)}) collective-permute-start(bf16[160,512]{1,0:T(8,128)(2,1)} %copy-done.6), channel_id=1, source_target_pairs={{0,1},{1,2},{2,3},{3,4},{4,5},{5,6},{6,7},{7,0},{8,9},{9,10},{10,1... | collective-permute-start | bytes 491528 | tf_op jit(solution)/shard_map/ppermute | solution.py:307
  98.8 8.1 %collective-permute-start.20 = (bf16[160,512]{1,0:T(8,128)(2,1)}, bf16[160,512]{1,0:T(8,128)(2,1)S(1)}, u32[]{:S(2)}, u32[]{:S(2)}) collective-permute-start(bf16[160,512]{1,0:T(8,128)(2,1)} %collective-permute-done.16.refs_0_), channel_id=1, source_target_pairs={{0,7},{1,0},{2,1},{3,2},{4,3},{5,4},{6,5},{7,6},{8,15},{9,8},{10,9... | collective-permute-start | bytes 491528 | tf_op jit(solution)/shard_map/ppermute | solution.py:307
  100.0 8.0 %collective-permute-start.21 = (bf16[160,512]{1,0:T(8,128)(2,1)}, bf16[160,512]{1,0:T(8,128)(2,1)S(1)}, u32[]{:S(2)}, u32[]{:S(2)}) collective-permute-start(bf16[160,512]{1,0:T(8,128)(2,1)} %collective-permute-done.17.refs_3_), channel_id=1, source_target_pairs={{0,1},{1,2},{2,3},{3,4},{4,5},{5,6},{6,7},{7,0},{8,9},{9,10},{10,1... | collective-permute-start | bytes 491528 | tf_op jit(solution)/shard_map/ppermute | solution.py:307
  114.8 1.8 %collective-permute-start.23 = (bf16[128,128]{1,0:T(8,128)(2,1)S(1)}, bf16[128,128]{1,0:T(8,128)(2,1)S(1)}, u32[]{:S(2)}, u32[]{:S(2)}) collective-permute-start(bf16[128,128]{1,0:T(8,128)(2,1)S(1)} %get-tuple-element.42), channel_id=1, source_target_pairs={{0,8},{8,0},{1,9},{9,1},{2,10},{10,2},{3,11},{11,3},{4,12},{12,4},... | collective-permute-start | bytes 98312 | tf_op jit(solution)/shard_map/ppermute | solution.py:311
  (12 other events, 29.0 us)

commit v3 on v2

v3 whole, which is shorter than its diff:
```python
import functools
import math

import jax
import jax.numpy as jnp
from jax import lax
from jax.experimental import pallas as pl
from jax.experimental.pallas import tpu as pltpu
from jax.sharding import Mesh, PartitionSpec as P

DH = 128
BF = jnp.bfloat16
F32 = jnp.float32
VMEM = pl.BlockSpec(memory_space=pltpu.VMEM)
SMEM = pl.BlockSpec(memory_space=pltpu.SMEM)
HBM = pl.BlockSpec(memory_space=pltpu.HBM)
SEQ = ("chip", "core")
ANY = pl.BlockSpec(memory_space=pl.ANY)
NT = (((1,), (1,)), ((), ()))


def params(mebibytes=16):
    return pltpu.CompilerParams(vmem_limit_bytes=mebibytes * 1024 * 1024)


def tags_kernel(rows, index, out):
    spans, slots = index.shape
    for dest in range(out.shape[0]):
        out[dest, 0, 0] = 0
    for j in range(spans * slots):
        entry = index[j // slots, j % slots]
        out[entry // rows, 0, 0] = entry % rows + 1


def make_tags(rows, index, devices):
    return pl.pallas_call(
        functools.partial(tags_kernel, rows),
        out_shape=jax.ShapeDtypeStruct((devices, 1, 1), jnp.int32),
        in_specs=[SMEM],
        out_specs=SMEM,
    )(index)


def product_kernel(place, matrix, *refs):
    pieces, (out, left, result, sems) = refs[:-4], refs[-4:]
    part = left.shape[0] // len(pieces)
    copies = [
        pltpu.make_async_copy(p, left.at[pl.ds(i * part, part)], sems.at[i])
        for i, p in enumerate(pieces)
    ]
    for copy in copies:
        copy.start()
    for copy in copies:
        copy.wait()
    first = pl.multiple_of(place[1] * 2 * DH, 2 * DH)
    right = matrix[:, pl.ds(first, 2 * DH)]
    result[...] = jnp.dot(left[...], right, preferred_element_type=F32).astype(BF)
    copies = [
        pltpu.make_async_copy(result, out.at[p], sems.at[p]) for p in range(out.shape[0])
    ]
    for copy in copies:
        copy.start()
    for copy in copies:
        copy.wait()


def multiply(place, matrix, pieces, copies):
    rows = len(pieces) * pieces[0].shape[0]
    pieces = [pltpu.with_memory_space_constraint(p, pltpu.HBM) for p in pieces]
    return pl.pallas_call(
        product_kernel,
        out_shape=pltpu.HBM((copies, rows, 2 * DH), BF),
        in_specs=[SMEM, VMEM] + [HBM] * len(pieces),
        out_specs=HBM,
        scratch_shapes=[
            pltpu.VMEM((rows, pieces[0].shape[1]), BF),
            pltpu.VMEM((rows, 2 * DH), BF),
            pltpu.SemaphoreType.DMA((max(copies, len(pieces)),)),
        ],
        compiler_params=params(),
    )(place, matrix, *pieces)


def outbox_kernel(tags, query, out, sems):
    count = out.shape[0]

    def copy(dest):
        return pltpu.make_async_copy(query.at[tags[dest, 0, 0] - 1], out.at[dest], sems.at[dest])

    for dest in range(count):

        @pl.when(tags[dest, 0, 0] > 0)
        def _():
            copy(dest).start()

    for dest in range(count):

        @pl.when(tags[dest, 0, 0] > 0)
        def _():
            copy(dest).wait()


def outbox(tags, query, buckets):
    return pl.pallas_call(
        outbox_kernel,
        out_shape=jax.ShapeDtypeStruct((buckets,) + query.shape[1:], BF),
        in_specs=[SMEM, VMEM],
        out_specs=HBM,
        scratch_shapes=[pltpu.SemaphoreType.DMA((buckets,))],
        compiler_params=params(60),
    )(tags, query)


def encode_kernel(rows, index, inbox, pairs, out0, out1, held, sems):
    spans, slots = index.shape
    span_len = pairs.shape[0] // spans
    copies = []
    for j in range(spans * slots):
        home = index[j // slots, j % slots] // rows
        copies.append(pltpu.make_async_copy(inbox.at[home], held.at[j], sems.at[j]))
        copies[-1].start()
    for c in range(spans):
        for j in range(c * slots, (c + 1) * slots):
            copies[j].wait()
        for head, out in enumerate((out0, out1)):
            at = slice(head * DH, (head + 1) * DH)
            keys = pairs[c * span_len : (c + 1) * span_len, at]
            queries = held[c * slots : (c + 1) * slots, :, at].reshape(-1, DH)
            scores = lax.dot_general(
                keys, queries, NT, preferred_element_type=F32
            ) / math.sqrt(DH)
            exponent = jnp.exp(scores - jnp.max(scores, axis=0, keepdims=True))
            weights = exponent / jnp.sum(exponent, axis=0, keepdims=True)
            out[c * span_len : (c + 1) * span_len] = weights.astype(BF)
    tokens = pairs.shape[0]
    rows = tokens // slots
    for head, out in enumerate((out0, out1)):
        values = pairs[:, (2 + head) * DH : (3 + head) * DH]
        out[tokens:] = jnp.concatenate(
            [values[k * rows : (k + 1) * rows] for k in range(slots)], axis=1
        )


def encode(index, inbox, pairs):
    spans, slots = index.shape
    tokens = pairs.shape[0]
    shape = jax.ShapeDtypeStruct((tokens + tokens // slots, slots * inbox.shape[1]), BF)
    return pl.pallas_call(
        functools.partial(encode_kernel, spans * slots),
        out_shape=(shape, shape),
        in_specs=[SMEM, HBM, VMEM],
        out_specs=(VMEM, VMEM),
        scratch_shapes=[
            pltpu.VMEM((spans * slots,) + inbox.shape[1:], BF),
            pltpu.SemaphoreType.DMA((spans * slots,)),
        ],
        compiler_params=params(),
    )(index, inbox, pairs)


def decode_kernel(part, order, place, counts, query, product, *refs):
    out, send, folded, held, pieces, sems = refs[-6:]
    groups = len(order)
    spans = folded.shape[0]
    tokens = query.shape[0]
    span_len = tokens // spans
    slots = pieces.shape[2] // DH
    slot_tokens = slots * DH
    copies = [
        pltpu.make_async_copy(product.at[:, k], held.at[k], sems.at[k]) for k in range(2)
    ]
    arrive = [
        pltpu.make_async_copy(piece, pieces.at[i], sems.at[2 + i])
        for i, piece in enumerate(refs[:-6])
    ]
    for copy in copies[:1] + arrive + copies[1:]:
        copy.start()

    def riding(i):
        rows = pieces[i][tokens:]
        return jnp.concatenate([rows[:, k * DH : (k + 1) * DH] for k in range(slots)], axis=0)

    for k in range(2):
        copies[k].wait()
        for n, g in enumerate(order):
            if k == 0:
                arrive[2 * n].wait()
                arrive[2 * n + 1].wait()
            at = slice(g * part, (g + 1) * part)
            rows = jnp.concatenate([held[k, p, at] for p in range(held.shape[1])], axis=0)
            low = jnp.dot(riding(2 * n), rows[:DH], preferred_element_type=F32)
            high = jnp.dot(riding(2 * n + 1), rows[DH:], preferred_element_type=F32)
            for c in range(spans):
                span = slice(c * span_len, (c + 1) * span_len)
                both = jnp.concatenate([low[span], high[span]], axis=0).astype(BF)
                columns = slice(n * 2 * span_len, (n + 1) * 2 * span_len)
                folded[c, k * 2 * DH : (k + 1) * 2 * DH, columns] = both.T
    for c in range(spans):
        weights = pieces[:, c * span_len : (c + 1) * span_len].reshape(-1, slot_tokens)
        both = jnp.dot(folded[c], weights, preferred_element_type=F32).astype(BF)
        usable = lax.broadcasted_iota(jnp.int32, (span_len, slot_tokens), 1) < counts[c] * DH
        for h in range(2):
            at = slice(c * span_len, (c + 1) * span_len)
            keys = both[h * DH : (h + 1) * DH]
            head_values = both[(2 + h) * DH : (3 + h) * DH]
            scores = jnp.dot(
                query[at, h * DH : (h + 1) * DH], keys, preferred_element_type=F32
            ) / math.sqrt(DH)
            scores = jnp.where(usable, scores, -1e30)
            exponent = jnp.exp(scores - jnp.max(scores, axis=1, keepdims=True))
            share = (exponent / jnp.sum(exponent, axis=1, keepdims=True)).astype(BF)
            result = lax.dot_general(share, head_values, NT, preferred_element_type=F32)
            out[at, h * DH : (h + 1) * DH] = result.astype(BF)
    send[...] = out[...]


def decode(place, counts, query, product, pieces, order):
    tokens, width = query.shape
    spans = counts.shape[0]
    part = product.shape[2] // len(order)
    shape = jax.ShapeDtypeStruct((tokens, width), BF)
    return pl.pallas_call(
        functools.partial(decode_kernel, part, order),
        out_shape=(shape, shape),
        in_specs=[SMEM, SMEM, VMEM, ANY] + [HBM] * len(pieces),
        out_specs=(VMEM, VMEM),
        scratch_shapes=[
            pltpu.VMEM((spans, 4 * DH, 2 * len(order) * tokens // spans), BF),
            pltpu.VMEM((2, product.shape[0]) + product.shape[2:], BF),
            pltpu.VMEM((len(pieces),) + pieces[0].shape, BF),
            pltpu.SemaphoreType.DMA((2 + len(pieces),)),
        ],
        compiler_params=params(),
    )(place, counts, query, product, *pieces)


def partial_kernel(place, attended, near, grad, near_grad, out):
    left = jnp.concatenate([attended[...], near[...]], axis=0).T
    width = out.shape[2]

    def block(p):
        at = pl.ds(pl.multiple_of((2 * p + place[1]) * width, width), width)
        return jnp.concatenate([grad[:, at], near_grad[:, at]], axis=0)

    for p in range(0, out.shape[0], 2):
        right = jnp.concatenate([block(p), block(p + 1)], axis=1)
        term = jnp.dot(left, right, preferred_element_type=F32).astype(BF)
        out[p] = term[:, :width]
        out[p + 1] = term[:, width:]


def partial_grad(place, attended, near, grad, near_grad, chips):
    return pl.pallas_call(
        partial_kernel,
        out_shape=jax.ShapeDtypeStruct(
            (chips, attended.shape[1], grad.shape[1] // (2 * chips)), BF
        ),
        in_specs=[SMEM, VMEM, VMEM, VMEM, VMEM],
        out_specs=VMEM,
        compiler_params=params(),
    )(place, attended, near, grad, near_grad)


def total_kernel(parts, out):
    total = parts[0].astype(F32)
    for p in range(1, parts.shape[0]):
        total += parts[p].astype(F32)
    out[...] = total


def total_grad(parts):
    return pl.pallas_call(
        total_kernel,
        out_shape=jax.ShapeDtypeStruct(parts.shape[1:], F32),
        in_specs=[VMEM],
        out_specs=VMEM,
        compiler_params=params(),
    )(parts)


def shift(x, axis, step):
    n = lax.axis_size(axis)
    return lax.ppermute(x, axis, [(i, (i + step) % n) for i in range(n)])


def sibling(x):
    return lax.ppermute(x, "core", [(0, 1), (1, 0)])


def exchange_over(x, axis):
    return lax.all_to_all(x, axis, split_axis=0, concat_axis=0, tiled=True)


def exchange(x):
    return lax.all_to_all(x, SEQ, split_axis=0, concat_axis=0, tiled=True)


def local(
    span_states, dec_query, nbr_query, nbr_index, nbr_count, wkv_enc, wo_enc, wkv_dec, grad_out
):
    chips = lax.axis_size("chip")
    devices = 2 * chips
    groups = lax.axis_size("mp")
    chip, core, z = lax.axis_index("chip"), lax.axis_index("core"), lax.axis_index("mp")
    place = jnp.stack([z, core]).astype(jnp.int32)
    spans = nbr_count.shape[0]
    rows = nbr_query.shape[0]
    hidden = span_states.shape[1]

    def ring(x, forward):
        up = [x]
        down = [x]
        for _ in range(3):
            up.append(shift(up[-1], "mp", -1))
            down.append(shift(down[-1], "mp", 1))
        last = shift(up[-1], "mp", -1) if forward else shift(down[-1], "mp", 1)
        return up + [last] + down[:0:-1]

    tags = exchange(make_tags(rows, nbr_index, devices))

    pairs = jnp.dot(
        span_states, wkv_enc.reshape(hidden, -1), preferred_element_type=F32
    ).astype(BF)
    part = 2 * DH // chips
    wo_rows = lax.dynamic_slice_in_dim(wo_enc, chip * part, part, 0)
    tags, wo_rows, pairs = lax.optimization_barrier((tags, wo_rows, pairs))

    box = outbox(tags, nbr_query, devices)
    box, wkv_dec, wo_rows, pairs = lax.optimization_barrier((box, wkv_dec, wo_rows, pairs))
    inbox = exchange(box)

    wo_rows = ring(wo_rows, True)
    product = multiply(place, wkv_dec.reshape(hidden, -1), wo_rows, devices)
    grad_near = sibling(grad_out)
    inbox, product, grad_near = lax.optimization_barrier((inbox, product, grad_near))

    w0, w1 = encode(nbr_index, inbox, pairs)
    product = exchange(product).reshape((chips, 2) + product.shape[1:])

    up, down = [[w0, w1]], [[w0, w1]]
    for _ in range(3):
        up.append([shift(w, "mp", -1) for w in up[-1]])
        down.append([shift(w, "mp", 1) for w in down[-1]])
    last = [shift(up[3][0], "mp", -1), shift(down[3][1], "mp", 1)]
    pieces = [w0, w1] + [w for step in zip(up[1:], down[1:]) for side in step for w in side]
    order = (0, 1, groups - 1, 2, groups - 2, 3, groups - 3, 4)
    pieces = [pltpu.with_memory_space_constraint(w, pltpu.HBM) for w in pieces + last]
    attended, send = decode(place, nbr_count, dec_query, product, pieces, order)

    near = sibling(send)
    parts = partial_grad(place, send, near, grad_out, grad_near, chips)
    parts = exchange_over(parts, "chip")
    return attended, total_grad(parts)


def solution(mesh):
    devices = mesh.devices
    fine = Mesh(devices.reshape(-1, 2, devices.shape[1]), SEQ + ("mp",))
    return jax.shard_map(
        local,
        mesh=fine,
        in_specs=(
            P(SEQ, None),
            P(SEQ, "mp"),
            P(SEQ, None, "mp"),
            P(SEQ, None),
            P(SEQ),
            P(None, None, "mp"),
            P("mp", None),
            P(None, None, "mp"),
            P(SEQ, None),
        ),
        out_specs=(P(SEQ, "mp"), P("mp", SEQ)),
        check_vma=False,
    )
```

time: 146 us -> 139 us (0.952)
  waiting for transfers between devices: 20 us -> 13.8 us
  starting transfers between devices: 64.2 us -> 68.2 us
  local copies, waits for them, and re-layouts: 13.2 us -> 9.97 us
  blocking collectives: 25.2 us -> 23.4 us
    all_to_all x2 -> x3, starting transfers between devices: 16 us -> 25.9 us  [exchange(): return lax.all_to_all(x, SEQ, split_axis=0, concat_axis=0, tiled=True)]
    all_to_all x1 -> x0, starting transfers between devices: 6.73 us -> none  [exchange_over(): return lax.all_to_all(x, axis, split_axis=0, concat_axis=0, tiled=True)]
    ppermute x21, waiting for transfers between devices: 19.1 us -> 12.8 us  [shift(): return lax.ppermute(x, axis, [(i, (i + step) % n) for i in range(n)])]
    ppermute x21, starting transfers between devices: 33.2 us -> 38.3 us  [shift(): return lax.ppermute(x, axis, [(i, (i + step) % n) for i in range(n)])]
    ppermute x3 -> x2, starting transfers between devices: 8.23 us -> 4.02 us  [sibling(): return lax.ppermute(x, 'core', [(0, 1), (1, 0)])]
    unnamed x36 -> x58, local copies, waits for them, and re-layouts: 13.2 us -> 9.96 us
    all_to_all x1, blocking collectives: 25.2 us -> 23.4 us  [exchange_over(): return lax.all_to_all(x, axis, split_axis=0, concat_axis=0, tiled=True)]
    pallas_call x1, Pallas kernels: 5.46 us -> 6.96 us  [decode(): pl.pallas_call(functools.partial(decode_kernel, part, order), out_shape=(...]
  transfers between devices with their start and end apart: 27 -> 26, of which waited for: 12 -> 10; matrix products, arithmetic and copies ran while one was open for 8% -> 8% of each run, Pallas kernels for 5% -> 4%
where the time goes in v3:
time: 139 us
  starting transfers between devices  68.2 us (49%)
  blocking collectives  23.4 us (17%)
  Pallas kernels  19.4 us (14%)
  waiting for transfers between devices  13.8 us (10%)
  local copies, waits for them, and re-layouts  9.97 us (7%)
  matrix products  2.96 us (2%)
    ppermute x21, starting transfers between devices, shift(): return lax.ppermute(x, axis, [(i, (i + step) % n) for i in range(n)])  38.3 us
    all_to_all x3, starting transfers between devices, exchange(): return lax.all_to_all(x, SEQ, split_axis=0, concat_axis=0, tiled=True)  25.9 us
    all_to_all x1, blocking collectives, exchange_over(): return lax.all_to_all(x, axis, split_axis=0, concat_axis=0, tiled=True)  23.4 us
    ppermute x21, waiting for transfers between devices, shift(): return lax.ppermute(x, axis, [(i, (i + step) % n) for i in range(n)])  12.8 us
    unnamed x58, local copies, waits for them, and re-layouts  9.96 us
    pallas_call x1, Pallas kernels, decode(): pl.pallas_call(functools.partial(decode_kernel, part, order), out_shape=(...  6.96 us
    ppermute x2, starting transfers between devices, sibling(): return lax.ppermute(x, 'core', [(0, 1), (1, 0)])  4.02 us
    pallas_call x1, Pallas kernels, multiply(): pl.pallas_call(product_kernel, out_shape=pltpu.HBM((copies, rows, 2 * DH)...  3.92 us
  transfers between devices with their start and end apart: 26, of which 10 were waited for; matrix products, arithmetic and copies ran while one was open for 8% of the time, Pallas kernels for 4%

profile of v3, /device:TPU:1, one launch (start us, length us, event | category | flops | bytes accessed | tf_op | source)
XLA Modules:
  0.0 138.9 jit_solution(6064188781788688211)
XLA Ops:
  0.6 1.7 %shard_map.104 = s32[32,1,1]{2,1,0:T(1,128)} custom-call(s32[2,4]{1,0:T(2,128)} %index.3), custom_call_target="tpu_custom_call" | custom-call | tf_op jit(solution)/shard_map/pallas_call | solution.py:36
  2.3 8.6 %all-to-all-start = ((s32[32,1,1]{2,1,0:T(1,128)}), s32[32,1,1]{2,1,0:T(1,128)S(1)}, u32[]{:S(2)}, u32[]{:S(2)}) async-start(s32[32,1,1]{2,1,0:T(1,128)} %shard_map.104), calls=%async_computation | async-start | bytes 32768 | tf_op jit(solution)/shard_map/all_to_all | solution.py:295
  10.9 5.0 %copy.11 = bf16[512,8,2,256]{3,1,2,0:T(8,128)(2,1)} copy(bf16[512,8,2,256]{3,2,1,0:T(2,128)(2,1)} %bitcast.11) | data formatting | bytes 8388608
  16.0 3.0 %convolution_convert_fusion.pairs = bf16[128,512]{1,0:T(8,128)(2,1)S(1)} fusion(bf16[128,4096]{1,0:T(8,128)(2,1)S(1)} %copy-done.7, bf16[4096,512]{1,0:T(8,128)(2,1)} %bitcast.10), kind=kOutput, calls=%fused_computation | convolution fusion | flops 536936448 | bytes 5373952 | tf_op jit(solution)/shard_map/dot_general | solution.py:321
  19.6 2.2 %shard_map.105 = bf16[32,128,256]{2,1,0:T(8,128)(2,1)} custom-call(s32[32,1,1]{2,1,0:T(1,128)} %copy-done.27, bf16[8,128,256]{2,1,0:T(8,128)(2,1)} %query.2), custom_call_target="tpu_custom_call" | custom-call | tf_op jit(solution)/shard_map/pallas_call | solution.py:104
  21.8 7.4 %all-to-all-start.1 = ((bf16[32,128,256]{2,1,0:T(8,128)(2,1)}), bf16[32,128,256]{2,1,0:T(8,128)(2,1)}, u32[]{:S(2)}, u32[]{:S(2)}) async-start(bf16[32,128,256]{2,1,0:T(8,128)(2,1)} %shard_map.105), calls=%async_computation.1 | async-start | bytes 4194304 | tf_op jit(solution)/shard_map/all_to_all | solution.py:295
  29.6 5.6 %collective-permute-start = (bf16[16,4096]{1,0:T(8,128)(2,1)S(1)}, bf16[16,4096]{1,0:T(8,128)(2,1)S(1)}, u32[]{:S(2)}, u32[]{:S(2)}) collective-permute-start(bf16[16,4096]{1,0:T(8,128)(2,1)S(1)} %constant_dynamic-slice_fusion.refs_0_), channel_id=1, source_target_pairs={{0,7},{1,0},{2,1},{3,2},{4,3},{5,4},{6,5},{7,6},{8,15},{9,8},{10,9... | collective-permute-start | bytes 393224 | tf_op jit(solution)/shard_map/ppermute | solution.py:283
  35.2 2.7 %collective-permute-done.refs_1_ = bf16[16,4096]{1,0:T(8,128)(2,1)S(1)} collective-permute-done((bf16[16,4096]{1,0:T(8,128)(2,1)S(1)}, bf16[16,4096]{1,0:T(8,128)(2,1)S(1)}, u32[]{:S(2)}, u32[]{:S(2)}) %collective-permute-start) | collective-permute-done | bytes 131104 | tf_op jit(solution)/shard_map/ppermute | solution.py:283
  37.9 3.5 %collective-permute-start.1 = (bf16[16,4096]{1,0:T(8,128)(2,1)S(1)}, bf16[16,4096]{1,0:T(8,128)(2,1)S(1)}, u32[]{:S(2)}, u32[]{:S(2)}) collective-permute-start(bf16[16,4096]{1,0:T(8,128)(2,1)S(1)} %collective-permute-done.refs_1_), channel_id=1, source_target_pairs={{0,7},{1,0},{2,1},{3,2},{4,3},{5,4},{6,5},{7,6},{8,15},{9,8},{10,9... | collective-permute-start | bytes 393224 | tf_op jit(solution)/shard_map/ppermute | solution.py:283
  41.5 1.9 %collective-permute-done.1.refs_2_ = bf16[16,4096]{1,0:T(8,128)(2,1)S(1)} collective-permute-done((bf16[16,4096]{1,0:T(8,128)(2,1)S(1)}, bf16[16,4096]{1,0:T(8,128)(2,1)S(1)}, u32[]{:S(2)}, u32[]{:S(2)}) %collective-permute-start.1) | collective-permute-done | bytes 131104 | tf_op jit(solution)/shard_map/ppermute | solution.py:283
  43.3 3.5 %collective-permute-start.2 = (bf16[16,4096]{1,0:T(8,128)(2,1)S(1)}, bf16[16,4096]{1,0:T(8,128)(2,1)S(1)}, u32[]{:S(2)}, u32[]{:S(2)}) collective-permute-start(bf16[16,4096]{1,0:T(8,128)(2,1)S(1)} %collective-permute-done.1.refs_2_), channel_id=1, source_target_pairs={{0,7},{1,0},{2,1},{3,2},{4,3},{5,4},{6,5},{7,6},{8,15},{9,8},{10,9... | collective-permute-start | bytes 393224 | tf_op jit(solution)/shard_map/ppermute | solution.py:283
  46.9 1.9 %collective-permute-done.2.refs_3_ = bf16[16,4096]{1,0:T(8,128)(2,1)S(1)} collective-permute-done((bf16[16,4096]{1,0:T(8,128)(2,1)S(1)}, bf16[16,4096]{1,0:T(8,128)(2,1)S(1)}, u32[]{:S(2)}, u32[]{:S(2)}) %collective-permute-start.2) | collective-permute-done | bytes 131104 | tf_op jit(solution)/shard_map/ppermute | solution.py:283
  48.8 3.5 %collective-permute-start.3 = (bf16[16,4096]{1,0:T(8,128)(2,1)S(1)}, bf16[16,4096]{1,0:T(8,128)(2,1)}, u32[]{:S(2)}, u32[]{:S(2)}) collective-permute-start(bf16[16,4096]{1,0:T(8,128)(2,1)S(1)} %collective-permute-done.2.refs_3_), channel_id=1, source_target_pairs={{0,7},{1,0},{2,1},{3,2},{4,3},{5,4},{6,5},{7,6},{8,15},{9,8},{10,9... | collective-permute-start | bytes 393224 | tf_op jit(solution)/shard_map/ppermute | solution.py:283
  52.3 2.9 %copy.12 = bf16[512,8,2,256]{3,1,2,0:T(8,128)(2,1)S(1)} copy(bf16[512,8,2,256]{3,2,1,0:T(2,128)(2,1)} %bitcast.12) | data formatting | bytes 8388608
  55.3 3.9 %shard_map.106 = bf16[32,128,256]{2,1,0:T(8,128)(2,1)} custom-call(s32[2]{0:T(128)S(1)} %pad_add_fusion.place, bf16[4096,512]{1,0:T(8,128)(2,1)S(1)} %bitcast.9, bf16[16,4096]{1,0:T(8,128)(2,1)} %copy-done.8, bf16[16,4096]{1,0:T(8,128)(2,1)} %copy-done.22, bf16[16,4096]{1,0:T(8,128)(2,1)} %copy-done.24, bf16[16,4096]{1,0:T(8,128)(2,1)} %copy-done.26, ...), custom_call_target="tpu_custom_call" | custom-call | tf_op jit(solution)/shard_map/pallas_call | solution.py:70
  59.3 9.9 %all-to-all-start.2 = ((bf16[32,128,256]{2,1,0:T(8,128)(2,1)}), bf16[32,128,256]{2,1,0:T(8,128)(2,1)}, u32[]{:S(2)}, u32[]{:S(2)}) async-start(bf16[32,128,256]{2,1,0:T(8,128)(2,1)} %shard_map.106), calls=%async_computation.2 | async-start | bytes 4194304 | tf_op jit(solution)/shard_map/all_to_all | solution.py:295
  69.2 2.1 %shard_map.107 = (bf16[160,512]{1,0:T(8,128)(2,1)S(1)}, bf16[160,512]{1,0:T(8,128)(2,1)S(1)}) custom-call(s32[2,4]{1,0:T(2,128)S(1)} %copy-done.5, bf16[32,128,256]{2,1,0:T(8,128)(2,1)} %all-to-all-done.1.inbox, bf16[128,512]{1,0:T(8,128)(2,1)S(1)} %convolution_convert_fusion.pairs), custom_call_target="tpu_custom_call" | custom-call | tf_op jit(solution)/shard_map/pallas_call | solution.py:148
  71.3 3.0 %collective-permute-start.8 = (bf16[160,512]{1,0:T(8,128)(2,1)S(1)}, bf16[160,512]{1,0:T(8,128)(2,1)S(1)}, u32[]{:S(2)}, u32[]{:S(2)}) collective-permute-start(bf16[160,512]{1,0:T(8,128)(2,1)S(1)} %get-tuple-element.25.refs_0_), channel_id=1, source_target_pairs={{0,7},{1,0},{2,1},{3,2},{4,3},{5,4},{6,5},{7,6},{8,15},{9,8},{10,9... | collective-permute-start | bytes 491528 | tf_op jit(solution)/shard_map/ppermute | solution.py:283
  74.4 2.7 %collective-permute-start.9 = (bf16[160,512]{1,0:T(8,128)(2,1)S(1)}, bf16[160,512]{1,0:T(8,128)(2,1)S(1)}, u32[]{:S(2)}, u32[]{:S(2)}) collective-permute-start(bf16[160,512]{1,0:T(8,128)(2,1)S(1)} %get-tuple-element.26.refs_1_), channel_id=1, source_target_pairs={{0,7},{1,0},{2,1},{3,2},{4,3},{5,4},{6,5},{7,6},{8,15},{9,8},{10,9... | collective-permute-start | bytes 491528 | tf_op jit(solution)/shard_map/ppermute | solution.py:283
  77.6 3.5 %collective-permute-start.12 = (bf16[160,512]{1,0:T(8,128)(2,1)S(1)}, bf16[160,512]{1,0:T(8,128)(2,1)S(1)}, u32[]{:S(2)}, u32[]{:S(2)}) collective-permute-start(bf16[160,512]{1,0:T(8,128)(2,1)S(1)} %collective-permute-done.8.refs_2_), channel_id=1, source_target_pairs={{0,7},{1,0},{2,1},{3,2},{4,3},{5,4},{6,5},{7,6},{8,15},{9,8},{10,9... | collective-permute-start | bytes 491528 | tf_op jit(solution)/shard_map/ppermute | solution.py:283
  81.2 3.5 %collective-permute-start.13 = (bf16[160,512]{1,0:T(8,128)(2,1)S(1)}, bf16[160,512]{1,0:T(8,128)(2,1)S(1)}, u32[]{:S(2)}, u32[]{:S(2)}) collective-permute-start(bf16[160,512]{1,0:T(8,128)(2,1)S(1)} %collective-permute-done.9.refs_3_), channel_id=1, source_target_pairs={{0,7},{1,0},{2,1},{3,2},{4,3},{5,4},{6,5},{7,6},{8,15},{9,8},{10,9... | collective-permute-start | bytes 491528 | tf_op jit(solution)/shard_map/ppermute | solution.py:283
  84.8 2.7 %collective-permute-start.16 = (bf16[160,512]{1,0:T(8,128)(2,1)S(1)}, bf16[160,512]{1,0:T(8,128)(2,1)S(1)}, u32[]{:S(2)}, u32[]{:S(2)}) collective-permute-start(bf16[160,512]{1,0:T(8,128)(2,1)S(1)} %collective-permute-done.12.refs_6_), channel_id=1, source_target_pairs={{0,7},{1,0},{2,1},{3,2},{4,3},{5,4},{6,5},{7,6},{8,15},{9,8},{10,9... | collective-permute-start | bytes 491528 | tf_op jit(solution)/shard_map/ppermute | solution.py:283
  87.6 3.5 %collective-permute-start.17 = (bf16[160,512]{1,0:T(8,128)(2,1)S(1)}, bf16[160,512]{1,0:T(8,128)(2,1)S(1)}, u32[]{:S(2)}, u32[]{:S(2)}) collective-permute-start(bf16[160,512]{1,0:T(8,128)(2,1)S(1)} %collective-permute-done.13.refs_7_), channel_id=1, source_target_pairs={{0,7},{1,0},{2,1},{3,2},{4,3},{5,4},{6,5},{7,6},{8,15},{9,8},{10,9... | collective-permute-start | bytes 491528 | tf_op jit(solution)/shard_map/ppermute | solution.py:283
  91.4 3.1 %collective-permute-start.20 = (bf16[160,512]{1,0:T(8,128)(2,1)S(1)}, bf16[160,512]{1,0:T(8,128)(2,1)S(1)}, u32[]{:S(2)}, u32[]{:S(2)}) collective-permute-start(bf16[160,512]{1,0:T(8,128)(2,1)S(1)} %collective-permute-done.16.refs_10_), channel_id=1, source_target_pairs={{0,7},{1,0},{2,1},{3,2},{4,3},{5,4},{6,5},{7,6},{8,15},{9,8},{10,9... | collective-permute-start | bytes 491528 | tf_op jit(solution)/shard_map/ppermute | solution.py:283
  94.6 3.8 %collective-permute-done.18.refs_12_ = bf16[160,512]{1,0:T(8,128)(2,1)S(1)} collective-permute-done((bf16[160,512]{1,0:T(8,128)(2,1)S(1)}, bf16[160,512]{1,0:T(8,128)(2,1)S(1)}, u32[]{:S(2)}, u32[]{:S(2)}) %collective-permute-start.18) | collective-permute-done | bytes 163872 | tf_op jit(solution)/shard_map/ppermute | solution.py:283
  99.8 1.6 %collective-permute-done.21.refs_15_ = bf16[160,512]{1,0:T(8,128)(2,1)} collective-permute-done((bf16[160,512]{1,0:T(8,128)(2,1)S(1)}, bf16[160,512]{1,0:T(8,128)(2,1)}, u32[]{:S(2)}, u32[]{:S(2)}) %collective-permute-start.21) | collective-permute-done | bytes 163872 | tf_op jit(solution)/shard_map/ppermute | solution.py:283
  101.4 7.0 %shard_map.108 = (bf16[128,256]{1,0:T(8,128)(2,1)}, bf16[128,256]{1,0:T(8,128)(2,1)S(1)}) custom-call(s32[2]{0:T(128)S(1)} %pad_add_fusion.place, s32[2]{0:T(128)S(1)} %copy-done.6, bf16[128,256]{1,0:T(8,128)(2,1)S(1)} %copy-done.4, bf16[16,2,128,256]{3,2,1,0:T(8,128)(2,1)} %bitcast.2.product, bf16[160,512]{1,0:T(8,128)(2,1)} %copy-done.2, ...), custom_call_target="tpu_custom_call" | custom-call | tf_op jit(solution)/shard_map/pallas_call | solution.py:222
  108.4 3.6 %collective-permute-start.22 = (bf16[128,256]{1,0:T(8,128)(2,1)S(1)}, bf16[128,256]{1,0:T(8,128)(2,1)S(1)}, u32[]{:S(2)}, u32[]{:S(2)}) collective-permute-start(bf16[128,256]{1,0:T(8,128)(2,1)S(1)} %get-tuple-element.28.attended), channel_id=1, source_target_pairs={{0,8},{8,0},{1,9},{9,1},{2,10},{10,2},{3,11},{11,3},{4,12},{12,4},... | collective-permute-start | bytes 196616 | tf_op jit(solution)/shard_map/ppermute | solution.py:287
  112.0 0.9 collective-permute-done.22.near
  112.9 1.7 %shard_map.109 = bf16[16,256,128]{2,1,0:T(8,128)(2,1)S(1)} custom-call(s32[2]{0:T(128)S(1)} %pad_add_fusion.place, bf16[128,256]{1,0:T(8,128)(2,1)S(1)} %get-tuple-element.28.attended, bf16[128,256]{1,0:T(8,128)(2,1)S(1)} %collective-permute-done.22.near, bf16[128,4096]{1,0:T(8,128)(2,1)S(1)} %copy-done.1, bf16[128,4096]{1,0:T(8,128)(2,1)} %collective-permute-done.7.near_grad), custom_call_target="tpu_custom_call" | custom-call | tf_op jit(solution)/shard_map/pallas_call | solution.py:253
  114.7 23.4 %all_to_all.20.parts = bf16[16,256,128]{2,1,0:T(8,128)(2,1)S(1)} all-to-all(bf16[16,256,128]{2,1,0:T(8,128)(2,1)S(1)} %shard_map.109), channel_id=1, replica_groups=mesh['chip'=16,'core'=2,'mp'=8] {'chip'}, dimensions={0} | all-to-all | bytes 2097152 | tf_op jit(solution)/shard_map/all_to_all | solution.py:291
  138.1 0.8 shard_map.110
  (89 shorter events, 3.8 us)
Async XLA Ops:
  0.6 15.3 %copy-start = (bf16[256,4096]{1,0:T(8,128)(2,1)S(1)}, bf16[256,4096]{1,0:T(8,128)(2,1)}, u32[]{:S(2)}) copy-start(bf16[256,4096]{1,0:T(8,128)(2,1)} %param.15) | copy-start | bytes 6291460
  2.3 16.6 %all-to-all-start = ((s32[32,1,1]{2,1,0:T(1,128)}), s32[32,1,1]{2,1,0:T(1,128)S(1)}, u32[]{:S(2)}, u32[]{:S(2)}) async-start(s32[32,1,1]{2,1,0:T(1,128)} %shard_map.104), calls=%async_computation | async-start | bytes 32768 | tf_op jit(solution)/shard_map/all_to_all | solution.py:295
  16.0 19.2 %copy-start.8 = (bf16[16,4096]{1,0:T(8,128)(2,1)}, bf16[16,4096]{1,0:T(8,128)(2,1)S(1)}, u32[]{:S(2)}) copy-start(bf16[16,4096]{1,0:T(8,128)(2,1)S(1)} %constant_dynamic-slice_fusion.refs_0_) | copy-start | bytes 393220
  21.8 37.5 %all-to-all-start.1 = ((bf16[32,128,256]{2,1,0:T(8,128)(2,1)}), bf16[32,128,256]{2,1,0:T(8,128)(2,1)}, u32[]{:S(2)}, u32[]{:S(2)}) async-start(bf16[32,128,256]{2,1,0:T(8,128)(2,1)} %shard_map.105), calls=%async_computation.1 | async-start | bytes 4194304 | tf_op jit(solution)/shard_map/all_to_all | solution.py:295
  29.2 30.1 %collective-permute-start.7 = (bf16[128,4096]{1,0:T(8,128)(2,1)S(1)}, bf16[128,4096]{1,0:T(8,128)(2,1)}, u32[]{:S(2)}, u32[]{:S(2)}) collective-permute-start(bf16[128,4096]{1,0:T(8,128)(2,1)S(1)} %copy-done.1), channel_id=1, source_target_pairs={{0,8},{8,0},{1,9},{9,1},{2,10},{10,2},{3,11},{11,3},{4,12},{12,4},... | collective-permute-start | bytes 3145736 | tf_op jit(solution)/shard_map/ppermute | solution.py:287
  29.6 8.3 %collective-permute-start = (bf16[16,4096]{1,0:T(8,128)(2,1)S(1)}, bf16[16,4096]{1,0:T(8,128)(2,1)S(1)}, u32[]{:S(2)}, u32[]{:S(2)}) collective-permute-start(bf16[16,4096]{1,0:T(8,128)(2,1)S(1)} %constant_dynamic-slice_fusion.refs_0_), channel_id=1, source_target_pairs={{0,7},{1,0},{2,1},{3,2},{4,3},{5,4},{6,5},{7,6},{8,15},{9,8},{10,9... | collective-permute-start | bytes 393224 | tf_op jit(solution)/shard_map/ppermute | solution.py:283
  35.2 6.2 %collective-permute-start.4 = (bf16[16,4096]{1,0:T(8,128)(2,1)S(1)}, bf16[16,4096]{1,0:T(8,128)(2,1)S(1)}, u32[]{:S(2)}, u32[]{:S(2)}) collective-permute-start(bf16[16,4096]{1,0:T(8,128)(2,1)S(1)} %constant_dynamic-slice_fusion.refs_0_), channel_id=1, source_target_pairs={{0,1},{1,2},{2,3},{3,4},{4,5},{5,6},{6,7},{7,0},{8,9},{9,10},{10,1... | collective-permute-start | bytes 393224 | tf_op jit(solution)/shard_map/ppermute | solution.py:283
  37.9 5.5 %collective-permute-start.1 = (bf16[16,4096]{1,0:T(8,128)(2,1)S(1)}, bf16[16,4096]{1,0:T(8,128)(2,1)S(1)}, u32[]{:S(2)}, u32[]{:S(2)}) collective-permute-start(bf16[16,4096]{1,0:T(8,128)(2,1)S(1)} %collective-permute-done.refs_1_), channel_id=1, source_target_pairs={{0,7},{1,0},{2,1},{3,2},{4,3},{5,4},{6,5},{7,6},{8,15},{9,8},{10,9... | collective-permute-start | bytes 393224 | tf_op jit(solution)/shard_map/ppermute | solution.py:283
  41.4 5.5 %collective-permute-start.5 = (bf16[16,4096]{1,0:T(8,128)(2,1)S(1)}, bf16[16,4096]{1,0:T(8,128)(2,1)S(1)}, u32[]{:S(2)}, u32[]{:S(2)}) collective-permute-start(bf16[16,4096]{1,0:T(8,128)(2,1)S(1)} %collective-permute-done.4.refs_7_), channel_id=1, source_target_pairs={{0,1},{1,2},{2,3},{3,4},{4,5},{5,6},{6,7},{7,0},{8,9},{9,10},{10,1... | collective-permute-start | bytes 393224 | tf_op jit(solution)/shard_map/ppermute | solution.py:283
  43.3 5.4 %collective-permute-start.2 = (bf16[16,4096]{1,0:T(8,128)(2,1)S(1)}, bf16[16,4096]{1,0:T(8,128)(2,1)S(1)}, u32[]{:S(2)}, u32[]{:S(2)}) collective-permute-start(bf16[16,4096]{1,0:T(8,128)(2,1)S(1)} %collective-permute-done.1.refs_2_), channel_id=1, source_target_pairs={{0,7},{1,0},{2,1},{3,2},{4,3},{5,4},{6,5},{7,6},{8,15},{9,8},{10,9... | collective-permute-start | bytes 393224 | tf_op jit(solution)/shard_map/ppermute | solution.py:283
  46.9 8.4 %collective-permute-start.6 = (bf16[16,4096]{1,0:T(8,128)(2,1)S(1)}, bf16[16,4096]{1,0:T(8,128)(2,1)}, u32[]{:S(2)}, u32[]{:S(2)}) collective-permute-start(bf16[16,4096]{1,0:T(8,128)(2,1)S(1)} %collective-permute-done.5.refs_6_), channel_id=1, source_target_pairs={{0,1},{1,2},{2,3},{3,4},{4,5},{5,6},{6,7},{7,0},{8,9},{9,10},{10,1... | collective-permute-start | bytes 393224 | tf_op jit(solution)/shard_map/ppermute | solution.py:283
  48.8 6.5 %collective-permute-start.3 = (bf16[16,4096]{1,0:T(8,128)(2,1)S(1)}, bf16[16,4096]{1,0:T(8,128)(2,1)}, u32[]{:S(2)}, u32[]{:S(2)}) collective-permute-start(bf16[16,4096]{1,0:T(8,128)(2,1)S(1)} %collective-permute-done.2.refs_3_), channel_id=1, source_target_pairs={{0,7},{1,0},{2,1},{3,2},{4,3},{5,4},{6,5},{7,6},{8,15},{9,8},{10,9... | collective-permute-start | bytes 393224 | tf_op jit(solution)/shard_map/ppermute | solution.py:283
  55.3 13.9 %copy-start.5 = (s32[2,4]{1,0:T(2,128)S(1)}, s32[2,4]{1,0:T(2,128)}, u32[]{:S(2)}) copy-start(s32[2,4]{1,0:T(2,128)} %index.3) | copy-start | bytes 100
  59.2 42.2 %copy-start.4 = (bf16[128,256]{1,0:T(8,128)(2,1)S(1)}, bf16[128,256]{1,0:T(8,128)(2,1)}, u32[]{:S(2)}) copy-start(bf16[128,256]{1,0:T(8,128)(2,1)} %query.3) | copy-start | bytes 196612
  59.2 42.2 %copy-start.6 = (s32[2]{0:T(128)S(1)}, s32[2]{0:T(128)}, u32[]{:S(2)}) copy-start(s32[2]{0:T(128)} %counts.1) | copy-start | bytes 28
  59.3 42.1 %all-to-all-start.2 = ((bf16[32,128,256]{2,1,0:T(8,128)(2,1)}), bf16[32,128,256]{2,1,0:T(8,128)(2,1)}, u32[]{:S(2)}, u32[]{:S(2)}) async-start(bf16[32,128,256]{2,1,0:T(8,128)(2,1)} %shard_map.106), calls=%async_computation.2 | async-start | bytes 4194304 | tf_op jit(solution)/shard_map/all_to_all | solution.py:295
  71.3 30.1 %copy-start.2 = (bf16[160,512]{1,0:T(8,128)(2,1)}, bf16[160,512]{1,0:T(8,128)(2,1)S(1)}, u32[]{:S(2)}) copy-start(bf16[160,512]{1,0:T(8,128)(2,1)S(1)} %get-tuple-element.25.refs_0_) | copy-start | bytes 491524
  71.3 6.3 %collective-permute-start.8 = (bf16[160,512]{1,0:T(8,128)(2,1)S(1)}, bf16[160,512]{1,0:T(8,128)(2,1)S(1)}, u32[]{:S(2)}, u32[]{:S(2)}) collective-permute-start(bf16[160,512]{1,0:T(8,128)(2,1)S(1)} %get-tuple-element.25.refs_0_), channel_id=1, source_target_pairs={{0,7},{1,0},{2,1},{3,2},{4,3},{5,4},{6,5},{7,6},{8,15},{9,8},{10,9... | collective-permute-start | bytes 491528 | tf_op jit(solution)/shard_map/ppermute | solution.py:283
  74.4 6.8 %collective-permute-start.11 = (bf16[160,512]{1,0:T(8,128)(2,1)S(1)}, bf16[160,512]{1,0:T(8,128)(2,1)S(1)}, u32[]{:S(2)}, u32[]{:S(2)}) collective-permute-start(bf16[160,512]{1,0:T(8,128)(2,1)S(1)} %get-tuple-element.26.refs_1_), channel_id=1, source_target_pairs={{0,1},{1,2},{2,3},{3,4},{4,5},{5,6},{6,7},{7,0},{8,9},{9,10},{10,1... | collective-permute-start | bytes 491528 | tf_op jit(solution)/shard_map/ppermute | solution.py:283
  74.4 6.8 %collective-permute-start.9 = (bf16[160,512]{1,0:T(8,128)(2,1)S(1)}, bf16[160,512]{1,0:T(8,128)(2,1)S(1)}, u32[]{:S(2)}, u32[]{:S(2)}) collective-permute-start(bf16[160,512]{1,0:T(8,128)(2,1)S(1)} %get-tuple-element.26.refs_1_), channel_id=1, source_target_pairs={{0,7},{1,0},{2,1},{3,2},{4,3},{5,4},{6,5},{7,6},{8,15},{9,8},{10,9... | collective-permute-start | bytes 491528 | tf_op jit(solution)/shard_map/ppermute | solution.py:283
  77.0 7.6 %collective-permute-start.10 = (bf16[160,512]{1,0:T(8,128)(2,1)S(1)}, bf16[160,512]{1,0:T(8,128)(2,1)S(1)}, u32[]{:S(2)}, u32[]{:S(2)}) collective-permute-start(bf16[160,512]{1,0:T(8,128)(2,1)S(1)} %get-tuple-element.25.refs_0_), channel_id=1, source_target_pairs={{0,1},{1,2},{2,3},{3,4},{4,5},{5,6},{6,7},{7,0},{8,9},{9,10},{10,1... | collective-permute-start | bytes 491528 | tf_op jit(solution)/shard_map/ppermute | solution.py:283
  77.6 7.1 %collective-permute-start.12 = (bf16[160,512]{1,0:T(8,128)(2,1)S(1)}, bf16[160,512]{1,0:T(8,128)(2,1)S(1)}, u32[]{:S(2)}, u32[]{:S(2)}) collective-permute-start(bf16[160,512]{1,0:T(8,128)(2,1)S(1)} %collective-permute-done.8.refs_2_), channel_id=1, source_target_pairs={{0,7},{1,0},{2,1},{3,2},{4,3},{5,4},{6,5},{7,6},{8,15},{9,8},{10,9... | collective-permute-start | bytes 491528 | tf_op jit(solution)/shard_map/ppermute | solution.py:283
  81.2 6.4 %collective-permute-start.15 = (bf16[160,512]{1,0:T(8,128)(2,1)S(1)}, bf16[160,512]{1,0:T(8,128)(2,1)S(1)}, u32[]{:S(2)}, u32[]{:S(2)}) collective-permute-start(bf16[160,512]{1,0:T(8,128)(2,1)S(1)} %collective-permute-done.11.refs_5_), channel_id=1, source_target_pairs={{0,1},{1,2},{2,3},{3,4},{4,5},{5,6},{6,7},{7,0},{8,9},{9,10},{10,1... | collective-permute-start | bytes 491528 | tf_op jit(solution)/shard_map/ppermute | solution.py:283
  81.2 6.4 %collective-permute-start.13 = (bf16[160,512]{1,0:T(8,128)(2,1)S(1)}, bf16[160,512]{1,0:T(8,128)(2,1)S(1)}, u32[]{:S(2)}, u32[]{:S(2)}) collective-permute-start(bf16[160,512]{1,0:T(8,128)(2,1)S(1)} %collective-permute-done.9.refs_3_), channel_id=1, source_target_pairs={{0,7},{1,0},{2,1},{3,2},{4,3},{5,4},{6,5},{7,6},{8,15},{9,8},{10,9... | collective-permute-start | bytes 491528 | tf_op jit(solution)/shard_map/ppermute | solution.py:283
  84.7 6.6 %collective-permute-start.14 = (bf16[160,512]{1,0:T(8,128)(2,1)S(1)}, bf16[160,512]{1,0:T(8,128)(2,1)S(1)}, u32[]{:S(2)}, u32[]{:S(2)}) collective-permute-start(bf16[160,512]{1,0:T(8,128)(2,1)S(1)} %collective-permute-done.10.refs_4_), channel_id=1, source_target_pairs={{0,1},{1,2},{2,3},{3,4},{4,5},{5,6},{6,7},{7,0},{8,9},{9,10},{10,1... | collective-permute-start | bytes 491528 | tf_op jit(solution)/shard_map/ppermute | solution.py:283
  84.8 6.5 %collective-permute-start.16 = (bf16[160,512]{1,0:T(8,128)(2,1)S(1)}, bf16[160,512]{1,0:T(8,128)(2,1)S(1)}, u32[]{:S(2)}, u32[]{:S(2)}) collective-permute-start(bf16[160,512]{1,0:T(8,128)(2,1)S(1)} %collective-permute-done.12.refs_6_), channel_id=1, source_target_pairs={{0,7},{1,0},{2,1},{3,2},{4,3},{5,4},{6,5},{7,6},{8,15},{9,8},{10,9... | collective-permute-start | bytes 491528 | tf_op jit(solution)/shard_map/ppermute | solution.py:283
  87.5 7.0 %collective-permute-start.19 = (bf16[160,512]{1,0:T(8,128)(2,1)S(1)}, bf16[160,512]{1,0:T(8,128)(2,1)S(1)}, u32[]{:S(2)}, u32[]{:S(2)}) collective-permute-start(bf16[160,512]{1,0:T(8,128)(2,1)S(1)} %collective-permute-done.15.refs_9_), channel_id=1, source_target_pairs={{0,1},{1,2},{2,3},{3,4},{4,5},{5,6},{6,7},{7,0},{8,9},{9,10},{10,1... | collective-permute-start | bytes 491528 | tf_op jit(solution)/shard_map/ppermute | solution.py:283
  87.6 6.9 %collective-permute-start.17 = (bf16[160,512]{1,0:T(8,128)(2,1)S(1)}, bf16[160,512]{1,0:T(8,128)(2,1)S(1)}, u32[]{:S(2)}, u32[]{:S(2)}) collective-permute-start(bf16[160,512]{1,0:T(8,128)(2,1)S(1)} %collective-permute-done.13.refs_7_), channel_id=1, source_target_pairs={{0,7},{1,0},{2,1},{3,2},{4,3},{5,4},{6,5},{7,6},{8,15},{9,8},{10,9... | collective-permute-start | bytes 491528 | tf_op jit(solution)/shard_map/ppermute | solution.py:283
  91.3 7.1 %collective-permute-start.18 = (bf16[160,512]{1,0:T(8,128)(2,1)S(1)}, bf16[160,512]{1,0:T(8,128)(2,1)S(1)}, u32[]{:S(2)}, u32[]{:S(2)}) collective-permute-start(bf16[160,512]{1,0:T(8,128)(2,1)S(1)} %collective-permute-done.14.refs_8_), channel_id=1, source_target_pairs={{0,1},{1,2},{2,3},{3,4},{4,5},{5,6},{6,7},{7,0},{8,9},{9,10},{10,1... | collective-permute-start | bytes 491528 | tf_op jit(solution)/shard_map/ppermute | solution.py:283
  91.4 7.0 %collective-permute-start.20 = (bf16[160,512]{1,0:T(8,128)(2,1)S(1)}, bf16[160,512]{1,0:T(8,128)(2,1)S(1)}, u32[]{:S(2)}, u32[]{:S(2)}) collective-permute-start(bf16[160,512]{1,0:T(8,128)(2,1)S(1)} %collective-permute-done.16.refs_10_), channel_id=1, source_target_pairs={{0,7},{1,0},{2,1},{3,2},{4,3},{5,4},{6,5},{7,6},{8,15},{9,8},{10,9... | collective-permute-start | bytes 491528 | tf_op jit(solution)/shard_map/ppermute | solution.py:283
  94.5 6.9 %collective-permute-start.21 = (bf16[160,512]{1,0:T(8,128)(2,1)S(1)}, bf16[160,512]{1,0:T(8,128)(2,1)}, u32[]{:S(2)}, u32[]{:S(2)}) collective-permute-start(bf16[160,512]{1,0:T(8,128)(2,1)S(1)} %collective-permute-done.19.refs_13_), channel_id=1, source_target_pairs={{0,1},{1,2},{2,3},{3,4},{4,5},{5,6},{6,7},{7,0},{8,9},{9,10},{10,1... | collective-permute-start | bytes 491528 | tf_op jit(solution)/shard_map/ppermute | solution.py:283
  108.4 4.5 %collective-permute-start.22 = (bf16[128,256]{1,0:T(8,128)(2,1)S(1)}, bf16[128,256]{1,0:T(8,128)(2,1)S(1)}, u32[]{:S(2)}, u32[]{:S(2)}) collective-permute-start(bf16[128,256]{1,0:T(8,128)(2,1)S(1)} %get-tuple-element.28.attended), channel_id=1, source_target_pairs={{0,8},{8,0},{1,9},{9,1},{2,10},{10,2},{3,11},{11,3},{4,12},{12,4},... | collective-permute-start | bytes 196616 | tf_op jit(solution)/shard_map/ppermute | solution.py:287
  (22 other events, 109.8 us)

commit v4 on v3

--- a/solution.py
+++ b/solution.py
@@ -318,21 +318,23 @@
 
     tags = exchange(make_tags(rows, nbr_index, devices))
 
+    part = 2 * DH // chips
+    wo_rows = lax.dynamic_slice_in_dim(wo_enc, chip * part, part, 0)
+    tags, wo_rows = lax.optimization_barrier((tags, wo_rows))
+
+    box = outbox(tags, nbr_query, devices)
+    box, wkv_dec, wo_rows, wkv_enc = lax.optimization_barrier((box, wkv_dec, wo_rows, wkv_enc))
+    inbox = exchange(box)
+
     pairs = jnp.dot(
         span_states, wkv_enc.reshape(hidden, -1), preferred_element_type=F32
     ).astype(BF)
-    part = 2 * DH // chips
-    wo_rows = lax.dynamic_slice_in_dim(wo_enc, chip * part, part, 0)
-    tags, wo_rows, pairs = lax.optimization_barrier((tags, wo_rows, pairs))
-
-    box = outbox(tags, nbr_query, devices)
-    box, wkv_dec, wo_rows, pairs = lax.optimization_barrier((box, wkv_dec, wo_rows, pairs))
-    inbox = exchange(box)
-
     wo_rows = ring(wo_rows, True)
     product = multiply(place, wkv_dec.reshape(hidden, -1), wo_rows, devices)
     grad_near = sibling(grad_out)
-    inbox, product, grad_near = lax.optimization_barrier((inbox, product, grad_near))
+    inbox, product, grad_near, pairs = lax.optimization_barrier(
+        (inbox, product, grad_near, pairs)
+    )
 
     w0, w1 = encode(nbr_index, inbox, pairs)
     product = exchange(product).reshape((chips, 2) + product.shape[1:])

time: 139 us -> 137 us (0.986)
  waiting for transfers between devices: 13.8 us -> 19.9 us
  local copies, waits for them, and re-layouts: 9.97 us -> 6.69 us
  starting transfers between devices: 68.2 us -> 65.2 us
  matrix products: 2.96 us -> 0.72 us
    all_to_all x3, waiting for transfers between devices: 0.01 us -> 6.82 us  [exchange(): return lax.all_to_all(x, SEQ, split_axis=0, concat_axis=0, tiled=True)]
    unnamed x58 -> x60, local copies, waits for them, and re-layouts: 9.96 us -> 6.67 us
    all_to_all x3, starting transfers between devices: 25.9 us -> 23.6 us  [exchange(): return lax.all_to_all(x, SEQ, split_axis=0, concat_axis=0, tiled=True)]
    dot_general x1, matrix products: 2.96 us -> 0.72 us  [local(): jnp.dot(span_states, wkv_enc.reshape(hidden, -1), preferred_element_type=...]
  transfers between devices with their start and end apart: 26 -> 26, of which waited for: 10 -> 10; matrix products, arithmetic and copies ran while one was open for 8% -> 3% of each run, Pallas kernels for 4% -> 4%
where the time goes in v4:
time: 137 us
  starting transfers between devices  65.2 us (48%)
  blocking collectives  23.5 us (17%)
  waiting for transfers between devices  19.9 us (15%)
  Pallas kernels  19.4 us (14%)
  local copies, waits for them, and re-layouts  6.69 us (5%)
    ppermute x21, starting transfers between devices, shift(): return lax.ppermute(x, axis, [(i, (i + step) % n) for i in range(n)])  37.6 us
    all_to_all x3, starting transfers between devices, exchange(): return lax.all_to_all(x, SEQ, split_axis=0, concat_axis=0, tiled=True)  23.6 us
    all_to_all x1, blocking collectives, exchange_over(): return lax.all_to_all(x, axis, split_axis=0, concat_axis=0, tiled=True)  23.5 us
    ppermute x21, waiting for transfers between devices, shift(): return lax.ppermute(x, axis, [(i, (i + step) % n) for i in range(n)])  12.1 us
    pallas_call x1, Pallas kernels, decode(): pl.pallas_call(functools.partial(decode_kernel, part, order), out_shape=(...  6.96 us
    all_to_all x3, waiting for transfers between devices, exchange(): return lax.all_to_all(x, SEQ, split_axis=0, concat_axis=0, tiled=True)  6.82 us
    unnamed x60, local copies, waits for them, and re-layouts  6.67 us
    ppermute x2, starting transfers between devices, sibling(): return lax.ppermute(x, 'core', [(0, 1), (1, 0)])  3.99 us
  transfers between devices with their start and end apart: 26, of which 10 were waited for; matrix products, arithmetic and copies ran while one was open for 3% of the time, Pallas kernels for 4%

profile of v4, /device:TPU:1, one launch (start us, length us, event | category | flops | bytes accessed | tf_op | source)
XLA Modules:
  0.0 136.5 jit_solution(5050683397125071655)
XLA Ops:
  0.7 1.7 %shard_map.104 = s32[32,1,1]{2,1,0:T(1,128)} custom-call(s32[2,4]{1,0:T(2,128)} %index.3), custom_call_target="tpu_custom_call" | custom-call | tf_op jit(solution)/shard_map/pallas_call | solution.py:36
  2.3 8.6 %all-to-all-start = ((s32[32,1,1]{2,1,0:T(1,128)}), s32[32,1,1]{2,1,0:T(1,128)S(1)}, u32[]{:S(2)}, u32[]{:S(2)}) async-start(s32[32,1,1]{2,1,0:T(1,128)} %shard_map.104), calls=%async_computation | async-start | bytes 32768 | tf_op jit(solution)/shard_map/all_to_all | solution.py:295
  11.0 6.8 %all-to-all-done.tags = s32[32,1,1]{2,1,0:T(1,128)S(1)} async-done(((s32[32,1,1]{2,1,0:T(1,128)}), s32[32,1,1]{2,1,0:T(1,128)S(1)}, u32[]{:S(2)}, u32[]{:S(2)}) %all-to-all-start) | async-done | bytes 160 | tf_op jit(solution)/shard_map/all_to_all | solution.py:295
  18.4 2.2 %shard_map.105 = bf16[32,128,256]{2,1,0:T(8,128)(2,1)} custom-call(s32[32,1,1]{2,1,0:T(1,128)} %copy-done.28, bf16[8,128,256]{2,1,0:T(8,128)(2,1)} %query.2), custom_call_target="tpu_custom_call" | custom-call | tf_op jit(solution)/shard_map/pallas_call | solution.py:104
  20.6 5.0 %all-to-all-start.1 = ((bf16[32,128,256]{2,1,0:T(8,128)(2,1)}), bf16[32,128,256]{2,1,0:T(8,128)(2,1)}, u32[]{:S(2)}, u32[]{:S(2)}) async-start(bf16[32,128,256]{2,1,0:T(8,128)(2,1)} %shard_map.105), calls=%async_computation.1 | async-start | bytes 4194304 | tf_op jit(solution)/shard_map/all_to_all | solution.py:295
  26.1 5.6 %collective-permute-start = (bf16[16,4096]{1,0:T(8,128)(2,1)S(1)}, bf16[16,4096]{1,0:T(8,128)(2,1)S(1)}, u32[]{:S(2)}, u32[]{:S(2)}) collective-permute-start(bf16[16,4096]{1,0:T(8,128)(2,1)S(1)} %constant_dynamic-slice_fusion.refs_0_), channel_id=1, source_target_pairs={{0,7},{1,0},{2,1},{3,2},{4,3},{5,4},{6,5},{7,6},{8,15},{9,8},{10,9... | collective-permute-start | bytes 393224 | tf_op jit(solution)/shard_map/ppermute | solution.py:283
  31.7 2.8 %collective-permute-done.refs_1_ = bf16[16,4096]{1,0:T(8,128)(2,1)S(1)} collective-permute-done((bf16[16,4096]{1,0:T(8,128)(2,1)S(1)}, bf16[16,4096]{1,0:T(8,128)(2,1)S(1)}, u32[]{:S(2)}, u32[]{:S(2)}) %collective-permute-start) | collective-permute-done | bytes 131104 | tf_op jit(solution)/shard_map/ppermute | solution.py:283
  34.5 3.5 %collective-permute-start.1 = (bf16[16,4096]{1,0:T(8,128)(2,1)S(1)}, bf16[16,4096]{1,0:T(8,128)(2,1)S(1)}, u32[]{:S(2)}, u32[]{:S(2)}) collective-permute-start(bf16[16,4096]{1,0:T(8,128)(2,1)S(1)} %collective-permute-done.refs_1_), channel_id=1, source_target_pairs={{0,7},{1,0},{2,1},{3,2},{4,3},{5,4},{6,5},{7,6},{8,15},{9,8},{10,9... | collective-permute-start | bytes 393224 | tf_op jit(solution)/shard_map/ppermute | solution.py:283
  38.1 1.9 %collective-permute-done.1.refs_2_ = bf16[16,4096]{1,0:T(8,128)(2,1)S(1)} collective-permute-done((bf16[16,4096]{1,0:T(8,128)(2,1)S(1)}, bf16[16,4096]{1,0:T(8,128)(2,1)S(1)}, u32[]{:S(2)}, u32[]{:S(2)}) %collective-permute-start.1) | collective-permute-done | bytes 131104 | tf_op jit(solution)/shard_map/ppermute | solution.py:283
  40.0 3.6 %collective-permute-start.2 = (bf16[16,4096]{1,0:T(8,128)(2,1)S(1)}, bf16[16,4096]{1,0:T(8,128)(2,1)}, u32[]{:S(2)}, u32[]{:S(2)}) collective-permute-start(bf16[16,4096]{1,0:T(8,128)(2,1)S(1)} %collective-permute-done.1.refs_2_), channel_id=1, source_target_pairs={{0,7},{1,0},{2,1},{3,2},{4,3},{5,4},{6,5},{7,6},{8,15},{9,8},{10,9... | collective-permute-start | bytes 393224 | tf_op jit(solution)/shard_map/ppermute | solution.py:283
  43.7 3.0 %copy.14 = bf16[512,8,2,256]{3,1,2,0:T(8,128)(2,1)S(1)} copy(bf16[512,8,2,256]{3,2,1,0:T(2,128)(2,1)} %bitcast.13) | data formatting | bytes 8388608
  46.9 2.7 %collective-permute-start.3 = (bf16[16,4096]{1,0:T(8,128)(2,1)}, bf16[16,4096]{1,0:T(8,128)(2,1)S(1)}, u32[]{:S(2)}, u32[]{:S(2)}) collective-permute-start(bf16[16,4096]{1,0:T(8,128)(2,1)} %collective-permute-done.2.refs_3_), channel_id=1, source_target_pairs={{0,7},{1,0},{2,1},{3,2},{4,3},{5,4},{6,5},{7,6},{8,15},{9,8},{10,9... | collective-permute-start | bytes 393224 | tf_op jit(solution)/shard_map/ppermute | solution.py:283
  50.3 0.9 copy.13
  51.2 0.9 collective-permute-done.6.refs_5_
  52.8 3.9 %shard_map.106 = bf16[32,128,256]{2,1,0:T(8,128)(2,1)} custom-call(s32[2]{0:T(128)S(1)} %pad_add_fusion.place, bf16[4096,512]{1,0:T(8,128)(2,1)S(1)} %bitcast.11, bf16[16,4096]{1,0:T(8,128)(2,1)} %copy-done.9, bf16[16,4096]{1,0:T(8,128)(2,1)} %copy-done.23, bf16[16,4096]{1,0:T(8,128)(2,1)} %copy-done.25, bf16[16,4096]{1,0:T(8,128)(2,1)} %collective-permute-done.2.refs_3_, ...), custom_call_target="tpu_custom_call" | custom-call | tf_op jit(solution)/shard_map/pallas_call | solution.py:70
  56.8 10.0 %all-to-all-start.2 = ((bf16[32,128,256]{2,1,0:T(8,128)(2,1)}), bf16[32,128,256]{2,1,0:T(8,128)(2,1)}, u32[]{:S(2)}, u32[]{:S(2)}) async-start(bf16[32,128,256]{2,1,0:T(8,128)(2,1)} %shard_map.106), calls=%async_computation.2 | async-start | bytes 4194304 | tf_op jit(solution)/shard_map/all_to_all | solution.py:295
  66.8 2.1 %shard_map.107 = (bf16[160,512]{1,0:T(8,128)(2,1)S(1)}, bf16[160,512]{1,0:T(8,128)(2,1)S(1)}) custom-call(s32[2,4]{1,0:T(2,128)S(1)} %copy-done.5, bf16[32,128,256]{2,1,0:T(8,128)(2,1)} %all-to-all-done.1.inbox, bf16[128,512]{1,0:T(8,128)(2,1)S(1)} %fusion.pairs), custom_call_target="tpu_custom_call" | custom-call | tf_op jit(solution)/shard_map/pallas_call | solution.py:148
  69.0 3.0 %collective-permute-start.8 = (bf16[160,512]{1,0:T(8,128)(2,1)S(1)}, bf16[160,512]{1,0:T(8,128)(2,1)S(1)}, u32[]{:S(2)}, u32[]{:S(2)}) collective-permute-start(bf16[160,512]{1,0:T(8,128)(2,1)S(1)} %get-tuple-element.25.refs_0_), channel_id=1, source_target_pairs={{0,7},{1,0},{2,1},{3,2},{4,3},{5,4},{6,5},{7,6},{8,15},{9,8},{10,9... | collective-permute-start | bytes 491528 | tf_op jit(solution)/shard_map/ppermute | solution.py:283
  71.9 2.7 %collective-permute-start.9 = (bf16[160,512]{1,0:T(8,128)(2,1)S(1)}, bf16[160,512]{1,0:T(8,128)(2,1)S(1)}, u32[]{:S(2)}, u32[]{:S(2)}) collective-permute-start(bf16[160,512]{1,0:T(8,128)(2,1)S(1)} %get-tuple-element.26.refs_1_), channel_id=1, source_target_pairs={{0,7},{1,0},{2,1},{3,2},{4,3},{5,4},{6,5},{7,6},{8,15},{9,8},{10,9... | collective-permute-start | bytes 491528 | tf_op jit(solution)/shard_map/ppermute | solution.py:283
  75.2 3.5 %collective-permute-start.12 = (bf16[160,512]{1,0:T(8,128)(2,1)S(1)}, bf16[160,512]{1,0:T(8,128)(2,1)S(1)}, u32[]{:S(2)}, u32[]{:S(2)}) collective-permute-start(bf16[160,512]{1,0:T(8,128)(2,1)S(1)} %collective-permute-done.8.refs_2_), channel_id=1, source_target_pairs={{0,7},{1,0},{2,1},{3,2},{4,3},{5,4},{6,5},{7,6},{8,15},{9,8},{10,9... | collective-permute-start | bytes 491528 | tf_op jit(solution)/shard_map/ppermute | solution.py:283
  78.8 3.5 %collective-permute-start.13 = (bf16[160,512]{1,0:T(8,128)(2,1)S(1)}, bf16[160,512]{1,0:T(8,128)(2,1)S(1)}, u32[]{:S(2)}, u32[]{:S(2)}) collective-permute-start(bf16[160,512]{1,0:T(8,128)(2,1)S(1)} %collective-permute-done.9.refs_3_), channel_id=1, source_target_pairs={{0,7},{1,0},{2,1},{3,2},{4,3},{5,4},{6,5},{7,6},{8,15},{9,8},{10,9... | collective-permute-start | bytes 491528 | tf_op jit(solution)/shard_map/ppermute | solution.py:283
  82.4 2.7 %collective-permute-start.16 = (bf16[160,512]{1,0:T(8,128)(2,1)S(1)}, bf16[160,512]{1,0:T(8,128)(2,1)S(1)}, u32[]{:S(2)}, u32[]{:S(2)}) collective-permute-start(bf16[160,512]{1,0:T(8,128)(2,1)S(1)} %collective-permute-done.12.refs_6_), channel_id=1, source_target_pairs={{0,7},{1,0},{2,1},{3,2},{4,3},{5,4},{6,5},{7,6},{8,15},{9,8},{10,9... | collective-permute-start | bytes 491528 | tf_op jit(solution)/shard_map/ppermute | solution.py:283
  85.2 3.5 %collective-permute-start.17 = (bf16[160,512]{1,0:T(8,128)(2,1)S(1)}, bf16[160,512]{1,0:T(8,128)(2,1)S(1)}, u32[]{:S(2)}, u32[]{:S(2)}) collective-permute-start(bf16[160,512]{1,0:T(8,128)(2,1)S(1)} %collective-permute-done.13.refs_7_), channel_id=1, source_target_pairs={{0,7},{1,0},{2,1},{3,2},{4,3},{5,4},{6,5},{7,6},{8,15},{9,8},{10,9... | collective-permute-start | bytes 491528 | tf_op jit(solution)/shard_map/ppermute | solution.py:283
  88.9 3.1 %collective-permute-start.20 = (bf16[160,512]{1,0:T(8,128)(2,1)S(1)}, bf16[160,512]{1,0:T(8,128)(2,1)S(1)}, u32[]{:S(2)}, u32[]{:S(2)}) collective-permute-start(bf16[160,512]{1,0:T(8,128)(2,1)S(1)} %collective-permute-done.16.refs_10_), channel_id=1, source_target_pairs={{0,7},{1,0},{2,1},{3,2},{4,3},{5,4},{6,5},{7,6},{8,15},{9,8},{10,9... | collective-permute-start | bytes 491528 | tf_op jit(solution)/shard_map/ppermute | solution.py:283
  92.2 3.8 %collective-permute-done.18.refs_12_ = bf16[160,512]{1,0:T(8,128)(2,1)S(1)} collective-permute-done((bf16[160,512]{1,0:T(8,128)(2,1)S(1)}, bf16[160,512]{1,0:T(8,128)(2,1)S(1)}, u32[]{:S(2)}, u32[]{:S(2)}) %collective-permute-start.18) | collective-permute-done | bytes 163872 | tf_op jit(solution)/shard_map/ppermute | solution.py:283
  97.4 1.8 %collective-permute-done.21.refs_15_ = bf16[160,512]{1,0:T(8,128)(2,1)} collective-permute-done((bf16[160,512]{1,0:T(8,128)(2,1)S(1)}, bf16[160,512]{1,0:T(8,128)(2,1)}, u32[]{:S(2)}, u32[]{:S(2)}) %collective-permute-start.21) | collective-permute-done | bytes 163872 | tf_op jit(solution)/shard_map/ppermute | solution.py:283
  99.1 7.0 %shard_map.108 = (bf16[128,256]{1,0:T(8,128)(2,1)}, bf16[128,256]{1,0:T(8,128)(2,1)S(1)}) custom-call(s32[2]{0:T(128)S(1)} %pad_add_fusion.place, s32[2]{0:T(128)S(1)} %copy-done.6, bf16[128,256]{1,0:T(8,128)(2,1)S(1)} %copy-done.4, bf16[16,2,128,256]{3,2,1,0:T(8,128)(2,1)} %bitcast.3.product, bf16[160,512]{1,0:T(8,128)(2,1)} %copy-done.2, ...), custom_call_target="tpu_custom_call" | custom-call | tf_op jit(solution)/shard_map/pallas_call | solution.py:222
  106.1 3.5 %collective-permute-start.22 = (bf16[128,256]{1,0:T(8,128)(2,1)S(1)}, bf16[128,256]{1,0:T(8,128)(2,1)S(1)}, u32[]{:S(2)}, u32[]{:S(2)}) collective-permute-start(bf16[128,256]{1,0:T(8,128)(2,1)S(1)} %get-tuple-element.28.attended), channel_id=1, source_target_pairs={{0,8},{8,0},{1,9},{9,1},{2,10},{10,2},{3,11},{11,3},{4,12},{12,4},... | collective-permute-start | bytes 196616 | tf_op jit(solution)/shard_map/ppermute | solution.py:287
  109.6 0.9 collective-permute-done.22.near
  110.5 1.7 %shard_map.109 = bf16[16,256,128]{2,1,0:T(8,128)(2,1)S(1)} custom-call(s32[2]{0:T(128)S(1)} %pad_add_fusion.place, bf16[128,256]{1,0:T(8,128)(2,1)S(1)} %get-tuple-element.28.attended, bf16[128,256]{1,0:T(8,128)(2,1)S(1)} %collective-permute-done.22.near, bf16[128,4096]{1,0:T(8,128)(2,1)S(1)} %copy-done.1, bf16[128,4096]{1,0:T(8,128)(2,1)} %collective-permute-done.7.near_grad), custom_call_target="tpu_custom_call" | custom-call | tf_op jit(solution)/shard_map/pallas_call | solution.py:253
  112.2 23.5 %all_to_all.20.parts = bf16[16,256,128]{2,1,0:T(8,128)(2,1)S(1)} all-to-all(bf16[16,256,128]{2,1,0:T(8,128)(2,1)S(1)} %shard_map.109), channel_id=1, replica_groups=mesh['chip'=16,'core'=2,'mp'=8] {'chip'}, dimensions={0} | all-to-all | bytes 2097152 | tf_op jit(solution)/shard_map/all_to_all | solution.py:291
  135.7 0.8 shard_map.110
  (91 shorter events, 5.4 us)
Async XLA Ops:
  0.6 24.9 %copy-start.1 = (bf16[128,4096]{1,0:T(8,128)(2,1)S(1)}, bf16[128,4096]{1,0:T(8,128)(2,1)}, u32[]{:S(2)}) copy-start(bf16[128,4096]{1,0:T(8,128)(2,1)} %grad.1) | copy-start | bytes 3145732
  2.3 15.5 %all-to-all-start = ((s32[32,1,1]{2,1,0:T(1,128)}), s32[32,1,1]{2,1,0:T(1,128)S(1)}, u32[]{:S(2)}, u32[]{:S(2)}) async-start(s32[32,1,1]{2,1,0:T(1,128)} %shard_map.104), calls=%async_computation | async-start | bytes 32768 | tf_op jit(solution)/shard_map/all_to_all | solution.py:295
  11.0 35.8 %copy-start.9 = (bf16[16,4096]{1,0:T(8,128)(2,1)}, bf16[16,4096]{1,0:T(8,128)(2,1)S(1)}, u32[]{:S(2)}) copy-start(bf16[16,4096]{1,0:T(8,128)(2,1)S(1)} %constant_dynamic-slice_fusion.refs_0_) | copy-start | bytes 393220
  20.6 36.2 %all-to-all-start.1 = ((bf16[32,128,256]{2,1,0:T(8,128)(2,1)}), bf16[32,128,256]{2,1,0:T(8,128)(2,1)}, u32[]{:S(2)}, u32[]{:S(2)}) async-start(bf16[32,128,256]{2,1,0:T(8,128)(2,1)} %shard_map.105), calls=%async_computation.1 | async-start | bytes 4194304 | tf_op jit(solution)/shard_map/all_to_all | solution.py:295
  25.6 31.2 %collective-permute-start.7 = (bf16[128,4096]{1,0:T(8,128)(2,1)S(1)}, bf16[128,4096]{1,0:T(8,128)(2,1)}, u32[]{:S(2)}, u32[]{:S(2)}) collective-permute-start(bf16[128,4096]{1,0:T(8,128)(2,1)S(1)} %copy-done.1), channel_id=1, source_target_pairs={{0,8},{8,0},{1,9},{9,1},{2,10},{10,2},{3,11},{11,3},{4,12},{12,4},... | collective-permute-start | bytes 3145736 | tf_op jit(solution)/shard_map/ppermute | solution.py:287
  26.1 8.4 %collective-permute-start = (bf16[16,4096]{1,0:T(8,128)(2,1)S(1)}, bf16[16,4096]{1,0:T(8,128)(2,1)S(1)}, u32[]{:S(2)}, u32[]{:S(2)}) collective-permute-start(bf16[16,4096]{1,0:T(8,128)(2,1)S(1)} %constant_dynamic-slice_fusion.refs_0_), channel_id=1, source_target_pairs={{0,7},{1,0},{2,1},{3,2},{4,3},{5,4},{6,5},{7,6},{8,15},{9,8},{10,9... | collective-permute-start | bytes 393224 | tf_op jit(solution)/shard_map/ppermute | solution.py:283
  31.7 6.4 %collective-permute-start.4 = (bf16[16,4096]{1,0:T(8,128)(2,1)S(1)}, bf16[16,4096]{1,0:T(8,128)(2,1)S(1)}, u32[]{:S(2)}, u32[]{:S(2)}) collective-permute-start(bf16[16,4096]{1,0:T(8,128)(2,1)S(1)} %constant_dynamic-slice_fusion.refs_0_), channel_id=1, source_target_pairs={{0,1},{1,2},{2,3},{3,4},{4,5},{5,6},{6,7},{7,0},{8,9},{9,10},{10,1... | collective-permute-start | bytes 393224 | tf_op jit(solution)/shard_map/ppermute | solution.py:283
  34.5 5.5 %collective-permute-start.1 = (bf16[16,4096]{1,0:T(8,128)(2,1)S(1)}, bf16[16,4096]{1,0:T(8,128)(2,1)S(1)}, u32[]{:S(2)}, u32[]{:S(2)}) collective-permute-start(bf16[16,4096]{1,0:T(8,128)(2,1)S(1)} %collective-permute-done.refs_1_), channel_id=1, source_target_pairs={{0,7},{1,0},{2,1},{3,2},{4,3},{5,4},{6,5},{7,6},{8,15},{9,8},{10,9... | collective-permute-start | bytes 393224 | tf_op jit(solution)/shard_map/ppermute | solution.py:283
  38.1 8.7 %collective-permute-start.5 = (bf16[16,4096]{1,0:T(8,128)(2,1)S(1)}, bf16[16,4096]{1,0:T(8,128)(2,1)}, u32[]{:S(2)}, u32[]{:S(2)}) collective-permute-start(bf16[16,4096]{1,0:T(8,128)(2,1)S(1)} %collective-permute-done.4.refs_7_), channel_id=1, source_target_pairs={{0,1},{1,2},{2,3},{3,4},{4,5},{5,6},{6,7},{7,0},{8,9},{9,10},{10,1... | collective-permute-start | bytes 393224 | tf_op jit(solution)/shard_map/ppermute | solution.py:283
  40.0 6.9 %collective-permute-start.2 = (bf16[16,4096]{1,0:T(8,128)(2,1)S(1)}, bf16[16,4096]{1,0:T(8,128)(2,1)}, u32[]{:S(2)}, u32[]{:S(2)}) collective-permute-start(bf16[16,4096]{1,0:T(8,128)(2,1)S(1)} %collective-permute-done.1.refs_2_), channel_id=1, source_target_pairs={{0,7},{1,0},{2,1},{3,2},{4,3},{5,4},{6,5},{7,6},{8,15},{9,8},{10,9... | collective-permute-start | bytes 393224 | tf_op jit(solution)/shard_map/ppermute | solution.py:283
  46.8 5.3 %collective-permute-start.6 = (bf16[16,4096]{1,0:T(8,128)(2,1)}, bf16[16,4096]{1,0:T(8,128)(2,1)S(1)}, u32[]{:S(2)}, u32[]{:S(2)}) collective-permute-start(bf16[16,4096]{1,0:T(8,128)(2,1)} %collective-permute-done.5.refs_6_), channel_id=1, source_target_pairs={{0,1},{1,2},{2,3},{3,4},{4,5},{5,6},{6,7},{7,0},{8,9},{9,10},{10,1... | collective-permute-start | bytes 393224 | tf_op jit(solution)/shard_map/ppermute | solution.py:283
  46.9 5.2 %collective-permute-start.3 = (bf16[16,4096]{1,0:T(8,128)(2,1)}, bf16[16,4096]{1,0:T(8,128)(2,1)S(1)}, u32[]{:S(2)}, u32[]{:S(2)}) collective-permute-start(bf16[16,4096]{1,0:T(8,128)(2,1)} %collective-permute-done.2.refs_3_), channel_id=1, source_target_pairs={{0,7},{1,0},{2,1},{3,2},{4,3},{5,4},{6,5},{7,6},{8,15},{9,8},{10,9... | collective-permute-start | bytes 393224 | tf_op jit(solution)/shard_map/ppermute | solution.py:283
  56.7 42.4 %copy-start.4 = (bf16[128,256]{1,0:T(8,128)(2,1)S(1)}, bf16[128,256]{1,0:T(8,128)(2,1)}, u32[]{:S(2)}) copy-start(bf16[128,256]{1,0:T(8,128)(2,1)} %query.3) | copy-start | bytes 196612
  56.7 42.4 %copy-start.6 = (s32[2]{0:T(128)S(1)}, s32[2]{0:T(128)}, u32[]{:S(2)}) copy-start(s32[2]{0:T(128)} %counts.1) | copy-start | bytes 28
  56.8 42.3 %all-to-all-start.2 = ((bf16[32,128,256]{2,1,0:T(8,128)(2,1)}), bf16[32,128,256]{2,1,0:T(8,128)(2,1)}, u32[]{:S(2)}, u32[]{:S(2)}) async-start(bf16[32,128,256]{2,1,0:T(8,128)(2,1)} %shard_map.106), calls=%async_computation.2 | async-start | bytes 4194304 | tf_op jit(solution)/shard_map/all_to_all | solution.py:295
  69.0 30.1 %copy-start.2 = (bf16[160,512]{1,0:T(8,128)(2,1)}, bf16[160,512]{1,0:T(8,128)(2,1)S(1)}, u32[]{:S(2)}) copy-start(bf16[160,512]{1,0:T(8,128)(2,1)S(1)} %get-tuple-element.25.refs_0_) | copy-start | bytes 491524
  69.0 6.2 %collective-permute-start.8 = (bf16[160,512]{1,0:T(8,128)(2,1)S(1)}, bf16[160,512]{1,0:T(8,128)(2,1)S(1)}, u32[]{:S(2)}, u32[]{:S(2)}) collective-permute-start(bf16[160,512]{1,0:T(8,128)(2,1)S(1)} %get-tuple-element.25.refs_0_), channel_id=1, source_target_pairs={{0,7},{1,0},{2,1},{3,2},{4,3},{5,4},{6,5},{7,6},{8,15},{9,8},{10,9... | collective-permute-start | bytes 491528 | tf_op jit(solution)/shard_map/ppermute | solution.py:283
  71.9 6.8 %collective-permute-start.11 = (bf16[160,512]{1,0:T(8,128)(2,1)S(1)}, bf16[160,512]{1,0:T(8,128)(2,1)S(1)}, u32[]{:S(2)}, u32[]{:S(2)}) collective-permute-start(bf16[160,512]{1,0:T(8,128)(2,1)S(1)} %get-tuple-element.26.refs_1_), channel_id=1, source_target_pairs={{0,1},{1,2},{2,3},{3,4},{4,5},{5,6},{6,7},{7,0},{8,9},{9,10},{10,1... | collective-permute-start | bytes 491528 | tf_op jit(solution)/shard_map/ppermute | solution.py:283
  71.9 6.8 %collective-permute-start.9 = (bf16[160,512]{1,0:T(8,128)(2,1)S(1)}, bf16[160,512]{1,0:T(8,128)(2,1)S(1)}, u32[]{:S(2)}, u32[]{:S(2)}) collective-permute-start(bf16[160,512]{1,0:T(8,128)(2,1)S(1)} %get-tuple-element.26.refs_1_), channel_id=1, source_target_pairs={{0,7},{1,0},{2,1},{3,2},{4,3},{5,4},{6,5},{7,6},{8,15},{9,8},{10,9... | collective-permute-start | bytes 491528 | tf_op jit(solution)/shard_map/ppermute | solution.py:283
  74.6 7.6 %collective-permute-start.10 = (bf16[160,512]{1,0:T(8,128)(2,1)S(1)}, bf16[160,512]{1,0:T(8,128)(2,1)S(1)}, u32[]{:S(2)}, u32[]{:S(2)}) collective-permute-start(bf16[160,512]{1,0:T(8,128)(2,1)S(1)} %get-tuple-element.25.refs_0_), channel_id=1, source_target_pairs={{0,1},{1,2},{2,3},{3,4},{4,5},{5,6},{6,7},{7,0},{8,9},{9,10},{10,1... | collective-permute-start | bytes 491528 | tf_op jit(solution)/shard_map/ppermute | solution.py:283
  75.2 23.9 %copy-start.10 = (bf16[160,512]{1,0:T(8,128)(2,1)}, bf16[160,512]{1,0:T(8,128)(2,1)S(1)}, u32[]{:S(2)}) copy-start(bf16[160,512]{1,0:T(8,128)(2,1)S(1)} %collective-permute-done.8.refs_2_) | copy-start | bytes 491524
  75.2 7.1 %collective-permute-start.12 = (bf16[160,512]{1,0:T(8,128)(2,1)S(1)}, bf16[160,512]{1,0:T(8,128)(2,1)S(1)}, u32[]{:S(2)}, u32[]{:S(2)}) collective-permute-start(bf16[160,512]{1,0:T(8,128)(2,1)S(1)} %collective-permute-done.8.refs_2_), channel_id=1, source_target_pairs={{0,7},{1,0},{2,1},{3,2},{4,3},{5,4},{6,5},{7,6},{8,15},{9,8},{10,9... | collective-permute-start | bytes 491528 | tf_op jit(solution)/shard_map/ppermute | solution.py:283
  78.7 6.3 %collective-permute-start.15 = (bf16[160,512]{1,0:T(8,128)(2,1)S(1)}, bf16[160,512]{1,0:T(8,128)(2,1)S(1)}, u32[]{:S(2)}, u32[]{:S(2)}) collective-permute-start(bf16[160,512]{1,0:T(8,128)(2,1)S(1)} %collective-permute-done.11.refs_5_), channel_id=1, source_target_pairs={{0,1},{1,2},{2,3},{3,4},{4,5},{5,6},{6,7},{7,0},{8,9},{9,10},{10,1... | collective-permute-start | bytes 491528 | tf_op jit(solution)/shard_map/ppermute | solution.py:283
  78.8 6.4 %collective-permute-start.13 = (bf16[160,512]{1,0:T(8,128)(2,1)S(1)}, bf16[160,512]{1,0:T(8,128)(2,1)S(1)}, u32[]{:S(2)}, u32[]{:S(2)}) collective-permute-start(bf16[160,512]{1,0:T(8,128)(2,1)S(1)} %collective-permute-done.9.refs_3_), channel_id=1, source_target_pairs={{0,7},{1,0},{2,1},{3,2},{4,3},{5,4},{6,5},{7,6},{8,15},{9,8},{10,9... | collective-permute-start | bytes 491528 | tf_op jit(solution)/shard_map/ppermute | solution.py:283
  82.3 6.6 %collective-permute-start.14 = (bf16[160,512]{1,0:T(8,128)(2,1)S(1)}, bf16[160,512]{1,0:T(8,128)(2,1)S(1)}, u32[]{:S(2)}, u32[]{:S(2)}) collective-permute-start(bf16[160,512]{1,0:T(8,128)(2,1)S(1)} %collective-permute-done.10.refs_4_), channel_id=1, source_target_pairs={{0,1},{1,2},{2,3},{3,4},{4,5},{5,6},{6,7},{7,0},{8,9},{9,10},{10,1... | collective-permute-start | bytes 491528 | tf_op jit(solution)/shard_map/ppermute | solution.py:283
  82.4 6.5 %collective-permute-start.16 = (bf16[160,512]{1,0:T(8,128)(2,1)S(1)}, bf16[160,512]{1,0:T(8,128)(2,1)S(1)}, u32[]{:S(2)}, u32[]{:S(2)}) collective-permute-start(bf16[160,512]{1,0:T(8,128)(2,1)S(1)} %collective-permute-done.12.refs_6_), channel_id=1, source_target_pairs={{0,7},{1,0},{2,1},{3,2},{4,3},{5,4},{6,5},{7,6},{8,15},{9,8},{10,9... | collective-permute-start | bytes 491528 | tf_op jit(solution)/shard_map/ppermute | solution.py:283
  85.1 7.0 %collective-permute-start.19 = (bf16[160,512]{1,0:T(8,128)(2,1)S(1)}, bf16[160,512]{1,0:T(8,128)(2,1)S(1)}, u32[]{:S(2)}, u32[]{:S(2)}) collective-permute-start(bf16[160,512]{1,0:T(8,128)(2,1)S(1)} %collective-permute-done.15.refs_9_), channel_id=1, source_target_pairs={{0,1},{1,2},{2,3},{3,4},{4,5},{5,6},{6,7},{7,0},{8,9},{9,10},{10,1... | collective-permute-start | bytes 491528 | tf_op jit(solution)/shard_map/ppermute | solution.py:283
  85.2 6.9 %collective-permute-start.17 = (bf16[160,512]{1,0:T(8,128)(2,1)S(1)}, bf16[160,512]{1,0:T(8,128)(2,1)S(1)}, u32[]{:S(2)}, u32[]{:S(2)}) collective-permute-start(bf16[160,512]{1,0:T(8,128)(2,1)S(1)} %collective-permute-done.13.refs_7_), channel_id=1, source_target_pairs={{0,7},{1,0},{2,1},{3,2},{4,3},{5,4},{6,5},{7,6},{8,15},{9,8},{10,9... | collective-permute-start | bytes 491528 | tf_op jit(solution)/shard_map/ppermute | solution.py:283
  88.9 7.1 %collective-permute-start.18 = (bf16[160,512]{1,0:T(8,128)(2,1)S(1)}, bf16[160,512]{1,0:T(8,128)(2,1)S(1)}, u32[]{:S(2)}, u32[]{:S(2)}) collective-permute-start(bf16[160,512]{1,0:T(8,128)(2,1)S(1)} %collective-permute-done.14.refs_8_), channel_id=1, source_target_pairs={{0,1},{1,2},{2,3},{3,4},{4,5},{5,6},{6,7},{7,0},{8,9},{9,10},{10,1... | collective-permute-start | bytes 491528 | tf_op jit(solution)/shard_map/ppermute | solution.py:283
  88.9 7.0 %collective-permute-start.20 = (bf16[160,512]{1,0:T(8,128)(2,1)S(1)}, bf16[160,512]{1,0:T(8,128)(2,1)S(1)}, u32[]{:S(2)}, u32[]{:S(2)}) collective-permute-start(bf16[160,512]{1,0:T(8,128)(2,1)S(1)} %collective-permute-done.16.refs_10_), channel_id=1, source_target_pairs={{0,7},{1,0},{2,1},{3,2},{4,3},{5,4},{6,5},{7,6},{8,15},{9,8},{10,9... | collective-permute-start | bytes 491528 | tf_op jit(solution)/shard_map/ppermute | solution.py:283
  92.1 7.0 %collective-permute-start.21 = (bf16[160,512]{1,0:T(8,128)(2,1)S(1)}, bf16[160,512]{1,0:T(8,128)(2,1)}, u32[]{:S(2)}, u32[]{:S(2)}) collective-permute-start(bf16[160,512]{1,0:T(8,128)(2,1)S(1)} %collective-permute-done.19.refs_13_), channel_id=1, source_target_pairs={{0,1},{1,2},{2,3},{3,4},{4,5},{5,6},{6,7},{7,0},{8,9},{9,10},{10,1... | collective-permute-start | bytes 491528 | tf_op jit(solution)/shard_map/ppermute | solution.py:283
  106.1 4.4 %collective-permute-start.22 = (bf16[128,256]{1,0:T(8,128)(2,1)S(1)}, bf16[128,256]{1,0:T(8,128)(2,1)S(1)}, u32[]{:S(2)}, u32[]{:S(2)}) collective-permute-start(bf16[128,256]{1,0:T(8,128)(2,1)S(1)} %get-tuple-element.28.attended), channel_id=1, source_target_pairs={{0,8},{8,0},{1,9},{9,1},{2,10},{10,2},{3,11},{11,3},{4,12},{12,4},... | collective-permute-start | bytes 196616 | tf_op jit(solution)/shard_map/ppermute | solution.py:287
  (23 other events, 117.4 us)

commit v5 on v4

--- a/solution.py
+++ b/solution.py
@@ -158,22 +158,28 @@
     )(index, inbox, pairs)
 
 
-def decode_kernel(part, order, place, counts, query, product, *refs):
-    out, send, folded, held, pieces, sems = refs[-6:]
-    groups = len(order)
+def project(part, order, ranges, product, sources, folded, held, pieces, sems):
     spans = folded.shape[0]
-    tokens = query.shape[0]
-    span_len = tokens // spans
+    span_len = folded.shape[2] // (2 * len(order))
+    tokens = spans * span_len
     slots = pieces.shape[2] // DH
-    slot_tokens = slots * DH
-    copies = [
-        pltpu.make_async_copy(product.at[:, k], held.at[k], sems.at[k]) for k in range(2)
+    arrive = [
+        pltpu.make_async_copy(piece, pieces.at[i], sems.at[i])
+        for i, piece in enumerate(sources)
     ]
-    arrive = [
-        pltpu.make_async_copy(piece, pieces.at[i], sems.at[2 + i])
-        for i, piece in enumerate(refs[:-6])
-    ]
-    for copy in copies[:1] + arrive + copies[1:]:
+    copies = []
+    for k in range(2):
+        for first, last in ranges:
+            rows = pl.ds(first * part, (last - first) * part)
+            copies.append(
+                pltpu.make_async_copy(
+                    product.at[:, k, rows],
+                    held.at[k, :, rows],
+                    sems.at[len(arrive) + len(copies)],
+                )
+            )
+    each = len(ranges)
+    for copy in copies[:each] + arrive + copies[each:]:
         copy.start()
 
     def riding(i):
@@ -181,7 +187,8 @@
         return jnp.concatenate([rows[:, k * DH : (k + 1) * DH] for k in range(slots)], axis=0)
 
     for k in range(2):
-        copies[k].wait()
+        for copy in copies[k * each : (k + 1) * each]:
+            copy.wait()
         for n, g in enumerate(order):
             if k == 0:
                 arrive[2 * n].wait()
@@ -195,10 +202,50 @@
                 both = jnp.concatenate([low[span], high[span]], axis=0).astype(BF)
                 columns = slice(n * 2 * span_len, (n + 1) * 2 * span_len)
                 folded[c, k * 2 * DH : (k + 1) * 2 * DH, columns] = both.T
+    result = []
     for c in range(spans):
-        weights = pieces[:, c * span_len : (c + 1) * span_len].reshape(-1, slot_tokens)
-        both = jnp.dot(folded[c], weights, preferred_element_type=F32).astype(BF)
-        usable = lax.broadcasted_iota(jnp.int32, (span_len, slot_tokens), 1) < counts[c] * DH
+        weights = pieces[:, c * span_len : (c + 1) * span_len].reshape(-1, slots * DH)
+        result.append(jnp.dot(folded[c], weights, preferred_element_type=F32))
+    return result
+
+
+def scratch(spans, tokens, order, ranges, product, pieces):
+    return [
+        pltpu.VMEM((spans, 4 * DH, 2 * len(order) * tokens // spans), BF),
+        pltpu.VMEM((2, product.shape[0]) + product.shape[2:], BF),
+        pltpu.VMEM((len(pieces),) + pieces[0].shape, BF),
+        pltpu.SemaphoreType.DMA((len(pieces) + 2 * len(ranges),)),
+    ]
+
+
+def begin_kernel(part, order, ranges, product, *refs):
+    out, folded, held, pieces, sems = refs[-5:]
+    for c, both in enumerate(
+        project(part, order, ranges, product, refs[:-5], folded, held, pieces, sems)
+    ):
+        out[c] = both
+
+
+def begin(spans, tokens, part, order, ranges, product, pieces):
+    pieces = [pltpu.with_memory_space_constraint(w, pltpu.HBM) for w in pieces]
+    return pl.pallas_call(
+        functools.partial(begin_kernel, part, order, ranges),
+        out_shape=jax.ShapeDtypeStruct((spans, 4 * DH, pieces[0].shape[1]), F32),
+        in_specs=[HBM] * (1 + len(pieces)),
+        out_specs=VMEM,
+        scratch_shapes=scratch(spans, tokens, order, ranges, product, pieces),
+        compiler_params=params(),
+    )(product, *pieces)
+
+
+def decode_kernel(part, order, ranges, counts, query, early, product, *refs):
+    out, send, folded, held, pieces, sems = refs[-6:]
+    spans = folded.shape[0]
+    span_len = query.shape[0] // spans
+    late = project(part, order, ranges, product, refs[:-6], folded, held, pieces, sems)
+    for c in range(spans):
+        both = (early[c] + late[c]).astype(BF)
+        usable = lax.broadcasted_iota(jnp.int32, (span_len, both.shape[1]), 1) < counts[c] * DH
         for h in range(2):
             at = slice(c * span_len, (c + 1) * span_len)
             keys = both[h * DH : (h + 1) * DH]
@@ -214,24 +261,19 @@
     send[...] = out[...]
 
 
-def decode(place, counts, query, product, pieces, order):
+def decode(part, order, ranges, counts, query, early, product, pieces):
     tokens, width = query.shape
     spans = counts.shape[0]
-    part = product.shape[2] // len(order)
+    pieces = [pltpu.with_memory_space_constraint(w, pltpu.HBM) for w in pieces]
     shape = jax.ShapeDtypeStruct((tokens, width), BF)
     return pl.pallas_call(
-        functools.partial(decode_kernel, part, order),
+        functools.partial(decode_kernel, part, order, ranges),
         out_shape=(shape, shape),
-        in_specs=[SMEM, SMEM, VMEM, ANY] + [HBM] * len(pieces),
+        in_specs=[SMEM, VMEM, VMEM] + [HBM] * (1 + len(pieces)),
         out_specs=(VMEM, VMEM),
-        scratch_shapes=[
-            pltpu.VMEM((spans, 4 * DH, 2 * len(order) * tokens // spans), BF),
-            pltpu.VMEM((2, product.shape[0]) + product.shape[2:], BF),
-            pltpu.VMEM((len(pieces),) + pieces[0].shape, BF),
-            pltpu.SemaphoreType.DMA((2 + len(pieces),)),
-        ],
-        compiler_params=params(),
-    )(place, counts, query, product, *pieces)
+        scratch_shapes=scratch(spans, tokens, order, ranges, product, pieces),
+        compiler_params=params(),
+    )(counts, query, early, product, *pieces)
 
 
 def partial_kernel(place, attended, near, grad, near_grad, out):
@@ -344,10 +386,28 @@
         up.append([shift(w, "mp", -1) for w in up[-1]])
         down.append([shift(w, "mp", 1) for w in down[-1]])
     last = [shift(up[3][0], "mp", -1), shift(down[3][1], "mp", 1)]
-    pieces = [w0, w1] + [w for step in zip(up[1:], down[1:]) for side in step for w in side]
-    order = (0, 1, groups - 1, 2, groups - 2, 3, groups - 3, 4)
-    pieces = [pltpu.with_memory_space_constraint(w, pltpu.HBM) for w in pieces + last]
-    attended, send = decode(place, nbr_count, dec_query, product, pieces, order)
+    pieces = [[w0, w1]] + [side for step in zip(up[1:], down[1:]) for side in step] + [last]
+    pieces = [w for pair in pieces for w in pair]
+    tokens = dec_query.shape[0]
+    early = begin(
+        spans,
+        tokens,
+        part,
+        (0, 1, groups - 1, 2, groups - 2),
+        ((0, 3), (groups - 2, groups)),
+        product,
+        pieces[:10],
+    )
+    attended, send = decode(
+        part,
+        (3, groups - 3, 4),
+        ((3, groups - 2),),
+        nbr_count,
+        dec_query,
+        early,
+        product,
+        pieces[10:],
+    )
 
     near = sibling(send)
     parts = partial_grad(place, send, near, grad_out, grad_near, chips)

time: 137 us -> 135 us (0.985)
  waiting for transfers between devices: 19.9 us -> 17.7 us
  Pallas kernels: 19.4 us -> 20.8 us
    ppermute x21, waiting for transfers between devices: 12.1 us -> 7.43 us  [shift(): return lax.ppermute(x, axis, [(i, (i + step) % n) for i in range(n)])]
    all_to_all x3, waiting for transfers between devices: 6.82 us -> 9.37 us  [exchange(): return lax.all_to_all(x, SEQ, split_axis=0, concat_axis=0, tiled=True)]
    pallas_call x1 -> x2, Pallas kernels: 6.96 us -> 8.41 us  [the longest x1 4.78 us: decode(): pl.pallas_call(functools.partial(decode_kernel, part, order, ranges), out...]
    unnamed x60 -> x46, local copies, waits for them, and re-layouts: 6.67 us -> 5.33 us
  transfers between devices with their start and end apart: 26 -> 26, of which waited for: 10 -> 10; matrix products, arithmetic and copies ran while one was open for 3% -> 4% of each run, Pallas kernels for 4% -> 7%
where the time goes in v5:
time: 135 us; the launch traced here: 134 us
  starting transfers between devices  65.2 us (48%)
  blocking collectives  23.4 us (17%)
  Pallas kernels  20.8 us (15%)
  waiting for transfers between devices  17.7 us (13%)
  local copies, waits for them, and re-layouts  5.35 us (4%)
    ppermute x21, starting transfers between devices, shift(): return lax.ppermute(x, axis, [(i, (i + step) % n) for i in range(n)])  37.7 us
    all_to_all x3, starting transfers between devices, exchange(): return lax.all_to_all(x, SEQ, split_axis=0, concat_axis=0, tiled=True)  23.6 us
    all_to_all x1, blocking collectives, exchange_over(): return lax.all_to_all(x, axis, split_axis=0, concat_axis=0, tiled=True)  23.4 us
    all_to_all x3, waiting for transfers between devices, exchange(): return lax.all_to_all(x, SEQ, split_axis=0, concat_axis=0, tiled=True)  9.37 us
    ppermute x21, waiting for transfers between devices, shift(): return lax.ppermute(x, axis, [(i, (i + step) % n) for i in range(n)])  7.43 us
    unnamed x46, local copies, waits for them, and re-layouts  5.33 us
    pallas_call x1, Pallas kernels, decode(): pl.pallas_call(functools.partial(decode_kernel, part, order, ranges), out...  4.78 us
    ppermute x2, starting transfers between devices, sibling(): return lax.ppermute(x, 'core', [(0, 1), (1, 0)])  3.97 us
  transfers between devices with their start and end apart: 26, of which 10 were waited for; matrix products, arithmetic and copies ran while one was open for 4% of the time, Pallas kernels for 7%

profile of v5, /device:TPU:1, one launch (start us, length us, event | category | flops | bytes accessed | tf_op | source)
XLA Modules:
  0.0 134.3 jit_solution(847094487434985092)
XLA Ops:
  0.7 1.7 %shard_map.104 = s32[32,1,1]{2,1,0:T(1,128)} custom-call(s32[2,4]{1,0:T(2,128)} %index.3), custom_call_target="tpu_custom_call" | custom-call | tf_op jit(solution)/shard_map/pallas_call | solution.py:36
  2.3 8.6 %all-to-all-start = ((s32[32,1,1]{2,1,0:T(1,128)}), s32[32,1,1]{2,1,0:T(1,128)S(1)}, u32[]{:S(2)}, u32[]{:S(2)}) async-start(s32[32,1,1]{2,1,0:T(1,128)} %shard_map.104), calls=%async_computation | async-start | bytes 32768 | tf_op jit(solution)/shard_map/all_to_all | solution.py:337
  11.0 6.8 %all-to-all-done.tags = s32[32,1,1]{2,1,0:T(1,128)S(1)} async-done(((s32[32,1,1]{2,1,0:T(1,128)}), s32[32,1,1]{2,1,0:T(1,128)S(1)}, u32[]{:S(2)}, u32[]{:S(2)}) %all-to-all-start) | async-done | bytes 160 | tf_op jit(solution)/shard_map/all_to_all | solution.py:337
  18.4 2.2 %shard_map.105 = bf16[32,128,256]{2,1,0:T(8,128)(2,1)} custom-call(s32[32,1,1]{2,1,0:T(1,128)} %copy-done.21, bf16[8,128,256]{2,1,0:T(8,128)(2,1)} %query.2), custom_call_target="tpu_custom_call" | custom-call | tf_op jit(solution)/shard_map/pallas_call | solution.py:104
  20.6 5.0 %all-to-all-start.1 = ((bf16[32,128,256]{2,1,0:T(8,128)(2,1)}), bf16[32,128,256]{2,1,0:T(8,128)(2,1)}, u32[]{:S(2)}, u32[]{:S(2)}) async-start(bf16[32,128,256]{2,1,0:T(8,128)(2,1)} %shard_map.105), calls=%async_computation.1 | async-start | bytes 4194304 | tf_op jit(solution)/shard_map/all_to_all | solution.py:337
  26.1 5.6 %collective-permute-start = (bf16[16,4096]{1,0:T(8,128)(2,1)S(1)}, bf16[16,4096]{1,0:T(8,128)(2,1)S(1)}, u32[]{:S(2)}, u32[]{:S(2)}) collective-permute-start(bf16[16,4096]{1,0:T(8,128)(2,1)S(1)} %constant_dynamic-slice_fusion.refs_0_), channel_id=1, source_target_pairs={{0,7},{1,0},{2,1},{3,2},{4,3},{5,4},{6,5},{7,6},{8,15},{9,8},{10,9... | collective-permute-start | bytes 393224 | tf_op jit(solution)/shard_map/ppermute | solution.py:325
  31.7 2.8 %collective-permute-done.refs_1_ = bf16[16,4096]{1,0:T(8,128)(2,1)S(1)} collective-permute-done((bf16[16,4096]{1,0:T(8,128)(2,1)S(1)}, bf16[16,4096]{1,0:T(8,128)(2,1)S(1)}, u32[]{:S(2)}, u32[]{:S(2)}) %collective-permute-start) | collective-permute-done | bytes 131104 | tf_op jit(solution)/shard_map/ppermute | solution.py:325
  34.5 3.5 %collective-permute-start.1 = (bf16[16,4096]{1,0:T(8,128)(2,1)S(1)}, bf16[16,4096]{1,0:T(8,128)(2,1)S(1)}, u32[]{:S(2)}, u32[]{:S(2)}) collective-permute-start(bf16[16,4096]{1,0:T(8,128)(2,1)S(1)} %collective-permute-done.refs_1_), channel_id=1, source_target_pairs={{0,7},{1,0},{2,1},{3,2},{4,3},{5,4},{6,5},{7,6},{8,15},{9,8},{10,9... | collective-permute-start | bytes 393224 | tf_op jit(solution)/shard_map/ppermute | solution.py:325
  38.1 1.9 %collective-permute-done.1.refs_2_ = bf16[16,4096]{1,0:T(8,128)(2,1)S(1)} collective-permute-done((bf16[16,4096]{1,0:T(8,128)(2,1)S(1)}, bf16[16,4096]{1,0:T(8,128)(2,1)S(1)}, u32[]{:S(2)}, u32[]{:S(2)}) %collective-permute-start.1) | collective-permute-done | bytes 131104 | tf_op jit(solution)/shard_map/ppermute | solution.py:325
  40.0 3.6 %collective-permute-start.2 = (bf16[16,4096]{1,0:T(8,128)(2,1)S(1)}, bf16[16,4096]{1,0:T(8,128)(2,1)}, u32[]{:S(2)}, u32[]{:S(2)}) collective-permute-start(bf16[16,4096]{1,0:T(8,128)(2,1)S(1)} %collective-permute-done.1.refs_2_), channel_id=1, source_target_pairs={{0,7},{1,0},{2,1},{3,2},{4,3},{5,4},{6,5},{7,6},{8,15},{9,8},{10,9... | collective-permute-start | bytes 393224 | tf_op jit(solution)/shard_map/ppermute | solution.py:325
  43.7 3.0 %copy.14 = bf16[512,8,2,256]{3,1,2,0:T(8,128)(2,1)S(1)} copy(bf16[512,8,2,256]{3,2,1,0:T(2,128)(2,1)} %bitcast.13) | data formatting | bytes 8388608
  46.9 2.7 %collective-permute-start.3 = (bf16[16,4096]{1,0:T(8,128)(2,1)}, bf16[16,4096]{1,0:T(8,128)(2,1)S(1)}, u32[]{:S(2)}, u32[]{:S(2)}) collective-permute-start(bf16[16,4096]{1,0:T(8,128)(2,1)} %collective-permute-done.2.refs_3_), channel_id=1, source_target_pairs={{0,7},{1,0},{2,1},{3,2},{4,3},{5,4},{6,5},{7,6},{8,15},{9,8},{10,9... | collective-permute-start | bytes 393224 | tf_op jit(solution)/shard_map/ppermute | solution.py:325
  50.3 0.9 copy.13
  51.2 0.9 collective-permute-done.6.refs_5_
  52.8 3.9 %shard_map.106 = bf16[32,128,256]{2,1,0:T(8,128)(2,1)} custom-call(s32[2]{0:T(128)S(1)} %pad_add_fusion.place, bf16[4096,512]{1,0:T(8,128)(2,1)S(1)} %bitcast.11, bf16[16,4096]{1,0:T(8,128)(2,1)} %copy-done.9, bf16[16,4096]{1,0:T(8,128)(2,1)} %copy-done.16, bf16[16,4096]{1,0:T(8,128)(2,1)} %copy-done.18, bf16[16,4096]{1,0:T(8,128)(2,1)} %collective-permute-done.2.refs_3_, ...), custom_call_target="tpu_custom_call" | custom-call | tf_op jit(solution)/shard_map/pallas_call | solution.py:70
  56.7 10.0 %all-to-all-start.2 = ((bf16[32,128,256]{2,1,0:T(8,128)(2,1)}), bf16[32,128,256]{2,1,0:T(8,128)(2,1)}, u32[]{:S(2)}, u32[]{:S(2)}) async-start(bf16[32,128,256]{2,1,0:T(8,128)(2,1)} %shard_map.106), calls=%async_computation.2 | async-start | bytes 4194304 | tf_op jit(solution)/shard_map/all_to_all | solution.py:337
  66.8 2.1 %shard_map.107 = (bf16[160,512]{1,0:T(8,128)(2,1)S(1)}, bf16[160,512]{1,0:T(8,128)(2,1)S(1)}) custom-call(s32[2,4]{1,0:T(2,128)S(1)} %copy-done.5, bf16[32,128,256]{2,1,0:T(8,128)(2,1)} %all-to-all-done.1.inbox, bf16[128,512]{1,0:T(8,128)(2,1)S(1)} %fusion.pairs), custom_call_target="tpu_custom_call" | custom-call | tf_op jit(solution)/shard_map/pallas_call | solution.py:148
  69.0 3.0 %collective-permute-start.8 = (bf16[160,512]{1,0:T(8,128)(2,1)S(1)}, bf16[160,512]{1,0:T(8,128)(2,1)S(1)}, u32[]{:S(2)}, u32[]{:S(2)}) collective-permute-start(bf16[160,512]{1,0:T(8,128)(2,1)S(1)} %get-tuple-element.25.refs_0_), channel_id=1, source_target_pairs={{0,7},{1,0},{2,1},{3,2},{4,3},{5,4},{6,5},{7,6},{8,15},{9,8},{10,9... | collective-permute-start | bytes 491528 | tf_op jit(solution)/shard_map/ppermute | solution.py:325
  71.9 2.7 %collective-permute-start.9 = (bf16[160,512]{1,0:T(8,128)(2,1)S(1)}, bf16[160,512]{1,0:T(8,128)(2,1)S(1)}, u32[]{:S(2)}, u32[]{:S(2)}) collective-permute-start(bf16[160,512]{1,0:T(8,128)(2,1)S(1)} %get-tuple-element.26.refs_1_), channel_id=1, source_target_pairs={{0,7},{1,0},{2,1},{3,2},{4,3},{5,4},{6,5},{7,6},{8,15},{9,8},{10,9... | collective-permute-start | bytes 491528 | tf_op jit(solution)/shard_map/ppermute | solution.py:325
  75.2 3.5 %collective-permute-start.12 = (bf16[160,512]{1,0:T(8,128)(2,1)S(1)}, bf16[160,512]{1,0:T(8,128)(2,1)S(1)}, u32[]{:S(2)}, u32[]{:S(2)}) collective-permute-start(bf16[160,512]{1,0:T(8,128)(2,1)S(1)} %collective-permute-done.8.refs_2_), channel_id=1, source_target_pairs={{0,7},{1,0},{2,1},{3,2},{4,3},{5,4},{6,5},{7,6},{8,15},{9,8},{10,9... | collective-permute-start | bytes 491528 | tf_op jit(solution)/shard_map/ppermute | solution.py:325
  78.8 3.5 %collective-permute-start.13 = (bf16[160,512]{1,0:T(8,128)(2,1)S(1)}, bf16[160,512]{1,0:T(8,128)(2,1)}, u32[]{:S(2)}, u32[]{:S(2)}) collective-permute-start(bf16[160,512]{1,0:T(8,128)(2,1)S(1)} %collective-permute-done.9.refs_3_), channel_id=1, source_target_pairs={{0,7},{1,0},{2,1},{3,2},{4,3},{5,4},{6,5},{7,6},{8,15},{9,8},{10,9... | collective-permute-start | bytes 491528 | tf_op jit(solution)/shard_map/ppermute | solution.py:325
  82.4 2.7 %collective-permute-start.16 = (bf16[160,512]{1,0:T(8,128)(2,1)S(1)}, bf16[160,512]{1,0:T(8,128)(2,1)}, u32[]{:S(2)}, u32[]{:S(2)}) collective-permute-start(bf16[160,512]{1,0:T(8,128)(2,1)S(1)} %collective-permute-done.12.refs_6_), channel_id=1, source_target_pairs={{0,7},{1,0},{2,1},{3,2},{4,3},{5,4},{6,5},{7,6},{8,15},{9,8},{10,9... | collective-permute-start | bytes 491528 | tf_op jit(solution)/shard_map/ppermute | solution.py:325
  85.2 3.5 %collective-permute-start.17 = (bf16[160,512]{1,0:T(8,128)(2,1)}, bf16[160,512]{1,0:T(8,128)(2,1)}, u32[]{:S(2)}, u32[]{:S(2)}) collective-permute-start(bf16[160,512]{1,0:T(8,128)(2,1)} %collective-permute-done.13.refs_7_), channel_id=1, source_target_pairs={{0,7},{1,0},{2,1},{3,2},{4,3},{5,4},{6,5},{7,6},{8,15},{9,8},{10,9... | collective-permute-start | bytes 491528 | tf_op jit(solution)/shard_map/ppermute | solution.py:325
  88.9 3.1 %collective-permute-start.20 = (bf16[160,512]{1,0:T(8,128)(2,1)}, bf16[160,512]{1,0:T(8,128)(2,1)}, u32[]{:S(2)}, u32[]{:S(2)}) collective-permute-start(bf16[160,512]{1,0:T(8,128)(2,1)} %collective-permute-done.16.refs_0_), channel_id=1, source_target_pairs={{0,7},{1,0},{2,1},{3,2},{4,3},{5,4},{6,5},{7,6},{8,15},{9,8},{10,9... | collective-permute-start | bytes 491528 | tf_op jit(solution)/shard_map/ppermute | solution.py:325
  92.1 2.6 %all-to-all-done.2 = bf16[32,128,256]{2,1,0:T(8,128)(2,1)} async-done(((bf16[32,128,256]{2,1,0:T(8,128)(2,1)}), bf16[32,128,256]{2,1,0:T(8,128)(2,1)}, u32[]{:S(2)}, u32[]{:S(2)}) %all-to-all-start.2) | async-done | bytes 2097184 | tf_op jit(solution)/shard_map/all_to_all | solution.py:337
  94.7 3.6 %shard_map.108.early = f32[2,512,512]{2,1,0:T(8,128)S(1)} custom-call(bf16[16,2,128,256]{3,2,1,0:T(8,128)(2,1)} %bitcast.3.product, bf16[160,512]{1,0:T(8,128)(2,1)} %copy-done.2, bf16[160,512]{1,0:T(8,128)(2,1)} %copy-done.3, bf16[160,512]{1,0:T(8,128)(2,1)} %copy-done.10, bf16[160,512]{1,0:T(8,128)(2,1)} %copy-done.12, bf16[160,512]{1,0:T(8,128)(2,1)} %copy-done.13, ...), custom_call_target="tpu_custom_call" | custom-call | tf_op jit(solution)/shard_map/pallas_call | solution.py:231
  98.3 0.9 collective-permute-done.21.refs_5_
  99.2 4.8 %shard_map.109 = (bf16[128,256]{1,0:T(8,128)(2,1)}, bf16[128,256]{1,0:T(8,128)(2,1)S(1)}) custom-call(s32[2]{0:T(128)S(1)} %copy-done.6, bf16[128,256]{1,0:T(8,128)(2,1)S(1)} %copy-done.4, f32[2,512,512]{2,1,0:T(8,128)S(1)} %shard_map.108.early, bf16[16,2,128,256]{3,2,1,0:T(8,128)(2,1)} %bitcast.3.product, bf16[160,512]{1,0:T(8,128)(2,1)} %collective-permute-done.16.refs_0_, ...), custom_call_target="tpu_custom_call" | custom-call | tf_op jit(solution)/shard_map/pallas_call | solution.py:269
  104.0 3.5 %collective-permute-start.22 = (bf16[128,256]{1,0:T(8,128)(2,1)S(1)}, bf16[128,256]{1,0:T(8,128)(2,1)S(1)}, u32[]{:S(2)}, u32[]{:S(2)}) collective-permute-start(bf16[128,256]{1,0:T(8,128)(2,1)S(1)} %get-tuple-element.28.attended), channel_id=1, source_target_pairs={{0,8},{8,0},{1,9},{9,1},{2,10},{10,2},{3,11},{11,3},{4,12},{12,4},... | collective-permute-start | bytes 196616 | tf_op jit(solution)/shard_map/ppermute | solution.py:329
  107.5 0.9 collective-permute-done.22.near
  108.4 1.7 %shard_map.110 = bf16[16,256,128]{2,1,0:T(8,128)(2,1)S(1)} custom-call(s32[2]{0:T(128)S(1)} %pad_add_fusion.place, bf16[128,256]{1,0:T(8,128)(2,1)S(1)} %get-tuple-element.28.attended, bf16[128,256]{1,0:T(8,128)(2,1)S(1)} %collective-permute-done.22.near, bf16[128,4096]{1,0:T(8,128)(2,1)S(1)} %copy-done.1, bf16[128,4096]{1,0:T(8,128)(2,1)} %collective-permute-done.7.near_grad), custom_call_target="tpu_custom_call" | custom-call | tf_op jit(solution)/shard_map/pallas_call | solution.py:295
  110.1 23.4 %all_to_all.20.parts = bf16[16,256,128]{2,1,0:T(8,128)(2,1)S(1)} all-to-all(bf16[16,256,128]{2,1,0:T(8,128)(2,1)S(1)} %shard_map.110), channel_id=1, replica_groups=mesh['chip'=16,'core'=2,'mp'=8] {'chip'}, dimensions={0} | all-to-all | bytes 2097152 | tf_op jit(solution)/shard_map/all_to_all | solution.py:333
  (78 shorter events, 4.8 us)
Async XLA Ops:
  0.6 24.9 %copy-start.1 = (bf16[128,4096]{1,0:T(8,128)(2,1)S(1)}, bf16[128,4096]{1,0:T(8,128)(2,1)}, u32[]{:S(2)}) copy-start(bf16[128,4096]{1,0:T(8,128)(2,1)} %grad.1) | copy-start | bytes 3145732
  2.3 15.5 %all-to-all-start = ((s32[32,1,1]{2,1,0:T(1,128)}), s32[32,1,1]{2,1,0:T(1,128)S(1)}, u32[]{:S(2)}, u32[]{:S(2)}) async-start(s32[32,1,1]{2,1,0:T(1,128)} %shard_map.104), calls=%async_computation | async-start | bytes 32768 | tf_op jit(solution)/shard_map/all_to_all | solution.py:337
  11.0 35.7 %copy-start.9 = (bf16[16,4096]{1,0:T(8,128)(2,1)}, bf16[16,4096]{1,0:T(8,128)(2,1)S(1)}, u32[]{:S(2)}) copy-start(bf16[16,4096]{1,0:T(8,128)(2,1)S(1)} %constant_dynamic-slice_fusion.refs_0_) | copy-start | bytes 393220
  20.6 36.1 %all-to-all-start.1 = ((bf16[32,128,256]{2,1,0:T(8,128)(2,1)}), bf16[32,128,256]{2,1,0:T(8,128)(2,1)}, u32[]{:S(2)}, u32[]{:S(2)}) async-start(bf16[32,128,256]{2,1,0:T(8,128)(2,1)} %shard_map.105), calls=%async_computation.1 | async-start | bytes 4194304 | tf_op jit(solution)/shard_map/all_to_all | solution.py:337
  25.6 31.2 %collective-permute-start.7 = (bf16[128,4096]{1,0:T(8,128)(2,1)S(1)}, bf16[128,4096]{1,0:T(8,128)(2,1)}, u32[]{:S(2)}, u32[]{:S(2)}) collective-permute-start(bf16[128,4096]{1,0:T(8,128)(2,1)S(1)} %copy-done.1), channel_id=1, source_target_pairs={{0,8},{8,0},{1,9},{9,1},{2,10},{10,2},{3,11},{11,3},{4,12},{12,4},... | collective-permute-start | bytes 3145736 | tf_op jit(solution)/shard_map/ppermute | solution.py:329
  26.1 8.4 %collective-permute-start = (bf16[16,4096]{1,0:T(8,128)(2,1)S(1)}, bf16[16,4096]{1,0:T(8,128)(2,1)S(1)}, u32[]{:S(2)}, u32[]{:S(2)}) collective-permute-start(bf16[16,4096]{1,0:T(8,128)(2,1)S(1)} %constant_dynamic-slice_fusion.refs_0_), channel_id=1, source_target_pairs={{0,7},{1,0},{2,1},{3,2},{4,3},{5,4},{6,5},{7,6},{8,15},{9,8},{10,9... | collective-permute-start | bytes 393224 | tf_op jit(solution)/shard_map/ppermute | solution.py:325
  31.7 6.4 %collective-permute-start.4 = (bf16[16,4096]{1,0:T(8,128)(2,1)S(1)}, bf16[16,4096]{1,0:T(8,128)(2,1)S(1)}, u32[]{:S(2)}, u32[]{:S(2)}) collective-permute-start(bf16[16,4096]{1,0:T(8,128)(2,1)S(1)} %constant_dynamic-slice_fusion.refs_0_), channel_id=1, source_target_pairs={{0,1},{1,2},{2,3},{3,4},{4,5},{5,6},{6,7},{7,0},{8,9},{9,10},{10,1... | collective-permute-start | bytes 393224 | tf_op jit(solution)/shard_map/ppermute | solution.py:325
  34.5 5.5 %collective-permute-start.1 = (bf16[16,4096]{1,0:T(8,128)(2,1)S(1)}, bf16[16,4096]{1,0:T(8,128)(2,1)S(1)}, u32[]{:S(2)}, u32[]{:S(2)}) collective-permute-start(bf16[16,4096]{1,0:T(8,128)(2,1)S(1)} %collective-permute-done.refs_1_), channel_id=1, source_target_pairs={{0,7},{1,0},{2,1},{3,2},{4,3},{5,4},{6,5},{7,6},{8,15},{9,8},{10,9... | collective-permute-start | bytes 393224 | tf_op jit(solution)/shard_map/ppermute | solution.py:325
  38.0 8.7 %collective-permute-start.5 = (bf16[16,4096]{1,0:T(8,128)(2,1)S(1)}, bf16[16,4096]{1,0:T(8,128)(2,1)}, u32[]{:S(2)}, u32[]{:S(2)}) collective-permute-start(bf16[16,4096]{1,0:T(8,128)(2,1)S(1)} %collective-permute-done.4.refs_7_), channel_id=1, source_target_pairs={{0,1},{1,2},{2,3},{3,4},{4,5},{5,6},{6,7},{7,0},{8,9},{9,10},{10,1... | collective-permute-start | bytes 393224 | tf_op jit(solution)/shard_map/ppermute | solution.py:325
  40.0 6.9 %collective-permute-start.2 = (bf16[16,4096]{1,0:T(8,128)(2,1)S(1)}, bf16[16,4096]{1,0:T(8,128)(2,1)}, u32[]{:S(2)}, u32[]{:S(2)}) collective-permute-start(bf16[16,4096]{1,0:T(8,128)(2,1)S(1)} %collective-permute-done.1.refs_2_), channel_id=1, source_target_pairs={{0,7},{1,0},{2,1},{3,2},{4,3},{5,4},{6,5},{7,6},{8,15},{9,8},{10,9... | collective-permute-start | bytes 393224 | tf_op jit(solution)/shard_map/ppermute | solution.py:325
  46.8 5.3 %collective-permute-start.6 = (bf16[16,4096]{1,0:T(8,128)(2,1)}, bf16[16,4096]{1,0:T(8,128)(2,1)S(1)}, u32[]{:S(2)}, u32[]{:S(2)}) collective-permute-start(bf16[16,4096]{1,0:T(8,128)(2,1)} %collective-permute-done.5.refs_6_), channel_id=1, source_target_pairs={{0,1},{1,2},{2,3},{3,4},{4,5},{5,6},{6,7},{7,0},{8,9},{9,10},{10,1... | collective-permute-start | bytes 393224 | tf_op jit(solution)/shard_map/ppermute | solution.py:325
  46.9 5.2 %collective-permute-start.3 = (bf16[16,4096]{1,0:T(8,128)(2,1)}, bf16[16,4096]{1,0:T(8,128)(2,1)S(1)}, u32[]{:S(2)}, u32[]{:S(2)}) collective-permute-start(bf16[16,4096]{1,0:T(8,128)(2,1)} %collective-permute-done.2.refs_3_), channel_id=1, source_target_pairs={{0,7},{1,0},{2,1},{3,2},{4,3},{5,4},{6,5},{7,6},{8,15},{9,8},{10,9... | collective-permute-start | bytes 393224 | tf_op jit(solution)/shard_map/ppermute | solution.py:325
  56.7 37.9 %all-to-all-start.2 = ((bf16[32,128,256]{2,1,0:T(8,128)(2,1)}), bf16[32,128,256]{2,1,0:T(8,128)(2,1)}, u32[]{:S(2)}, u32[]{:S(2)}) async-start(bf16[32,128,256]{2,1,0:T(8,128)(2,1)} %shard_map.106), calls=%async_computation.2 | async-start | bytes 4194304 | tf_op jit(solution)/shard_map/all_to_all | solution.py:337
  66.8 32.4 %copy-start.4 = (bf16[128,256]{1,0:T(8,128)(2,1)S(1)}, bf16[128,256]{1,0:T(8,128)(2,1)}, u32[]{:S(2)}) copy-start(bf16[128,256]{1,0:T(8,128)(2,1)} %query.3) | copy-start | bytes 196612
  66.8 32.4 %copy-start.6 = (s32[2]{0:T(128)S(1)}, s32[2]{0:T(128)}, u32[]{:S(2)}) copy-start(s32[2]{0:T(128)} %counts.1) | copy-start | bytes 28
  69.0 25.7 %copy-start.2 = (bf16[160,512]{1,0:T(8,128)(2,1)}, bf16[160,512]{1,0:T(8,128)(2,1)S(1)}, u32[]{:S(2)}) copy-start(bf16[160,512]{1,0:T(8,128)(2,1)S(1)} %get-tuple-element.25.refs_0_) | copy-start | bytes 491524
  69.0 6.2 %collective-permute-start.8 = (bf16[160,512]{1,0:T(8,128)(2,1)S(1)}, bf16[160,512]{1,0:T(8,128)(2,1)S(1)}, u32[]{:S(2)}, u32[]{:S(2)}) collective-permute-start(bf16[160,512]{1,0:T(8,128)(2,1)S(1)} %get-tuple-element.25.refs_0_), channel_id=1, source_target_pairs={{0,7},{1,0},{2,1},{3,2},{4,3},{5,4},{6,5},{7,6},{8,15},{9,8},{10,9... | collective-permute-start | bytes 491528 | tf_op jit(solution)/shard_map/ppermute | solution.py:325
  71.9 6.8 %collective-permute-start.11 = (bf16[160,512]{1,0:T(8,128)(2,1)S(1)}, bf16[160,512]{1,0:T(8,128)(2,1)S(1)}, u32[]{:S(2)}, u32[]{:S(2)}) collective-permute-start(bf16[160,512]{1,0:T(8,128)(2,1)S(1)} %get-tuple-element.26.refs_1_), channel_id=1, source_target_pairs={{0,1},{1,2},{2,3},{3,4},{4,5},{5,6},{6,7},{7,0},{8,9},{9,10},{10,1... | collective-permute-start | bytes 491528 | tf_op jit(solution)/shard_map/ppermute | solution.py:325
  71.9 6.8 %collective-permute-start.9 = (bf16[160,512]{1,0:T(8,128)(2,1)S(1)}, bf16[160,512]{1,0:T(8,128)(2,1)S(1)}, u32[]{:S(2)}, u32[]{:S(2)}) collective-permute-start(bf16[160,512]{1,0:T(8,128)(2,1)S(1)} %get-tuple-element.26.refs_1_), channel_id=1, source_target_pairs={{0,7},{1,0},{2,1},{3,2},{4,3},{5,4},{6,5},{7,6},{8,15},{9,8},{10,9... | collective-permute-start | bytes 491528 | tf_op jit(solution)/shard_map/ppermute | solution.py:325
  74.6 7.6 %collective-permute-start.10 = (bf16[160,512]{1,0:T(8,128)(2,1)S(1)}, bf16[160,512]{1,0:T(8,128)(2,1)S(1)}, u32[]{:S(2)}, u32[]{:S(2)}) collective-permute-start(bf16[160,512]{1,0:T(8,128)(2,1)S(1)} %get-tuple-element.25.refs_0_), channel_id=1, source_target_pairs={{0,1},{1,2},{2,3},{3,4},{4,5},{5,6},{6,7},{7,0},{8,9},{9,10},{10,1... | collective-permute-start | bytes 491528 | tf_op jit(solution)/shard_map/ppermute | solution.py:325
  75.2 19.5 %copy-start.10 = (bf16[160,512]{1,0:T(8,128)(2,1)}, bf16[160,512]{1,0:T(8,128)(2,1)S(1)}, u32[]{:S(2)}) copy-start(bf16[160,512]{1,0:T(8,128)(2,1)S(1)} %collective-permute-done.8.refs_2_) | copy-start | bytes 491524
  75.2 7.1 %collective-permute-start.12 = (bf16[160,512]{1,0:T(8,128)(2,1)S(1)}, bf16[160,512]{1,0:T(8,128)(2,1)S(1)}, u32[]{:S(2)}, u32[]{:S(2)}) collective-permute-start(bf16[160,512]{1,0:T(8,128)(2,1)S(1)} %collective-permute-done.8.refs_2_), channel_id=1, source_target_pairs={{0,7},{1,0},{2,1},{3,2},{4,3},{5,4},{6,5},{7,6},{8,15},{9,8},{10,9... | collective-permute-start | bytes 491528 | tf_op jit(solution)/shard_map/ppermute | solution.py:325
  78.7 6.3 %collective-permute-start.15 = (bf16[160,512]{1,0:T(8,128)(2,1)S(1)}, bf16[160,512]{1,0:T(8,128)(2,1)S(1)}, u32[]{:S(2)}, u32[]{:S(2)}) collective-permute-start(bf16[160,512]{1,0:T(8,128)(2,1)S(1)} %collective-permute-done.11.refs_5_), channel_id=1, source_target_pairs={{0,1},{1,2},{2,3},{3,4},{4,5},{5,6},{6,7},{7,0},{8,9},{9,10},{10,1... | collective-permute-start | bytes 491528 | tf_op jit(solution)/shard_map/ppermute | solution.py:325
  78.8 6.4 %collective-permute-start.13 = (bf16[160,512]{1,0:T(8,128)(2,1)S(1)}, bf16[160,512]{1,0:T(8,128)(2,1)}, u32[]{:S(2)}, u32[]{:S(2)}) collective-permute-start(bf16[160,512]{1,0:T(8,128)(2,1)S(1)} %collective-permute-done.9.refs_3_), channel_id=1, source_target_pairs={{0,7},{1,0},{2,1},{3,2},{4,3},{5,4},{6,5},{7,6},{8,15},{9,8},{10,9... | collective-permute-start | bytes 491528 | tf_op jit(solution)/shard_map/ppermute | solution.py:325
  82.2 6.6 %collective-permute-start.14 = (bf16[160,512]{1,0:T(8,128)(2,1)S(1)}, bf16[160,512]{1,0:T(8,128)(2,1)}, u32[]{:S(2)}, u32[]{:S(2)}) collective-permute-start(bf16[160,512]{1,0:T(8,128)(2,1)S(1)} %collective-permute-done.10.refs_4_), channel_id=1, source_target_pairs={{0,1},{1,2},{2,3},{3,4},{4,5},{5,6},{6,7},{7,0},{8,9},{9,10},{10,1... | collective-permute-start | bytes 491528 | tf_op jit(solution)/shard_map/ppermute | solution.py:325
  82.4 6.5 %collective-permute-start.16 = (bf16[160,512]{1,0:T(8,128)(2,1)S(1)}, bf16[160,512]{1,0:T(8,128)(2,1)}, u32[]{:S(2)}, u32[]{:S(2)}) collective-permute-start(bf16[160,512]{1,0:T(8,128)(2,1)S(1)} %collective-permute-done.12.refs_6_), channel_id=1, source_target_pairs={{0,7},{1,0},{2,1},{3,2},{4,3},{5,4},{6,5},{7,6},{8,15},{9,8},{10,9... | collective-permute-start | bytes 491528 | tf_op jit(solution)/shard_map/ppermute | solution.py:325
  85.1 7.0 %collective-permute-start.19 = (bf16[160,512]{1,0:T(8,128)(2,1)S(1)}, bf16[160,512]{1,0:T(8,128)(2,1)}, u32[]{:S(2)}, u32[]{:S(2)}) collective-permute-start(bf16[160,512]{1,0:T(8,128)(2,1)S(1)} %collective-permute-done.15.refs_9_), channel_id=1, source_target_pairs={{0,1},{1,2},{2,3},{3,4},{4,5},{5,6},{6,7},{7,0},{8,9},{9,10},{10,1... | collective-permute-start | bytes 491528 | tf_op jit(solution)/shard_map/ppermute | solution.py:325
  85.2 13.1 %collective-permute-start.17 = (bf16[160,512]{1,0:T(8,128)(2,1)}, bf16[160,512]{1,0:T(8,128)(2,1)}, u32[]{:S(2)}, u32[]{:S(2)}) collective-permute-start(bf16[160,512]{1,0:T(8,128)(2,1)} %collective-permute-done.13.refs_7_), channel_id=1, source_target_pairs={{0,7},{1,0},{2,1},{3,2},{4,3},{5,4},{6,5},{7,6},{8,15},{9,8},{10,9... | collective-permute-start | bytes 491528 | tf_op jit(solution)/shard_map/ppermute | solution.py:325
  88.9 9.4 %collective-permute-start.18 = (bf16[160,512]{1,0:T(8,128)(2,1)}, bf16[160,512]{1,0:T(8,128)(2,1)}, u32[]{:S(2)}, u32[]{:S(2)}) collective-permute-start(bf16[160,512]{1,0:T(8,128)(2,1)} %collective-permute-done.14.refs_8_), channel_id=1, source_target_pairs={{0,1},{1,2},{2,3},{3,4},{4,5},{5,6},{6,7},{7,0},{8,9},{9,10},{10,1... | collective-permute-start | bytes 491528 | tf_op jit(solution)/shard_map/ppermute | solution.py:325
  88.9 9.4 %collective-permute-start.20 = (bf16[160,512]{1,0:T(8,128)(2,1)}, bf16[160,512]{1,0:T(8,128)(2,1)}, u32[]{:S(2)}, u32[]{:S(2)}) collective-permute-start(bf16[160,512]{1,0:T(8,128)(2,1)} %collective-permute-done.16.refs_0_), channel_id=1, source_target_pairs={{0,7},{1,0},{2,1},{3,2},{4,3},{5,4},{6,5},{7,6},{8,15},{9,8},{10,9... | collective-permute-start | bytes 491528 | tf_op jit(solution)/shard_map/ppermute | solution.py:325
  92.1 7.1 %collective-permute-start.21 = (bf16[160,512]{1,0:T(8,128)(2,1)}, bf16[160,512]{1,0:T(8,128)(2,1)}, u32[]{:S(2)}, u32[]{:S(2)}) collective-permute-start(bf16[160,512]{1,0:T(8,128)(2,1)} %collective-permute-done.19.refs_3_), channel_id=1, source_target_pairs={{0,1},{1,2},{2,3},{3,4},{4,5},{5,6},{6,7},{7,0},{8,9},{9,10},{10,1... | collective-permute-start | bytes 491528 | tf_op jit(solution)/shard_map/ppermute | solution.py:325
  104.0 4.4 %collective-permute-start.22 = (bf16[128,256]{1,0:T(8,128)(2,1)S(1)}, bf16[128,256]{1,0:T(8,128)(2,1)S(1)}, u32[]{:S(2)}, u32[]{:S(2)}) collective-permute-start(bf16[128,256]{1,0:T(8,128)(2,1)S(1)} %get-tuple-element.28.attended), channel_id=1, source_target_pairs={{0,8},{8,0},{1,9},{9,1},{2,10},{10,2},{3,11},{11,3},{4,12},{12,4},... | collective-permute-start | bytes 196616 | tf_op jit(solution)/shard_map/ppermute | solution.py:329
  (16 other events, 91.1 us)

commit v6 on v5

--- a/solution.py
+++ b/solution.py
@@ -44,14 +44,8 @@
 def product_kernel(place, matrix, *refs):
     pieces, (out, left, result, sems) = refs[:-4], refs[-4:]
     part = left.shape[0] // len(pieces)
-    copies = [
-        pltpu.make_async_copy(p, left.at[pl.ds(i * part, part)], sems.at[i])
-        for i, p in enumerate(pieces)
-    ]
-    for copy in copies:
-        copy.start()
-    for copy in copies:
-        copy.wait()
+    for i, p in enumerate(pieces):
+        left[i * part : (i + 1) * part] = p[...]
     first = pl.multiple_of(place[1] * 2 * DH, 2 * DH)
     right = matrix[:, pl.ds(first, 2 * DH)]
     result[...] = jnp.dot(left[...], right, preferred_element_type=F32).astype(BF)
@@ -66,11 +60,10 @@
 
 def multiply(place, matrix, pieces, copies):
     rows = len(pieces) * pieces[0].shape[0]
-    pieces = [pltpu.with_memory_space_constraint(p, pltpu.HBM) for p in pieces]
     return pl.pallas_call(
         product_kernel,
         out_shape=pltpu.HBM((copies, rows, 2 * DH), BF),
-        in_specs=[SMEM, VMEM] + [HBM] * len(pieces),
+        in_specs=[SMEM, VMEM] + [VMEM] * len(pieces),
         out_specs=HBM,
         scratch_shapes=[
             pltpu.VMEM((rows, pieces[0].shape[1]), BF),

time: 135 us -> 134 us (level)
    unnamed x46 -> x38, local copies, waits for them, and re-layouts: 5.33 us -> 4.59 us
  transfers between devices with their start and end apart: 26 -> 26, of which waited for: 10 -> 9; matrix products, arithmetic and copies ran while one was open for 4% -> 4% of each run, Pallas kernels for 7% -> 7%
where the time goes in v6:
time: 134 us; the launch traced here: 133 us
  starting transfers between devices  65.6 us (49%)
  blocking collectives  23.4 us (17%)
  Pallas kernels  20 us (15%)
  waiting for transfers between devices  17.6 us (13%)
  local copies, waits for them, and re-layouts  4.6 us (3%)
    ppermute x21, starting transfers between devices, shift(): return lax.ppermute(x, axis, [(i, (i + step) % n) for i in range(n)])  37.7 us
    all_to_all x3, starting transfers between devices, exchange(): return lax.all_to_all(x, SEQ, split_axis=0, concat_axis=0, tiled=True)  23.7 us
    all_to_all x1, blocking collectives, exchange_over(): return lax.all_to_all(x, axis, split_axis=0, concat_axis=0, tiled=True)  23.4 us
    all_to_all x3, waiting for transfers between devices, exchange(): return lax.all_to_all(x, SEQ, split_axis=0, concat_axis=0, tiled=True)  9.36 us
    ppermute x21, waiting for transfers between devices, shift(): return lax.ppermute(x, axis, [(i, (i + step) % n) for i in range(n)])  7.32 us
    pallas_call x1, Pallas kernels, decode(): pl.pallas_call(functools.partial(decode_kernel, part, order, ranges), out...  4.78 us
    unnamed x38, local copies, waits for them, and re-layouts  4.59 us
    ppermute x2, starting transfers between devices, sibling(): return lax.ppermute(x, 'core', [(0, 1), (1, 0)])  4.18 us
  transfers between devices with their start and end apart: 26, of which 9 were waited for; matrix products, arithmetic and copies ran while one was open for 4% of the time, Pallas kernels for 7%

profile of v6, /device:TPU:1, one launch (start us, length us, event | category | flops | bytes accessed | tf_op | source)
XLA Modules:
  0.0 133.1 jit_solution(13637200924198592464)
XLA Ops:
  0.7 1.7 %shard_map.104 = s32[32,1,1]{2,1,0:T(1,128)} custom-call(s32[2,4]{1,0:T(2,128)} %index.3), custom_call_target="tpu_custom_call" | custom-call | tf_op jit(solution)/shard_map/pallas_call | solution.py:36
  2.3 8.6 %all-to-all-start = ((s32[32,1,1]{2,1,0:T(1,128)}), s32[32,1,1]{2,1,0:T(1,128)S(1)}, u32[]{:S(2)}, u32[]{:S(2)}) async-start(s32[32,1,1]{2,1,0:T(1,128)} %shard_map.104), calls=%async_computation | async-start | bytes 32768 | tf_op jit(solution)/shard_map/all_to_all | solution.py:330
  11.0 6.8 %all-to-all-done.tags = s32[32,1,1]{2,1,0:T(1,128)S(1)} async-done(((s32[32,1,1]{2,1,0:T(1,128)}), s32[32,1,1]{2,1,0:T(1,128)S(1)}, u32[]{:S(2)}, u32[]{:S(2)}) %all-to-all-start) | async-done | bytes 160 | tf_op jit(solution)/shard_map/all_to_all | solution.py:330
  18.4 2.2 %shard_map.105 = bf16[32,128,256]{2,1,0:T(8,128)(2,1)} custom-call(s32[32,1,1]{2,1,0:T(1,128)} %copy-done.17, bf16[8,128,256]{2,1,0:T(8,128)(2,1)} %query.2), custom_call_target="tpu_custom_call" | custom-call | tf_op jit(solution)/shard_map/pallas_call | solution.py:97
  20.6 5.0 %all-to-all-start.1 = ((bf16[32,128,256]{2,1,0:T(8,128)(2,1)}), bf16[32,128,256]{2,1,0:T(8,128)(2,1)}, u32[]{:S(2)}, u32[]{:S(2)}) async-start(bf16[32,128,256]{2,1,0:T(8,128)(2,1)} %shard_map.105), calls=%async_computation.1 | async-start | bytes 4194304 | tf_op jit(solution)/shard_map/all_to_all | solution.py:330
  26.1 5.6 %collective-permute-start = (bf16[16,4096]{1,0:T(8,128)(2,1)S(1)}, bf16[16,4096]{1,0:T(8,128)(2,1)S(1)}, u32[]{:S(2)}, u32[]{:S(2)}) collective-permute-start(bf16[16,4096]{1,0:T(8,128)(2,1)S(1)} %constant_dynamic-slice_fusion.refs_0_), channel_id=1, source_target_pairs={{0,7},{1,0},{2,1},{3,2},{4,3},{5,4},{6,5},{7,6},{8,15},{9,8},{10,9... | collective-permute-start | bytes 393224 | tf_op jit(solution)/shard_map/ppermute | solution.py:318
  31.7 2.8 %collective-permute-done.refs_1_ = bf16[16,4096]{1,0:T(8,128)(2,1)S(1)} collective-permute-done((bf16[16,4096]{1,0:T(8,128)(2,1)S(1)}, bf16[16,4096]{1,0:T(8,128)(2,1)S(1)}, u32[]{:S(2)}, u32[]{:S(2)}) %collective-permute-start) | collective-permute-done | bytes 131104 | tf_op jit(solution)/shard_map/ppermute | solution.py:318
  34.5 3.5 %collective-permute-start.1 = (bf16[16,4096]{1,0:T(8,128)(2,1)S(1)}, bf16[16,4096]{1,0:T(8,128)(2,1)}, u32[]{:S(2)}, u32[]{:S(2)}) collective-permute-start(bf16[16,4096]{1,0:T(8,128)(2,1)S(1)} %collective-permute-done.refs_1_), channel_id=1, source_target_pairs={{0,7},{1,0},{2,1},{3,2},{4,3},{5,4},{6,5},{7,6},{8,15},{9,8},{10,9... | collective-permute-start | bytes 393224 | tf_op jit(solution)/shard_map/ppermute | solution.py:318
  38.1 1.9 %collective-permute-done.1.refs_2_ = bf16[16,4096]{1,0:T(8,128)(2,1)} collective-permute-done((bf16[16,4096]{1,0:T(8,128)(2,1)S(1)}, bf16[16,4096]{1,0:T(8,128)(2,1)}, u32[]{:S(2)}, u32[]{:S(2)}) %collective-permute-start.1) | collective-permute-done | bytes 131104 | tf_op jit(solution)/shard_map/ppermute | solution.py:318
  40.0 3.6 %collective-permute-start.2 = (bf16[16,4096]{1,0:T(8,128)(2,1)}, bf16[16,4096]{1,0:T(8,128)(2,1)}, u32[]{:S(2)}, u32[]{:S(2)}) collective-permute-start(bf16[16,4096]{1,0:T(8,128)(2,1)} %collective-permute-done.1.refs_2_), channel_id=1, source_target_pairs={{0,7},{1,0},{2,1},{3,2},{4,3},{5,4},{6,5},{7,6},{8,15},{9,8},{10,9... | collective-permute-start | bytes 393224 | tf_op jit(solution)/shard_map/ppermute | solution.py:318
  43.7 3.0 %copy.14 = bf16[512,8,2,256]{3,1,2,0:T(8,128)(2,1)S(1)} copy(bf16[512,8,2,256]{3,2,1,0:T(2,128)(2,1)} %bitcast.13) | data formatting | bytes 8388608
  46.9 2.7 %collective-permute-start.3 = (bf16[16,4096]{1,0:T(8,128)(2,1)}, bf16[16,4096]{1,0:T(8,128)(2,1)S(1)}, u32[]{:S(2)}, u32[]{:S(2)}) collective-permute-start(bf16[16,4096]{1,0:T(8,128)(2,1)} %collective-permute-done.2.refs_3_), channel_id=1, source_target_pairs={{0,7},{1,0},{2,1},{3,2},{4,3},{5,4},{6,5},{7,6},{8,15},{9,8},{10,9... | collective-permute-start | bytes 393224 | tf_op jit(solution)/shard_map/ppermute | solution.py:318
  50.3 0.9 copy.13
  51.2 0.9 collective-permute-done.6.refs_5_
  52.1 3.1 %shard_map.106 = bf16[32,128,256]{2,1,0:T(8,128)(2,1)} custom-call(s32[2]{0:T(128)S(1)} %pad_add_fusion.place, bf16[4096,512]{1,0:T(8,128)(2,1)S(1)} %bitcast.11, bf16[16,4096]{1,0:T(8,128)(2,1)S(1)} %constant_dynamic-slice_fusion.refs_0_, bf16[16,4096]{1,0:T(8,128)(2,1)S(1)} %collective-permute-done.refs_1_, ...), custom_call_target="tpu_custom_call" | custom-call | tf_op jit(solution)/shard_map/pallas_call | solution.py:63
  55.3 10.1 %all-to-all-start.2 = ((bf16[32,128,256]{2,1,0:T(8,128)(2,1)}), bf16[32,128,256]{2,1,0:T(8,128)(2,1)}, u32[]{:S(2)}, u32[]{:S(2)}) async-start(bf16[32,128,256]{2,1,0:T(8,128)(2,1)} %shard_map.106), calls=%async_computation.2 | async-start | bytes 4194304 | tf_op jit(solution)/shard_map/all_to_all | solution.py:330
  65.4 2.1 %shard_map.107 = (bf16[160,512]{1,0:T(8,128)(2,1)S(1)}, bf16[160,512]{1,0:T(8,128)(2,1)S(1)}) custom-call(s32[2,4]{1,0:T(2,128)S(1)} %copy-done.7, bf16[32,128,256]{2,1,0:T(8,128)(2,1)} %all-to-all-done.1.inbox, bf16[128,512]{1,0:T(8,128)(2,1)S(1)} %fusion.pairs), custom_call_target="tpu_custom_call" | custom-call | tf_op jit(solution)/shard_map/pallas_call | solution.py:141
  67.6 3.1 %collective-permute-start.8 = (bf16[160,512]{1,0:T(8,128)(2,1)S(1)}, bf16[160,512]{1,0:T(8,128)(2,1)S(1)}, u32[]{:S(2)}, u32[]{:S(2)}) collective-permute-start(bf16[160,512]{1,0:T(8,128)(2,1)S(1)} %get-tuple-element.25.refs_0_), channel_id=1, source_target_pairs={{0,7},{1,0},{2,1},{3,2},{4,3},{5,4},{6,5},{7,6},{8,15},{9,8},{10,9... | collective-permute-start | bytes 491528 | tf_op jit(solution)/shard_map/ppermute | solution.py:318
  70.6 2.7 %collective-permute-start.9 = (bf16[160,512]{1,0:T(8,128)(2,1)S(1)}, bf16[160,512]{1,0:T(8,128)(2,1)S(1)}, u32[]{:S(2)}, u32[]{:S(2)}) collective-permute-start(bf16[160,512]{1,0:T(8,128)(2,1)S(1)} %get-tuple-element.26.refs_1_), channel_id=1, source_target_pairs={{0,7},{1,0},{2,1},{3,2},{4,3},{5,4},{6,5},{7,6},{8,15},{9,8},{10,9... | collective-permute-start | bytes 491528 | tf_op jit(solution)/shard_map/ppermute | solution.py:318
  73.9 3.5 %collective-permute-start.12 = (bf16[160,512]{1,0:T(8,128)(2,1)S(1)}, bf16[160,512]{1,0:T(8,128)(2,1)S(1)}, u32[]{:S(2)}, u32[]{:S(2)}) collective-permute-start(bf16[160,512]{1,0:T(8,128)(2,1)S(1)} %collective-permute-done.8.refs_2_), channel_id=1, source_target_pairs={{0,7},{1,0},{2,1},{3,2},{4,3},{5,4},{6,5},{7,6},{8,15},{9,8},{10,9... | collective-permute-start | bytes 491528 | tf_op jit(solution)/shard_map/ppermute | solution.py:318
  77.5 3.5 %collective-permute-start.13 = (bf16[160,512]{1,0:T(8,128)(2,1)S(1)}, bf16[160,512]{1,0:T(8,128)(2,1)}, u32[]{:S(2)}, u32[]{:S(2)}) collective-permute-start(bf16[160,512]{1,0:T(8,128)(2,1)S(1)} %collective-permute-done.9.refs_3_), channel_id=1, source_target_pairs={{0,7},{1,0},{2,1},{3,2},{4,3},{5,4},{6,5},{7,6},{8,15},{9,8},{10,9... | collective-permute-start | bytes 491528 | tf_op jit(solution)/shard_map/ppermute | solution.py:318
  81.1 2.7 %collective-permute-start.16 = (bf16[160,512]{1,0:T(8,128)(2,1)S(1)}, bf16[160,512]{1,0:T(8,128)(2,1)}, u32[]{:S(2)}, u32[]{:S(2)}) collective-permute-start(bf16[160,512]{1,0:T(8,128)(2,1)S(1)} %collective-permute-done.12.refs_6_), channel_id=1, source_target_pairs={{0,7},{1,0},{2,1},{3,2},{4,3},{5,4},{6,5},{7,6},{8,15},{9,8},{10,9... | collective-permute-start | bytes 491528 | tf_op jit(solution)/shard_map/ppermute | solution.py:318
  83.9 3.5 %collective-permute-start.17 = (bf16[160,512]{1,0:T(8,128)(2,1)}, bf16[160,512]{1,0:T(8,128)(2,1)}, u32[]{:S(2)}, u32[]{:S(2)}) collective-permute-start(bf16[160,512]{1,0:T(8,128)(2,1)} %collective-permute-done.13.refs_7_), channel_id=1, source_target_pairs={{0,7},{1,0},{2,1},{3,2},{4,3},{5,4},{6,5},{7,6},{8,15},{9,8},{10,9... | collective-permute-start | bytes 491528 | tf_op jit(solution)/shard_map/ppermute | solution.py:318
  87.6 3.1 %collective-permute-start.20 = (bf16[160,512]{1,0:T(8,128)(2,1)}, bf16[160,512]{1,0:T(8,128)(2,1)}, u32[]{:S(2)}, u32[]{:S(2)}) collective-permute-start(bf16[160,512]{1,0:T(8,128)(2,1)} %collective-permute-done.16.refs_0_), channel_id=1, source_target_pairs={{0,7},{1,0},{2,1},{3,2},{4,3},{5,4},{6,5},{7,6},{8,15},{9,8},{10,9... | collective-permute-start | bytes 491528 | tf_op jit(solution)/shard_map/ppermute | solution.py:318
  90.7 2.5 %all-to-all-done.2 = bf16[32,128,256]{2,1,0:T(8,128)(2,1)} async-done(((bf16[32,128,256]{2,1,0:T(8,128)(2,1)}), bf16[32,128,256]{2,1,0:T(8,128)(2,1)}, u32[]{:S(2)}, u32[]{:S(2)}) %all-to-all-start.2) | async-done | bytes 2097184 | tf_op jit(solution)/shard_map/all_to_all | solution.py:330
  93.3 3.6 %shard_map.108.early = f32[2,512,512]{2,1,0:T(8,128)S(1)} custom-call(bf16[16,2,128,256]{3,2,1,0:T(8,128)(2,1)} %bitcast.3.product, bf16[160,512]{1,0:T(8,128)(2,1)} %copy-done.2, bf16[160,512]{1,0:T(8,128)(2,1)} %copy-done.3, bf16[160,512]{1,0:T(8,128)(2,1)} %copy-done.11, bf16[160,512]{1,0:T(8,128)(2,1)} %copy-done.13, bf16[160,512]{1,0:T(8,128)(2,1)} %copy-done.14, ...), custom_call_target="tpu_custom_call" | custom-call | tf_op jit(solution)/shard_map/pallas_call | solution.py:224
  97.7 4.8 %shard_map.109 = (bf16[128,256]{1,0:T(8,128)(2,1)}, bf16[128,256]{1,0:T(8,128)(2,1)S(1)}) custom-call(s32[2]{0:T(128)S(1)} %copy-done.8, bf16[128,256]{1,0:T(8,128)(2,1)S(1)} %copy-done.6, f32[2,512,512]{2,1,0:T(8,128)S(1)} %shard_map.108.early, bf16[16,2,128,256]{3,2,1,0:T(8,128)(2,1)} %bitcast.3.product, bf16[160,512]{1,0:T(8,128)(2,1)} %collective-permute-done.16.refs_0_, ...), custom_call_target="tpu_custom_call" | custom-call | tf_op jit(solution)/shard_map/pallas_call | solution.py:262
  102.5 3.7 %collective-permute-start.22 = (bf16[128,256]{1,0:T(8,128)(2,1)S(1)}, bf16[128,256]{1,0:T(8,128)(2,1)S(1)}, u32[]{:S(2)}, u32[]{:S(2)}) collective-permute-start(bf16[128,256]{1,0:T(8,128)(2,1)S(1)} %get-tuple-element.28.attended), channel_id=1, source_target_pairs={{0,8},{8,0},{1,9},{9,1},{2,10},{10,2},{3,11},{11,3},{4,12},{12,4},... | collective-permute-start | bytes 196616 | tf_op jit(solution)/shard_map/ppermute | solution.py:322
  106.2 0.9 collective-permute-done.22.near
  107.1 1.7 %shard_map.110 = bf16[16,256,128]{2,1,0:T(8,128)(2,1)S(1)} custom-call(s32[2]{0:T(128)S(1)} %pad_add_fusion.place, bf16[128,256]{1,0:T(8,128)(2,1)S(1)} %get-tuple-element.28.attended, bf16[128,256]{1,0:T(8,128)(2,1)S(1)} %collective-permute-done.22.near, bf16[128,4096]{1,0:T(8,128)(2,1)S(1)} %copy-done.1, bf16[128,4096]{1,0:T(8,128)(2,1)} %collective-permute-done.7.near_grad), custom_call_target="tpu_custom_call" | custom-call | tf_op jit(solution)/shard_map/pallas_call | solution.py:288
  108.8 23.4 %all_to_all.20.parts = bf16[16,256,128]{2,1,0:T(8,128)(2,1)S(1)} all-to-all(bf16[16,256,128]{2,1,0:T(8,128)(2,1)S(1)} %shard_map.110), channel_id=1, replica_groups=mesh['chip'=16,'core'=2,'mp'=8] {'chip'}, dimensions={0} | all-to-all | bytes 2097152 | tf_op jit(solution)/shard_map/all_to_all | solution.py:326
  132.3 0.8 shard_map.111
  (70 shorter events, 3.9 us)
Async XLA Ops:
  0.6 24.9 %copy-start.1 = (bf16[128,4096]{1,0:T(8,128)(2,1)S(1)}, bf16[128,4096]{1,0:T(8,128)(2,1)}, u32[]{:S(2)}) copy-start(bf16[128,4096]{1,0:T(8,128)(2,1)} %grad.1) | copy-start | bytes 3145732
  2.3 15.5 %all-to-all-start = ((s32[32,1,1]{2,1,0:T(1,128)}), s32[32,1,1]{2,1,0:T(1,128)S(1)}, u32[]{:S(2)}, u32[]{:S(2)}) async-start(s32[32,1,1]{2,1,0:T(1,128)} %shard_map.104), calls=%async_computation | async-start | bytes 32768 | tf_op jit(solution)/shard_map/all_to_all | solution.py:330
  20.6 34.7 %all-to-all-start.1 = ((bf16[32,128,256]{2,1,0:T(8,128)(2,1)}), bf16[32,128,256]{2,1,0:T(8,128)(2,1)}, u32[]{:S(2)}, u32[]{:S(2)}) async-start(bf16[32,128,256]{2,1,0:T(8,128)(2,1)} %shard_map.105), calls=%async_computation.1 | async-start | bytes 4194304 | tf_op jit(solution)/shard_map/all_to_all | solution.py:330
  25.6 29.7 %collective-permute-start.7 = (bf16[128,4096]{1,0:T(8,128)(2,1)S(1)}, bf16[128,4096]{1,0:T(8,128)(2,1)}, u32[]{:S(2)}, u32[]{:S(2)}) collective-permute-start(bf16[128,4096]{1,0:T(8,128)(2,1)S(1)} %copy-done.1), channel_id=1, source_target_pairs={{0,8},{8,0},{1,9},{9,1},{2,10},{10,2},{3,11},{11,3},{4,12},{12,4},... | collective-permute-start | bytes 3145736 | tf_op jit(solution)/shard_map/ppermute | solution.py:322
  26.1 8.4 %collective-permute-start = (bf16[16,4096]{1,0:T(8,128)(2,1)S(1)}, bf16[16,4096]{1,0:T(8,128)(2,1)S(1)}, u32[]{:S(2)}, u32[]{:S(2)}) collective-permute-start(bf16[16,4096]{1,0:T(8,128)(2,1)S(1)} %constant_dynamic-slice_fusion.refs_0_), channel_id=1, source_target_pairs={{0,7},{1,0},{2,1},{3,2},{4,3},{5,4},{6,5},{7,6},{8,15},{9,8},{10,9... | collective-permute-start | bytes 393224 | tf_op jit(solution)/shard_map/ppermute | solution.py:318
  31.7 6.4 %collective-permute-start.4 = (bf16[16,4096]{1,0:T(8,128)(2,1)S(1)}, bf16[16,4096]{1,0:T(8,128)(2,1)S(1)}, u32[]{:S(2)}, u32[]{:S(2)}) collective-permute-start(bf16[16,4096]{1,0:T(8,128)(2,1)S(1)} %constant_dynamic-slice_fusion.refs_0_), channel_id=1, source_target_pairs={{0,1},{1,2},{2,3},{3,4},{4,5},{5,6},{6,7},{7,0},{8,9},{9,10},{10,1... | collective-permute-start | bytes 393224 | tf_op jit(solution)/shard_map/ppermute | solution.py:318
  34.5 5.5 %collective-permute-start.1 = (bf16[16,4096]{1,0:T(8,128)(2,1)S(1)}, bf16[16,4096]{1,0:T(8,128)(2,1)}, u32[]{:S(2)}, u32[]{:S(2)}) collective-permute-start(bf16[16,4096]{1,0:T(8,128)(2,1)S(1)} %collective-permute-done.refs_1_), channel_id=1, source_target_pairs={{0,7},{1,0},{2,1},{3,2},{4,3},{5,4},{6,5},{7,6},{8,15},{9,8},{10,9... | collective-permute-start | bytes 393224 | tf_op jit(solution)/shard_map/ppermute | solution.py:318
  38.1 8.7 %collective-permute-start.5 = (bf16[16,4096]{1,0:T(8,128)(2,1)S(1)}, bf16[16,4096]{1,0:T(8,128)(2,1)}, u32[]{:S(2)}, u32[]{:S(2)}) collective-permute-start(bf16[16,4096]{1,0:T(8,128)(2,1)S(1)} %collective-permute-done.4.refs_7_), channel_id=1, source_target_pairs={{0,1},{1,2},{2,3},{3,4},{4,5},{5,6},{6,7},{7,0},{8,9},{9,10},{10,1... | collective-permute-start | bytes 393224 | tf_op jit(solution)/shard_map/ppermute | solution.py:318
  40.0 6.8 %collective-permute-start.2 = (bf16[16,4096]{1,0:T(8,128)(2,1)}, bf16[16,4096]{1,0:T(8,128)(2,1)}, u32[]{:S(2)}, u32[]{:S(2)}) collective-permute-start(bf16[16,4096]{1,0:T(8,128)(2,1)} %collective-permute-done.1.refs_2_), channel_id=1, source_target_pairs={{0,7},{1,0},{2,1},{3,2},{4,3},{5,4},{6,5},{7,6},{8,15},{9,8},{10,9... | collective-permute-start | bytes 393224 | tf_op jit(solution)/shard_map/ppermute | solution.py:318
  46.8 5.3 %collective-permute-start.6 = (bf16[16,4096]{1,0:T(8,128)(2,1)}, bf16[16,4096]{1,0:T(8,128)(2,1)S(1)}, u32[]{:S(2)}, u32[]{:S(2)}) collective-permute-start(bf16[16,4096]{1,0:T(8,128)(2,1)} %collective-permute-done.5.refs_6_), channel_id=1, source_target_pairs={{0,1},{1,2},{2,3},{3,4},{4,5},{5,6},{6,7},{7,0},{8,9},{9,10},{10,1... | collective-permute-start | bytes 393224 | tf_op jit(solution)/shard_map/ppermute | solution.py:318
  46.9 5.2 %collective-permute-start.3 = (bf16[16,4096]{1,0:T(8,128)(2,1)}, bf16[16,4096]{1,0:T(8,128)(2,1)S(1)}, u32[]{:S(2)}, u32[]{:S(2)}) collective-permute-start(bf16[16,4096]{1,0:T(8,128)(2,1)} %collective-permute-done.2.refs_3_), channel_id=1, source_target_pairs={{0,7},{1,0},{2,1},{3,2},{4,3},{5,4},{6,5},{7,6},{8,15},{9,8},{10,9... | collective-permute-start | bytes 393224 | tf_op jit(solution)/shard_map/ppermute | solution.py:318
  55.3 38.0 %all-to-all-start.2 = ((bf16[32,128,256]{2,1,0:T(8,128)(2,1)}), bf16[32,128,256]{2,1,0:T(8,128)(2,1)}, u32[]{:S(2)}, u32[]{:S(2)}) async-start(bf16[32,128,256]{2,1,0:T(8,128)(2,1)} %shard_map.106), calls=%async_computation.2 | async-start | bytes 4194304 | tf_op jit(solution)/shard_map/all_to_all | solution.py:330
  65.4 32.3 %copy-start.6 = (bf16[128,256]{1,0:T(8,128)(2,1)S(1)}, bf16[128,256]{1,0:T(8,128)(2,1)}, u32[]{:S(2)}) copy-start(bf16[128,256]{1,0:T(8,128)(2,1)} %query.3) | copy-start | bytes 196612
  65.4 32.3 %copy-start.8 = (s32[2]{0:T(128)S(1)}, s32[2]{0:T(128)}, u32[]{:S(2)}) copy-start(s32[2]{0:T(128)} %counts.1) | copy-start | bytes 28
  67.5 13.4 %copy-start.3 = (bf16[160,512]{1,0:T(8,128)(2,1)}, bf16[160,512]{1,0:T(8,128)(2,1)S(1)}, u32[]{:S(2)}) copy-start(bf16[160,512]{1,0:T(8,128)(2,1)S(1)} %get-tuple-element.26.refs_1_) | copy-start | bytes 491524
  67.6 25.7 %copy-start.2 = (bf16[160,512]{1,0:T(8,128)(2,1)}, bf16[160,512]{1,0:T(8,128)(2,1)S(1)}, u32[]{:S(2)}) copy-start(bf16[160,512]{1,0:T(8,128)(2,1)S(1)} %get-tuple-element.25.refs_0_) | copy-start | bytes 491524
  67.6 6.4 %collective-permute-start.8 = (bf16[160,512]{1,0:T(8,128)(2,1)S(1)}, bf16[160,512]{1,0:T(8,128)(2,1)S(1)}, u32[]{:S(2)}, u32[]{:S(2)}) collective-permute-start(bf16[160,512]{1,0:T(8,128)(2,1)S(1)} %get-tuple-element.25.refs_0_), channel_id=1, source_target_pairs={{0,7},{1,0},{2,1},{3,2},{4,3},{5,4},{6,5},{7,6},{8,15},{9,8},{10,9... | collective-permute-start | bytes 491528 | tf_op jit(solution)/shard_map/ppermute | solution.py:318
  70.6 6.8 %collective-permute-start.11 = (bf16[160,512]{1,0:T(8,128)(2,1)S(1)}, bf16[160,512]{1,0:T(8,128)(2,1)S(1)}, u32[]{:S(2)}, u32[]{:S(2)}) collective-permute-start(bf16[160,512]{1,0:T(8,128)(2,1)S(1)} %get-tuple-element.26.refs_1_), channel_id=1, source_target_pairs={{0,1},{1,2},{2,3},{3,4},{4,5},{5,6},{6,7},{7,0},{8,9},{9,10},{10,1... | collective-permute-start | bytes 491528 | tf_op jit(solution)/shard_map/ppermute | solution.py:318
  70.6 6.8 %collective-permute-start.9 = (bf16[160,512]{1,0:T(8,128)(2,1)S(1)}, bf16[160,512]{1,0:T(8,128)(2,1)S(1)}, u32[]{:S(2)}, u32[]{:S(2)}) collective-permute-start(bf16[160,512]{1,0:T(8,128)(2,1)S(1)} %get-tuple-element.26.refs_1_), channel_id=1, source_target_pairs={{0,7},{1,0},{2,1},{3,2},{4,3},{5,4},{6,5},{7,6},{8,15},{9,8},{10,9... | collective-permute-start | bytes 491528 | tf_op jit(solution)/shard_map/ppermute | solution.py:318
  73.3 7.6 %collective-permute-start.10 = (bf16[160,512]{1,0:T(8,128)(2,1)S(1)}, bf16[160,512]{1,0:T(8,128)(2,1)S(1)}, u32[]{:S(2)}, u32[]{:S(2)}) collective-permute-start(bf16[160,512]{1,0:T(8,128)(2,1)S(1)} %get-tuple-element.25.refs_0_), channel_id=1, source_target_pairs={{0,1},{1,2},{2,3},{3,4},{4,5},{5,6},{6,7},{7,0},{8,9},{9,10},{10,1... | collective-permute-start | bytes 491528 | tf_op jit(solution)/shard_map/ppermute | solution.py:318
  73.9 19.3 %copy-start.11 = (bf16[160,512]{1,0:T(8,128)(2,1)}, bf16[160,512]{1,0:T(8,128)(2,1)S(1)}, u32[]{:S(2)}) copy-start(bf16[160,512]{1,0:T(8,128)(2,1)S(1)} %collective-permute-done.8.refs_2_) | copy-start | bytes 491524
  73.9 7.1 %collective-permute-start.12 = (bf16[160,512]{1,0:T(8,128)(2,1)S(1)}, bf16[160,512]{1,0:T(8,128)(2,1)S(1)}, u32[]{:S(2)}, u32[]{:S(2)}) collective-permute-start(bf16[160,512]{1,0:T(8,128)(2,1)S(1)} %collective-permute-done.8.refs_2_), channel_id=1, source_target_pairs={{0,7},{1,0},{2,1},{3,2},{4,3},{5,4},{6,5},{7,6},{8,15},{9,8},{10,9... | collective-permute-start | bytes 491528 | tf_op jit(solution)/shard_map/ppermute | solution.py:318
  77.4 6.3 %collective-permute-start.15 = (bf16[160,512]{1,0:T(8,128)(2,1)S(1)}, bf16[160,512]{1,0:T(8,128)(2,1)S(1)}, u32[]{:S(2)}, u32[]{:S(2)}) collective-permute-start(bf16[160,512]{1,0:T(8,128)(2,1)S(1)} %collective-permute-done.11.refs_5_), channel_id=1, source_target_pairs={{0,1},{1,2},{2,3},{3,4},{4,5},{5,6},{6,7},{7,0},{8,9},{9,10},{10,1... | collective-permute-start | bytes 491528 | tf_op jit(solution)/shard_map/ppermute | solution.py:318
  77.5 6.4 %collective-permute-start.13 = (bf16[160,512]{1,0:T(8,128)(2,1)S(1)}, bf16[160,512]{1,0:T(8,128)(2,1)}, u32[]{:S(2)}, u32[]{:S(2)}) collective-permute-start(bf16[160,512]{1,0:T(8,128)(2,1)S(1)} %collective-permute-done.9.refs_3_), channel_id=1, source_target_pairs={{0,7},{1,0},{2,1},{3,2},{4,3},{5,4},{6,5},{7,6},{8,15},{9,8},{10,9... | collective-permute-start | bytes 491528 | tf_op jit(solution)/shard_map/ppermute | solution.py:318
  81.0 6.6 %collective-permute-start.14 = (bf16[160,512]{1,0:T(8,128)(2,1)S(1)}, bf16[160,512]{1,0:T(8,128)(2,1)}, u32[]{:S(2)}, u32[]{:S(2)}) collective-permute-start(bf16[160,512]{1,0:T(8,128)(2,1)S(1)} %collective-permute-done.10.refs_4_), channel_id=1, source_target_pairs={{0,1},{1,2},{2,3},{3,4},{4,5},{5,6},{6,7},{7,0},{8,9},{9,10},{10,1... | collective-permute-start | bytes 491528 | tf_op jit(solution)/shard_map/ppermute | solution.py:318
  81.1 6.5 %collective-permute-start.16 = (bf16[160,512]{1,0:T(8,128)(2,1)S(1)}, bf16[160,512]{1,0:T(8,128)(2,1)}, u32[]{:S(2)}, u32[]{:S(2)}) collective-permute-start(bf16[160,512]{1,0:T(8,128)(2,1)S(1)} %collective-permute-done.12.refs_6_), channel_id=1, source_target_pairs={{0,7},{1,0},{2,1},{3,2},{4,3},{5,4},{6,5},{7,6},{8,15},{9,8},{10,9... | collective-permute-start | bytes 491528 | tf_op jit(solution)/shard_map/ppermute | solution.py:318
  83.8 6.9 %collective-permute-start.19 = (bf16[160,512]{1,0:T(8,128)(2,1)S(1)}, bf16[160,512]{1,0:T(8,128)(2,1)}, u32[]{:S(2)}, u32[]{:S(2)}) collective-permute-start(bf16[160,512]{1,0:T(8,128)(2,1)S(1)} %collective-permute-done.15.refs_9_), channel_id=1, source_target_pairs={{0,1},{1,2},{2,3},{3,4},{4,5},{5,6},{6,7},{7,0},{8,9},{9,10},{10,1... | collective-permute-start | bytes 491528 | tf_op jit(solution)/shard_map/ppermute | solution.py:318
  83.9 13.0 %collective-permute-start.17 = (bf16[160,512]{1,0:T(8,128)(2,1)}, bf16[160,512]{1,0:T(8,128)(2,1)}, u32[]{:S(2)}, u32[]{:S(2)}) collective-permute-start(bf16[160,512]{1,0:T(8,128)(2,1)} %collective-permute-done.13.refs_7_), channel_id=1, source_target_pairs={{0,7},{1,0},{2,1},{3,2},{4,3},{5,4},{6,5},{7,6},{8,15},{9,8},{10,9... | collective-permute-start | bytes 491528 | tf_op jit(solution)/shard_map/ppermute | solution.py:318
  87.6 9.3 %collective-permute-start.18 = (bf16[160,512]{1,0:T(8,128)(2,1)}, bf16[160,512]{1,0:T(8,128)(2,1)}, u32[]{:S(2)}, u32[]{:S(2)}) collective-permute-start(bf16[160,512]{1,0:T(8,128)(2,1)} %collective-permute-done.14.refs_8_), channel_id=1, source_target_pairs={{0,1},{1,2},{2,3},{3,4},{4,5},{5,6},{6,7},{7,0},{8,9},{9,10},{10,1... | collective-permute-start | bytes 491528 | tf_op jit(solution)/shard_map/ppermute | solution.py:318
  87.6 9.3 %collective-permute-start.20 = (bf16[160,512]{1,0:T(8,128)(2,1)}, bf16[160,512]{1,0:T(8,128)(2,1)}, u32[]{:S(2)}, u32[]{:S(2)}) collective-permute-start(bf16[160,512]{1,0:T(8,128)(2,1)} %collective-permute-done.16.refs_0_), channel_id=1, source_target_pairs={{0,7},{1,0},{2,1},{3,2},{4,3},{5,4},{6,5},{7,6},{8,15},{9,8},{10,9... | collective-permute-start | bytes 491528 | tf_op jit(solution)/shard_map/ppermute | solution.py:318
  90.7 7.0 %collective-permute-start.21 = (bf16[160,512]{1,0:T(8,128)(2,1)}, bf16[160,512]{1,0:T(8,128)(2,1)}, u32[]{:S(2)}, u32[]{:S(2)}) collective-permute-start(bf16[160,512]{1,0:T(8,128)(2,1)} %collective-permute-done.19.refs_3_), channel_id=1, source_target_pairs={{0,1},{1,2},{2,3},{3,4},{4,5},{5,6},{6,7},{7,0},{8,9},{9,10},{10,1... | collective-permute-start | bytes 491528 | tf_op jit(solution)/shard_map/ppermute | solution.py:318
  102.5 4.6 %collective-permute-start.22 = (bf16[128,256]{1,0:T(8,128)(2,1)S(1)}, bf16[128,256]{1,0:T(8,128)(2,1)S(1)}, u32[]{:S(2)}, u32[]{:S(2)}) collective-permute-start(bf16[128,256]{1,0:T(8,128)(2,1)S(1)} %get-tuple-element.28.attended), channel_id=1, source_target_pairs={{0,8},{8,0},{1,9},{9,1},{2,10},{10,2},{3,11},{11,3},{4,12},{12,4},... | collective-permute-start | bytes 196616 | tf_op jit(solution)/shard_map/ppermute | solution.py:322
  (12 other events, 67.3 us)
